TPU v7x, 512 devices: a whole 4x4x16 slice. The times are simulated.
512 devices in a mesh: req: 16 (over x, y_hi, core), mp: 32 (over y_lo, z).
Axes of the slice: x: 4, y: 4 (y_hi: 2, y_lo: 2; y = y_hi * 2 + y_lo), z: 16, core: 2. Of those that a mesh axis runs over, the one named last changes fastest.
Arguments:
- queries: bfloat16 [8192, 8192], P('req', 'mp')
- kv_new: bfloat16 [8192, 32, 256], P('req', 'mp')
- kv_pool: bfloat16 [4096, 16, 32, 256], P('req', None, 'mp')
- ssm_cache: float32 [256, 16, 8192], P('req', None, 'mp'), may hold values from -3 to 3
- mixer_in: bfloat16 [8192, 8192], P('req', 'mp'), may hold values from -3 to 3
- gate_in: bfloat16 [8192, 8192], P('req', 'mp'), may hold values from -2.5 to 2.5
- w_x: bfloat16 [8192, 544], P('mp'), may hold values from -0.0625 to 0.0625
- w_dt: bfloat16 [512, 8192], P(None, 'mp'), may hold values from -0.25 to 0.25
- b_dt: float32 [8192], P('mp'), may hold values from -5 to -1
- a_rate: float32 [16, 8192], P(None, 'mp'), may hold values from 0.05 to 1.5
- d_skip: float32 [8192], P('mp'), may hold values from 0.5 to 1.5
- kept_len: int32 [256], replicated, may hold values from 1 to 256, as said below
- new_len: int32 [256], replicated, may hold values from 1 to 32, as said below
- cache_index: int32 [256], replicated, may hold values from 0 to 255, as said below
- page_table: int32 [256, 16], replicated, may hold values from 0 to 4095, as said below
Outputs:
- attn_out: bfloat16 [8192, 8192], P('req', 'mp')
- mixer_out: bfloat16 [8192, 8192], P('req', 'mp')
- state_out: float32 [256, 16, 8192], P('req', None, 'mp')
Inputs may be any that keep to these rules, and one draw needn't show every extreme that they name: `kept_len`: every slot has at least one kept token; some slot has 256. `new_len`: some slot has 32. Every cache entry is named once; the entry of slot s lies on index cache_index[s] // 16 of req; the 16 slots of one index of req take their entries from exactly 8 indices, 2 from each. `page_table`: every page is named once; all pages of slot s lie on the same index of req as its cache entry, that is page // 256 == cache_index[s] // 16.
All inputs are finite; a program needn't handle non-finite values.
Results may differ from a plain program's by a relative error of at most 0.006.
Values may be sent and summed in bfloat16 or wider, within the bound.
No kernel may reach another device: no remote copies, remote signals or barrier semaphores. Data moves between devices by JAX's collectives and lax.ppermute only.
A program may use at most 128 MiB of HBM per device.

v0:
```python
import functools

import jax
import jax.numpy as jnp
from jax import lax
from jax.experimental import pallas as pl
from jax.experimental.pallas import tpu as pltpu
from jax.sharding import PartitionSpec as P

BF = jnp.bfloat16
F32 = jnp.float32
LOG2E = 1.4426950408889634

REQ = 16
NEW = 32
HD = 128
PAGES = 16
PAGE = 16
KEEP = PAGES * PAGE
NS = 16
RANK = 512
COLS = 640
CHUNK = 128
SUB = 16
STAT = 64
RET = 72
SEND = 96

VMEM = pl.BlockSpec(memory_space=pltpu.VMEM)
SMEM = pl.BlockSpec(memory_space=pltpu.SMEM)
PARAMS = pltpu.CompilerParams(vmem_limit_bytes=40 * 1024 * 1024)


def pack_kernel(tab, entries, q_ref, cache_ref, out_ref):
    for p in range(REQ):
        for k in range(2):
            slot = tab[k * REQ + p]
            out_ref[p, k * NEW : (k + 1) * NEW, :] = q_ref[
                pl.ds(pl.multiple_of(slot * NEW, NEW), NEW), :
            ]
            entry = entries[p * REQ + tab[(2 + k) * REQ + p]] & (REQ - 1)
            out_ref[p, 2 * NEW + k * NS : 2 * NEW + (k + 1) * NS, :] = cache_ref[entry].astype(BF)


def project_kernel(place, x_ref, w_ref, own_ref, *sent):
    for d in range(4):
        first = pl.multiple_of((place[0] ^ d) * CHUNK, CHUNK)
        rows = x_ref[pl.ds(first, CHUNK), :]
        low = jnp.dot(rows, w_ref[:, :RANK], preferred_element_type=F32)
        rest = jnp.dot(rows, w_ref[:, RANK:], preferred_element_type=F32)
        out = own_ref if d == 0 else sent[d - 1]
        out[:, :RANK] = low.astype(out.dtype)
        pad = jnp.zeros((CHUNK, COLS - RANK - rest.shape[1]), F32)
        out[:, RANK:] = jnp.concatenate([rest, pad], axis=1).astype(out.dtype)


def heads_down(block):
    return jnp.concatenate([block[:, :HD], block[:, HD:]], axis=0)


def cached_kernel(tab, place, table, kept, got_ref, pool_ref, out_ref):
    row = lax.broadcasted_iota(jnp.int32, (2 * NEW, HD), 0)
    lane = lax.broadcasted_iota(jnp.int32, (2 * NEW, HD), 1)
    key = lax.broadcasted_iota(jnp.int32, (2 * NEW, KEEP), 1)
    base = place[1] * (REQ * PAGES)

    def one_peer(p, carry):
        @pl.when(tab[4 * REQ + p] > 0)
        def _():
            stats = []
            for k in range(2):
                slot = p * REQ + tab[(2 + k) * REQ + p]
                pages = [pool_ref[table[slot * PAGES + t] - base] for t in range(PAGES)]
                rows = jnp.concatenate(pages, axis=0)
                q = heads_down(got_ref[p, k * NEW : (k + 1) * NEW, :])
                s = lax.dot_general(
                    q, rows[:, :HD], (((1,), (1,)), ((), ())), preferred_element_type=F32
                ) * (HD**-0.5)
                s = jnp.where(key < kept[slot], s, -1e30)
                top = jnp.max(s, axis=1, keepdims=True)
                w = jnp.exp(s - top)
                total = jnp.sum(w, axis=1, keepdims=True)
                o = jnp.dot(w.astype(BF), rows[:, HD:], preferred_element_type=F32) / total
                out_ref[p, k * NEW : (k + 1) * NEW, :] = jnp.concatenate(
                    [o[:NEW], o[NEW:]], axis=1
                ).astype(BF)
                lse = top + jnp.log(total)
                stats.append(jnp.sum(jnp.where(row == lane, lse, 0.0), axis=0, keepdims=True))
            flat = jnp.concatenate(stats, axis=0)
            hi = flat.astype(BF).astype(F32)
            mid = (flat - hi).astype(BF).astype(F32)
            low = flat - hi - mid
            none = jnp.zeros((6, HD), F32)
            left = jnp.concatenate([hi, low, none[:4]], axis=0)
            right = jnp.concatenate([mid, none], axis=0)
            out_ref[p, STAT:RET, :] = jnp.concatenate([left, right], axis=1).astype(BF)

        return carry

    lax.fori_loop(0, REQ, one_peer, 0)


def combine_kernel(tab, fresh_len, q_ref, kv_ref, got_ref, out_ref):
    row = lax.broadcasted_iota(jnp.int32, (2 * NEW, HD), 0)
    lane = lax.broadcasted_iota(jnp.int32, (2 * NEW, HD), 1)
    query = lax.broadcasted_iota(jnp.int32, (2 * NEW, NEW), 0) & (NEW - 1)
    key = lax.broadcasted_iota(jnp.int32, (2 * NEW, NEW), 1)
    place = lax.broadcasted_iota(jnp.int32, (NEW, 2 * HD), 0)

    def one_slot(i, carry):
        first = pl.multiple_of(i * NEW, NEW)
        owner = tab[5 * REQ + i]
        second = (tab[REQ + owner] == i).astype(jnp.int32)
        q = heads_down(q_ref[pl.ds(first, NEW), :])
        rows = kv_ref[pl.ds(first, NEW), :]
        s = lax.dot_general(
            q, rows[:, :HD], (((1,), (1,)), ((), ())), preferred_element_type=F32
        ) * (HD**-0.5)
        s = jnp.where(key <= query, s, -1e30)
        top = jnp.max(s, axis=1, keepdims=True)
        w = jnp.exp(s - top)
        total = jnp.sum(w, axis=1, keepdims=True)
        o = jnp.dot(w.astype(BF), rows[:, HD:], preferred_element_type=F32)
        old = heads_down(
            got_ref[owner, pl.ds(pl.multiple_of(second * NEW, NEW), NEW), :]
        ).astype(F32)
        stats = got_ref[owner, STAT:RET, :].astype(F32)
        exact = stats[0:2, :HD] + stats[0:2, HD:] + stats[2:4, :HD]
        flat = jnp.where(second > 0, exact[1:2], exact[0:1])
        lse = jnp.sum(jnp.where(row == lane, flat, 0.0), axis=1, keepdims=True)
        most = jnp.maximum(lse, top)
        share_old = jnp.exp(lse - most)
        share = jnp.exp(top - most)
        o = (old * share_old + o * share) / (share_old + total * share)
        o = jnp.concatenate([o[:NEW], o[NEW:]], axis=1)
        out_ref[pl.ds(first, NEW), :] = jnp.where(place < fresh_len[i], o, 0.0).astype(BF)
        return carry

    lax.fori_loop(0, REQ, one_slot, 0, unroll=2)


def scan_kernel(
    tab, place, fresh_len, p0, p1, p2, p3, wdt_ref, b_ref, a_ref, d_ref, x_ref, g_ref, got_ref,
    out_ref, state_ref, dt_s, u_s, bc_s, y_s, a_s, h_s,
):
    channels = x_ref.shape[1]
    halves = [slice(c * HD, (c + 1) * HD) for c in range(channels // HD)]
    step = lax.broadcasted_iota(jnp.int32, (NEW, channels), 0)
    for d, part in enumerate((p0, p1, p2, p3)):
        member = place[0] ^ d
        first = pl.multiple_of(member * CHUNK, CHUNK)
        pre = jnp.dot(part[:, :RANK], wdt_ref[...], preferred_element_type=F32) + b_ref[...]
        dt = jnp.maximum(pre, 0.0) + jnp.log1p(jnp.exp(-jnp.abs(pre)))
        bc_s[pl.ds(first, CHUNK), :] = part[:, RANK:].astype(F32)
        for j in range(CHUNK // NEW):
            here = pl.multiple_of(first + j * NEW, NEW)
            live = step < fresh_len[member * (CHUNK // NEW) + j]
            masked = jnp.where(live, dt[j * NEW : (j + 1) * NEW], 0.0)
            drive = masked * x_ref[pl.ds(here, NEW), :].astype(F32)
            for c, half in enumerate(halves):
                dt_s[c, pl.ds(here, NEW), :] = masked[:, half]
                u_s[c, pl.ds(here, NEW), :] = drive[:, half]
    for i in range(REQ):
        owner = tab[5 * REQ + i]
        second = (tab[REQ + owner] == i).astype(jnp.int32)
        start = pl.multiple_of(2 * NEW + second * NS, NS)
        state = got_ref[owner, pl.ds(start, NS), :].astype(F32)
        for c, half in enumerate(halves):
            h_s[c, i * NS : (i + 1) * NS, :] = state[:, half]
    for n in range(NS):
        a_s[n * 8 : (n + 1) * 8, :] = jnp.broadcast_to(a_ref[n : n + 1, :] * (-LOG2E), (8, channels))
    for g in range(2):
        begin = g * 8 * NS
        h0 = tuple(
            tuple(h_s[c, pl.ds(begin + n, 8, stride=NS), :] for c in range(len(halves)))
            for n in range(NS)
        )

        def one_step(i, hs):
            rows = pl.ds(g * 8 * NEW + i, 8, stride=NEW)
            dt = [dt_s[c, rows, :] for c in range(len(halves))]
            u = [u_s[c, rows, :] for c in range(len(halves))]
            bc = bc_s[rows, :]
            y = [0.0] * len(halves)
            new = []
            for n in range(NS):
                b_in = jnp.broadcast_to(bc[:, n : n + 1], (8, HD))
                c_out = jnp.broadcast_to(bc[:, NS + n : NS + n + 1], (8, HD))
                pair = []
                for c, half in enumerate(halves):
                    decay = jnp.exp2(dt[c] * a_s[n * 8 : (n + 1) * 8, half])
                    h = decay * hs[n][c] + u[c] * b_in
                    y[c] = y[c] + h * c_out
                    pair.append(h)
                new.append(tuple(pair))
            for c in range(len(halves)):
                y_s[c, rows, :] = y[c]
            return tuple(new)

        hs = lax.fori_loop(0, NEW, one_step, h0)
        for n in range(NS):
            for c in range(len(halves)):
                h_s[c, pl.ds(begin + n, 8, stride=NS), :] = hs[n][c]
    for c, half in enumerate(halves):
        state_ref[:, half] = h_s[c]
    for i in range(REQ):
        rows = slice(i * NEW, (i + 1) * NEW)
        for c, half in enumerate(halves):
            gate = g_ref[rows, half].astype(F32)
            y = y_s[c, rows, :] + d_ref[:, half] * x_ref[rows, half].astype(F32)
            y = y * (gate * jax.nn.sigmoid(gate))
            out_ref[rows, half] = jnp.where(step[:, half] < fresh_len[i], y, 0.0).astype(BF)


def on_device(
    queries, kv_new, kv_pool, ssm_cache, mixer_in, gate_in, w_x, w_dt, b_dt, a_rate, d_skip,
    kept_len, new_len, cache_index, page_table,
):
    rows, channels = mixer_in.shape
    me = lax.axis_index("req")
    at = lax.axis_index("mp")
    zs = lax.axis_size("mp") // 2
    member = (at // zs) * 2 + (at & 1)
    place = jnp.stack([member, me]).astype(jnp.int32)

    owners = cache_index.reshape(REQ, REQ) // REQ
    mine = lax.dynamic_slice_in_dim(owners, me, 1, 0)
    ids = jnp.arange(REQ, dtype=jnp.int32)

    def ends(match):
        first = jnp.min(jnp.where(match, ids[None, :], REQ), axis=1)
        last = jnp.max(jnp.where(match, ids[None, :], -1), axis=1)
        return jnp.minimum(first, REQ - 1), jnp.maximum(last, 0), last >= 0

    q_first, q_last, _ = ends(mine == ids[:, None])
    s_first, s_last, active = ends(owners == me)
    tab = jnp.concatenate([q_first, q_last, s_first, s_last, active.astype(jnp.int32), mine[0]])
    fresh_len = lax.dynamic_slice_in_dim(new_len, me * REQ, REQ, 0)

    packed = pl.pallas_call(
        pack_kernel,
        out_shape=jax.ShapeDtypeStruct((REQ, SEND, channels), BF),
        in_specs=[SMEM, SMEM, VMEM, VMEM],
        out_specs=VMEM,
        compiler_params=PARAMS,
        name="pack",
    )(tab, cache_index, queries, ssm_cache)
    got = lax.all_to_all(packed, "req", 0, 0, tiled=True)

    chunk = jax.ShapeDtypeStruct((CHUNK, COLS), BF)
    own, *sent = pl.pallas_call(
        project_kernel,
        out_shape=[jax.ShapeDtypeStruct((CHUNK, COLS), F32), chunk, chunk, chunk],
        in_specs=[SMEM, VMEM, VMEM],
        out_specs=[VMEM] * 4,
        compiler_params=PARAMS,
        name="project",
    )(place, mixer_in, w_x)

    def swap(array, d):
        pairs = []
        for i in range(2 * zs):
            y, z = i // zs, i % zs
            pairs.append((i, (y ^ (d >> 1)) * zs + (z ^ (d & 1))))
        return lax.ppermute(array, "mp", pairs)

    groups = [[y * zs + 2 * k + b for k in range(zs // 2)] for y in range(2) for b in range(2)]
    for d in (1, 2, 3):
        own = own + swap(sent[d - 1], d).astype(F32)
    parts = lax.all_to_all(
        own.astype(BF).reshape(-1, SUB, COLS), "mp", 0, 0, tiled=True, axis_index_groups=groups
    )
    summed = jnp.sum(parts.astype(F32), axis=0, keepdims=True).astype(BF)
    whole = lax.all_to_all(
        jnp.broadcast_to(summed, parts.shape), "mp", 0, 0, tiled=True, axis_index_groups=groups
    ).reshape(CHUNK, COLS)
    others = [swap(whole, d) for d in (1, 2, 3)]

    partial = pl.pallas_call(
        cached_kernel,
        out_shape=jax.ShapeDtypeStruct((REQ, RET, channels), BF),
        in_specs=[SMEM, SMEM, SMEM, SMEM, VMEM, VMEM],
        out_specs=VMEM,
        compiler_params=PARAMS,
        name="cached",
    )(tab, place, page_table.reshape(-1), kept_len, got, kv_pool.reshape(-1, PAGE, channels))
    back = lax.all_to_all(partial, "req", 0, 0, tiled=True)

    mixer_out, state_out = pl.pallas_call(
        scan_kernel,
        out_shape=[
            jax.ShapeDtypeStruct((rows, channels), BF),
            jax.ShapeDtypeStruct((REQ * NS, channels), F32),
        ],
        in_specs=[SMEM] * 3 + [VMEM] * 11,
        out_specs=[VMEM] * 2,
        scratch_shapes=[
            pltpu.VMEM((channels // HD, rows, HD), F32),
            pltpu.VMEM((channels // HD, rows, HD), F32),
            pltpu.VMEM((rows, COLS - RANK), F32),
            pltpu.VMEM((channels // HD, rows, HD), F32),
            pltpu.VMEM((NS * 8, channels), F32),
            pltpu.VMEM((channels // HD, REQ * NS, HD), F32),
        ],
        compiler_params=PARAMS,
        name="scan",
    )(
        tab, place, fresh_len, whole, *others, w_dt, b_dt.reshape(1, -1), a_rate,
        d_skip.reshape(1, -1), mixer_in, gate_in, got,
    )
    attn_out = pl.pallas_call(
        combine_kernel,
        out_shape=jax.ShapeDtypeStruct((rows, channels), BF),
        in_specs=[SMEM, SMEM, VMEM, VMEM, VMEM],
        out_specs=VMEM,
        compiler_params=PARAMS,
        name="combine",
    )(tab, fresh_len, queries, kv_new.reshape(rows, channels), back)
    return attn_out, mixer_out, state_out.reshape(REQ, NS, channels)


def solution(mesh):
    placed = (
        P("req", "mp"),
        P("req", "mp", None),
        P("req", None, "mp", None),
        P("req", None, "mp"),
        P("req", "mp"),
        P("req", "mp"),
        P("mp", None),
        P(None, "mp"),
        P("mp"),
        P(None, "mp"),
        P("mp"),
        P(),
        P(),
        P(),
        P(),
    )
    return jax.shard_map(
        on_device,
        mesh=mesh,
        in_specs=placed,
        out_specs=(P("req", "mp"), P("req", "mp"), P("req", None, "mp")),
        check_vma=False,
    )
```

profile of v0, /device:TPU:1, one launch (start us, length us, event | category | flops | bytes accessed | tf_op | source)
XLA Modules:
  0.0 126.6 jit_solution(8968692749366861076)
XLA Ops:
  0.7 1.2 copy.20.w_ref
  2.0 0.9 copy-done.2
  2.9 0.9 project.1
  3.8 5.4 %collective-permute-start.2 = (bf16[128,640]{1,0:T(8,128)(2,1)S(1)}, bf16[128,640]{1,0:T(8,128)(2,1)S(1)}, u32[]{:S(2)}, u32[]{:S(2)}) collective-permute-start(bf16[128,640]{1,0:T(8,128)(2,1)S(1)} %get-tuple-element.12), channel_id=1, source_target_pairs={{0,17},{1,16},{2,19},{3,18},{4,21},{5,20},{6,23},{7,22},{8,25},{9,... | collective-permute-start | bytes 491528 | tf_op jit(solution)/shard_map/ppermute | solution.py:265
  9.2 2.1 %collective-permute-start.1 = (bf16[128,640]{1,0:T(8,128)(2,1)S(1)}, bf16[128,640]{1,0:T(8,128)(2,1)S(1)}, u32[]{:S(2)}, u32[]{:S(2)}) collective-permute-start(bf16[128,640]{1,0:T(8,128)(2,1)S(1)} %get-tuple-element.11), channel_id=1, source_target_pairs={{0,16},{1,17},{2,18},{3,19},{4,20},{5,21},{6,22},{7,23},{8,24},{9,... | collective-permute-start | bytes 491528 | tf_op jit(solution)/shard_map/ppermute | solution.py:265
  11.3 2.0 %collective-permute-start = (bf16[128,640]{1,0:T(8,128)(2,1)S(1)}, bf16[128,640]{1,0:T(8,128)(2,1)S(1)}, u32[]{:S(2)}, u32[]{:S(2)}) collective-permute-start(bf16[128,640]{1,0:T(8,128)(2,1)S(1)} %get-tuple-element.10), channel_id=1, source_target_pairs={{0,1},{1,0},{2,3},{3,2},{4,5},{5,4},{6,7},{7,6},{8,9},{9,8},{10,11... | collective-permute-start | bytes 491528 | tf_op jit(solution)/shard_map/ppermute | solution.py:265
  13.4 0.8 reshape.37
  14.2 0.1 select_reduce_fusion
  14.3 1.0 collective-permute-done.1
  15.3 2.4 %collective-permute-done = bf16[128,640]{1,0:T(8,128)(2,1)S(1)} collective-permute-done((bf16[128,640]{1,0:T(8,128)(2,1)S(1)}, bf16[128,640]{1,0:T(8,128)(2,1)S(1)}, u32[]{:S(2)}, u32[]{:S(2)}) %collective-permute-start) | collective-permute-done | bytes 163872 | tf_op jit(solution)/shard_map/ppermute | solution.py:265
  17.7 0.7 add_convert_fusion
  18.4 14.0 %all-to-all-start.2 = ((bf16[8,16,640]{2,1,0:T(8,128)(2,1)}), bf16[8,16,640]{2,1,0:T(8,128)(2,1)}, u32[]{:S(2)}, u32[]{:S(2)}) async-start(bf16[8,16,640]{2,1,0:T(8,128)(2,1)} %bitcast.5), calls=%async_computation.2 | async-start | bytes 327680 | tf_op jit(solution)/shard_map/all_to_all | solution.py:270
  32.5 0.1 select_reduce_fusion.2
  32.7 1.5 %pack.1 = bf16[16,96,256]{2,1,0:T(8,128)(2,1)} custom-call(s32[96]{0:T(128)S(1)} %concatenate.3.tab, s32[256]{0:T(256)S(1)} %copy-done.9, bf16[512,256]{1,0:T(8,128)(2,1)S(1)} %copy-done.1, f32[16,16,256]{2,1,0:T(8,128)S(1)} %copy-done.4), custom_call_target="tpu_custom_call" | custom-call | tf_op jit(solution)/shard_map/pack/pallas_call | solution.py:240
  34.2 12.3 %all-to-all-done.2 = bf16[8,16,640]{2,1,0:T(8,128)(2,1)} async-done(((bf16[8,16,640]{2,1,0:T(8,128)(2,1)}), bf16[8,16,640]{2,1,0:T(8,128)(2,1)}, u32[]{:S(2)}, u32[]{:S(2)}) %all-to-all-start.2) | async-done | bytes 163872 | tf_op jit(solution)/shard_map/all_to_all | solution.py:270
  46.5 11.2 %all-to-all-start = ((bf16[16,96,256]{2,1,0:T(8,128)(2,1)}), bf16[16,96,256]{2,1,0:T(8,128)(2,1)S(1)}, u32[]{:S(2)}, u32[]{:S(2)}) async-start(bf16[16,96,256]{2,1,0:T(8,128)(2,1)} %pack.1), calls=%async_computation | async-start | bytes 1572864 | tf_op jit(solution)/shard_map/all_to_all | solution.py:248
  57.8 0.9 reduce_sum.12
  58.7 13.2 %all-to-all-done.got_ref = bf16[16,96,256]{2,1,0:T(8,128)(2,1)S(1)} async-done(((bf16[16,96,256]{2,1,0:T(8,128)(2,1)}), bf16[16,96,256]{2,1,0:T(8,128)(2,1)S(1)}, u32[]{:S(2)}, u32[]{:S(2)}) %all-to-all-start) | async-done | bytes 786464 | tf_op jit(solution)/shard_map/all_to_all | solution.py:248
  71.9 0.7 broadcast_in_dim.43
  72.6 3.4 %all-to-all-start.3 = ((bf16[8,16,640]{2,1,0:T(8,128)(2,1)}), bf16[8,16,640]{2,1,0:T(8,128)(2,1)S(1)}, u32[]{:S(2)}, u32[]{:S(2)}) async-start(bf16[8,16,640]{2,1,0:T(8,128)(2,1)} %broadcast_in_dim.43), calls=%async_computation.3 | async-start | bytes 327680 | tf_op jit(solution)/shard_map/all_to_all | solution.py:274
  76.0 0.8 copy.19
  76.8 0.1 reshape.39.table
  77.0 6.8 %cached.1 = bf16[16,72,256]{2,1,0:T(8,128)(2,1)} custom-call(s32[96]{0:T(128)S(1)} %concatenate.3.tab, s32[2]{0:T(128)S(1)} %pad_add_fusion.place, s32[4096]{0:T(1024)S(1)} %reshape.39.table, s32[256]{0:T(256)S(1)} %copy-done.10, bf16[16,96,256]{2,1,0:T(8,128)(2,1)S(1)} %all-to-all-done.got_ref, bf16[256,16,256]{2,1,0:T(8,128)(2,1)S(1)} %bitcast.11), custom_call_target="tpu_custom_call" | custom-call | tf_op jit(solution)/shard_map/cached/pallas_call | solution.py:279
  83.8 6.2 %all-to-all-done.3 = bf16[8,16,640]{2,1,0:T(8,128)(2,1)S(1)} async-done(((bf16[8,16,640]{2,1,0:T(8,128)(2,1)}), bf16[8,16,640]{2,1,0:T(8,128)(2,1)S(1)}, u32[]{:S(2)}, u32[]{:S(2)}) %all-to-all-start.3) | async-done | bytes 163872 | tf_op jit(solution)/shard_map/all_to_all | solution.py:274
  90.0 7.2 %all-to-all-start.1 = ((bf16[16,72,256]{2,1,0:T(8,128)(2,1)}), bf16[16,72,256]{2,1,0:T(8,128)(2,1)S(1)}, u32[]{:S(2)}, u32[]{:S(2)}) async-start(bf16[16,72,256]{2,1,0:T(8,128)(2,1)} %cached.1), calls=%async_computation.1 | async-start | bytes 1179648 | tf_op jit(solution)/shard_map/all_to_all | solution.py:287
  97.2 2.5 %collective-permute-start.3 = (bf16[128,640]{1,0:T(8,128)(2,1)S(1)}, bf16[128,640]{1,0:T(8,128)(2,1)S(1)}, u32[]{:S(2)}, u32[]{:S(2)}) collective-permute-start(bf16[128,640]{1,0:T(8,128)(2,1)S(1)} %bitcast.12), channel_id=1, source_target_pairs={{0,1},{1,0},{2,3},{3,2},{4,5},{5,4},{6,7},{7,6},{8,9},{9,8},{10,11... | collective-permute-start | bytes 491528 | tf_op jit(solution)/shard_map/ppermute | solution.py:265
  99.7 2.8 %collective-permute-start.4 = (bf16[128,640]{1,0:T(8,128)(2,1)S(1)}, bf16[128,640]{1,0:T(8,128)(2,1)S(1)}, u32[]{:S(2)}, u32[]{:S(2)}) collective-permute-start(bf16[128,640]{1,0:T(8,128)(2,1)S(1)} %bitcast.13), channel_id=1, source_target_pairs={{0,16},{1,17},{2,18},{3,19},{4,20},{5,21},{6,22},{7,23},{8,24},{9,... | collective-permute-start | bytes 491528 | tf_op jit(solution)/shard_map/ppermute | solution.py:265
  102.5 3.1 %collective-permute-start.5 = (bf16[128,640]{1,0:T(8,128)(2,1)S(1)}, bf16[128,640]{1,0:T(8,128)(2,1)S(1)}, u32[]{:S(2)}, u32[]{:S(2)}) collective-permute-start(bf16[128,640]{1,0:T(8,128)(2,1)S(1)} %bitcast.14), channel_id=1, source_target_pairs={{0,17},{1,16},{2,19},{3,18},{4,21},{5,20},{6,23},{7,22},{8,25},{9,... | collective-permute-start | bytes 491528 | tf_op jit(solution)/shard_map/ppermute | solution.py:265
  105.7 3.2 %all-to-all-done.1.got_ref = bf16[16,72,256]{2,1,0:T(8,128)(2,1)S(1)} async-done(((bf16[16,72,256]{2,1,0:T(8,128)(2,1)}), bf16[16,72,256]{2,1,0:T(8,128)(2,1)S(1)}, u32[]{:S(2)}, u32[]{:S(2)}) %all-to-all-start.1) | async-done | bytes 589856 | tf_op jit(solution)/shard_map/all_to_all | solution.py:287
  108.9 0.9 copy-done.5
  109.8 5.6 %combine.1 = bf16[512,256]{1,0:T(8,128)(2,1)} custom-call(s32[96]{0:T(128)S(1)} %concatenate.3.tab, s32[16]{0:T(128)S(1)} %dynamic_slice.7.fresh_len, bf16[512,256]{1,0:T(8,128)(2,1)S(1)} %copy-done.1, bf16[512,256]{1,0:T(8,128)(2,1)S(1)} %bitcast.16, bf16[16,72,256]{2,1,0:T(8,128)(2,1)S(1)} %all-to-all-done.1.got_ref), custom_call_target="tpu_custom_call" | custom-call | tf_op jit(solution)/shard_map/combine/pallas_call | solution.py:311
  115.6 11.1 %scan.1 = (bf16[512,256]{1,0:T(8,128)(2,1)}, f32[256,256]{1,0:T(8,128)}) custom-call(s32[96]{0:T(128)S(1)} %concatenate.3.tab, s32[2]{0:T(128)S(1)} %pad_add_fusion.place, s32[16]{0:T(128)S(1)} %dynamic_slice.7.fresh_len, bf16[128,640]{1,0:T(8,128)(2,1)S(1)} %bitcast.15, bf16[128,640]{1,0:T(8,128)(2,1)S(1)} %collective-permute-done.3.p1, ...), custom_call_target="tpu_custom_call" | custom-call | tf_op jit(solution)/shard_map/scan/pallas_call | solution.py:289
  (38 shorter events, 0.3 us)
Async XLA Ops:
  0.6 32.1 %copy-start.9 = (s32[256]{0:T(256)S(1)}, s32[256]{0:T(256)}, u32[]{:S(2)}) copy-start(s32[256]{0:T(256)} %entries.1) | copy-start | bytes 3076
  0.6 32.1 %copy-start.1 = (bf16[512,256]{1,0:T(8,128)(2,1)S(1)}, bf16[512,256]{1,0:T(8,128)(2,1)}, u32[]{:S(2)}) copy-start(bf16[512,256]{1,0:T(8,128)(2,1)} %q_ref.3) | copy-start | bytes 786436
  0.7 32.1 %copy-start.4 = (f32[16,16,256]{2,1,0:T(8,128)S(1)}, f32[16,16,256]{2,1,0:T(8,128)}, u32[]{:S(2)}) copy-start(f32[16,16,256]{2,1,0:T(8,128)} %cache_ref.1) | copy-start | bytes 786436
  2.0 1.0 copy-start.2
  3.8 10.4 %collective-permute-start.2 = (bf16[128,640]{1,0:T(8,128)(2,1)S(1)}, bf16[128,640]{1,0:T(8,128)(2,1)S(1)}, u32[]{:S(2)}, u32[]{:S(2)}) collective-permute-start(bf16[128,640]{1,0:T(8,128)(2,1)S(1)} %get-tuple-element.12), channel_id=1, source_target_pairs={{0,17},{1,16},{2,19},{3,18},{4,21},{5,20},{6,23},{7,22},{8,25},{9,... | collective-permute-start | bytes 491528 | tf_op jit(solution)/shard_map/ppermute | solution.py:265
  9.2 6.1 %collective-permute-start.1 = (bf16[128,640]{1,0:T(8,128)(2,1)S(1)}, bf16[128,640]{1,0:T(8,128)(2,1)S(1)}, u32[]{:S(2)}, u32[]{:S(2)}) collective-permute-start(bf16[128,640]{1,0:T(8,128)(2,1)S(1)} %get-tuple-element.11), channel_id=1, source_target_pairs={{0,16},{1,17},{2,18},{3,19},{4,20},{5,21},{6,22},{7,23},{8,24},{9,... | collective-permute-start | bytes 491528 | tf_op jit(solution)/shard_map/ppermute | solution.py:265
  11.3 6.4 %collective-permute-start = (bf16[128,640]{1,0:T(8,128)(2,1)S(1)}, bf16[128,640]{1,0:T(8,128)(2,1)S(1)}, u32[]{:S(2)}, u32[]{:S(2)}) collective-permute-start(bf16[128,640]{1,0:T(8,128)(2,1)S(1)} %get-tuple-element.10), channel_id=1, source_target_pairs={{0,1},{1,0},{2,3},{3,2},{4,5},{5,4},{6,7},{7,6},{8,9},{9,8},{10,11... | collective-permute-start | bytes 491528 | tf_op jit(solution)/shard_map/ppermute | solution.py:265
  18.4 58.5 %copy-start = (bf16[256,16,1,256]{3,1,2,0:T(8,128)(2,1)S(1)}, bf16[256,16,1,256]{3,1,2,0:T(8,128)(2,1)}, u32[]{:S(2)}) copy-start(bf16[256,16,1,256]{3,1,2,0:T(8,128)(2,1)} %param.17) | copy-start | bytes 6291460
  18.4 58.5 %copy-start.10 = (s32[256]{0:T(256)S(1)}, s32[256]{0:T(256)}, u32[]{:S(2)}) copy-start(s32[256]{0:T(256)} %kept.1) | copy-start | bytes 3076
  18.4 28.1 %all-to-all-start.2 = ((bf16[8,16,640]{2,1,0:T(8,128)(2,1)}), bf16[8,16,640]{2,1,0:T(8,128)(2,1)}, u32[]{:S(2)}, u32[]{:S(2)}) async-start(bf16[8,16,640]{2,1,0:T(8,128)(2,1)} %bitcast.5), calls=%async_computation.2 | async-start | bytes 327680 | tf_op jit(solution)/shard_map/all_to_all | solution.py:270
  46.5 25.4 %all-to-all-start = ((bf16[16,96,256]{2,1,0:T(8,128)(2,1)}), bf16[16,96,256]{2,1,0:T(8,128)(2,1)S(1)}, u32[]{:S(2)}, u32[]{:S(2)}) async-start(bf16[16,96,256]{2,1,0:T(8,128)(2,1)} %pack.1), calls=%async_computation | async-start | bytes 1572864 | tf_op jit(solution)/shard_map/all_to_all | solution.py:248
  72.6 17.4 %all-to-all-start.3 = ((bf16[8,16,640]{2,1,0:T(8,128)(2,1)}), bf16[8,16,640]{2,1,0:T(8,128)(2,1)S(1)}, u32[]{:S(2)}, u32[]{:S(2)}) async-start(bf16[8,16,640]{2,1,0:T(8,128)(2,1)} %broadcast_in_dim.43), calls=%async_computation.3 | async-start | bytes 327680 | tf_op jit(solution)/shard_map/all_to_all | solution.py:274
  76.9 28.7 %copy-start.13 = (s32[256]{0:T(256)S(1)}, s32[256]{0:T(256)}, u32[]{:S(2)}) copy-start(s32[256]{0:T(256)} %param.27) | copy-start | bytes 3076
  83.8 31.7 %copy-start.3 = (bf16[512,256]{1,0:T(8,128)(2,1)S(1)}, bf16[512,256]{1,0:T(8,128)(2,1)}, u32[]{:S(2)}) copy-start(bf16[512,256]{1,0:T(8,128)(2,1)} %x_ref.3) | copy-start | bytes 786436
  83.8 31.8 %copy-start.6 = (bf16[512,256]{1,0:T(8,128)(2,1)S(1)}, bf16[512,256]{1,0:T(8,128)(2,1)}, u32[]{:S(2)}) copy-start(bf16[512,256]{1,0:T(8,128)(2,1)} %wdt_ref.1) | copy-start | bytes 786436
  83.8 31.8 %copy-start.7 = (bf16[512,256]{1,0:T(8,128)(2,1)S(1)}, bf16[512,256]{1,0:T(8,128)(2,1)}, u32[]{:S(2)}) copy-start(bf16[512,256]{1,0:T(8,128)(2,1)} %g_ref.1) | copy-start | bytes 786436
  83.8 31.8 %copy-start.8 = (f32[16,256]{1,0:T(8,128)S(1)}, f32[16,256]{1,0:T(8,128)}, u32[]{:S(2)}) copy-start(f32[16,256]{1,0:T(8,128)} %a_ref.1) | copy-start | bytes 49156
  83.8 31.8 %copy-start.11 = (f32[256]{0:T(256)S(1)}, f32[256]{0:T(256)}, u32[]{:S(2)}) copy-start(f32[256]{0:T(256)} %param.23) | copy-start | bytes 3076
  83.8 31.8 %copy-start.12 = (f32[256]{0:T(256)S(1)}, f32[256]{0:T(256)}, u32[]{:S(2)}) copy-start(f32[256]{0:T(256)} %param.25) | copy-start | bytes 3076
  90.0 18.9 %all-to-all-start.1 = ((bf16[16,72,256]{2,1,0:T(8,128)(2,1)}), bf16[16,72,256]{2,1,0:T(8,128)(2,1)S(1)}, u32[]{:S(2)}, u32[]{:S(2)}) async-start(bf16[16,72,256]{2,1,0:T(8,128)(2,1)} %cached.1), calls=%async_computation.1 | async-start | bytes 1179648 | tf_op jit(solution)/shard_map/all_to_all | solution.py:287
  97.2 18.3 %collective-permute-start.3 = (bf16[128,640]{1,0:T(8,128)(2,1)S(1)}, bf16[128,640]{1,0:T(8,128)(2,1)S(1)}, u32[]{:S(2)}, u32[]{:S(2)}) collective-permute-start(bf16[128,640]{1,0:T(8,128)(2,1)S(1)} %bitcast.12), channel_id=1, source_target_pairs={{0,1},{1,0},{2,3},{3,2},{4,5},{5,4},{6,7},{7,6},{8,9},{9,8},{10,11... | collective-permute-start | bytes 491528 | tf_op jit(solution)/shard_map/ppermute | solution.py:265
  99.7 15.7 %collective-permute-start.4 = (bf16[128,640]{1,0:T(8,128)(2,1)S(1)}, bf16[128,640]{1,0:T(8,128)(2,1)S(1)}, u32[]{:S(2)}, u32[]{:S(2)}) collective-permute-start(bf16[128,640]{1,0:T(8,128)(2,1)S(1)} %bitcast.13), channel_id=1, source_target_pairs={{0,16},{1,17},{2,18},{3,19},{4,20},{5,21},{6,22},{7,23},{8,24},{9,... | collective-permute-start | bytes 491528 | tf_op jit(solution)/shard_map/ppermute | solution.py:265
  102.5 13.0 %collective-permute-start.5 = (bf16[128,640]{1,0:T(8,128)(2,1)S(1)}, bf16[128,640]{1,0:T(8,128)(2,1)S(1)}, u32[]{:S(2)}, u32[]{:S(2)}) collective-permute-start(bf16[128,640]{1,0:T(8,128)(2,1)S(1)} %bitcast.14), channel_id=1, source_target_pairs={{0,17},{1,16},{2,19},{3,18},{4,21},{5,20},{6,23},{7,22},{8,25},{9,... | collective-permute-start | bytes 491528 | tf_op jit(solution)/shard_map/ppermute | solution.py:265
  108.9 1.0 copy-start.5
where the time goes:
time: 127 us
  starting transfers between devices  53.7 us (42%)
  waiting for transfers between devices  38.3 us (30%)
  Pallas kernels  25.9 us (20%)
  local copies, waits for them, and re-layouts  5.68 us (4%)
  other arithmetic  2.02 us (2%)
    ppermute x6, starting transfers between devices, swap(): return lax.ppermute(array, 'mp', pairs)  17.9 us
    all_to_all x1, starting transfers between devices, on_device(): lax.all_to_all(own.astype(BF).reshape(-1, SUB, COLS), 'mp', 0, 0, tiled=T...  14 us
    all_to_all x1, waiting for transfers between devices, on_device(): got = lax.all_to_all(packed, 'req', 0, 0, tiled=True)  13.2 us
    all_to_all x1, waiting for transfers between devices, on_device(): lax.all_to_all(own.astype(BF).reshape(-1, SUB, COLS), 'mp', 0, 0, tiled=T...  12.3 us
    all_to_all x1, starting transfers between devices, on_device(): got = lax.all_to_all(packed, 'req', 0, 0, tiled=True)  11.2 us
    pallas_call x1, Pallas kernels, on_device(): pl.pallas_call(scan_kernel, out_shape=[jax.ShapeDtypeStruct((rows, channe...  11.1 us
    all_to_all x1, starting transfers between devices, on_device(): back = lax.all_to_all(partial, 'req', 0, 0, tiled=True)  7.2 us
    pallas_call x1, Pallas kernels, on_device(): pl.pallas_call(cached_kernel, out_shape=jax.ShapeDtypeStruct((REQ, RET, c...  6.79 us
  transfers between devices with their start and end apart: 10, of which 6 were waited for; matrix products, arithmetic and copies ran while one was open for 2% of the time, Pallas kernels for 11%

commit v1 on v0

--- a/solution.py
+++ b/solution.py
@@ -21,17 +21,41 @@
 RANK = 512
 COLS = 640
 CHUNK = 128
+BC = 2 * NS
 SUB = 16
 STAT = 64
 RET = 72
 SEND = 96
 
 VMEM = pl.BlockSpec(memory_space=pltpu.VMEM)
+ANY = pl.BlockSpec(memory_space=pl.ANY)
+HBM = pl.BlockSpec(memory_space=pltpu.HBM)
 SMEM = pl.BlockSpec(memory_space=pltpu.SMEM)
-PARAMS = pltpu.CompilerParams(vmem_limit_bytes=40 * 1024 * 1024)
-
-
-def pack_kernel(tab, entries, q_ref, cache_ref, out_ref):
+PARAMS = pltpu.CompilerParams(vmem_limit_bytes=60 * 1024 * 1024)
+
+
+def tail_of(rest):
+    lane = lax.broadcasted_iota(jnp.int32, rest.shape, 1)
+    high = rest.astype(BF).astype(F32)
+    low = pltpu.roll(rest - high, BC, 1)
+    return jnp.where(lane < BC, high, jnp.where(lane < 2 * BC, low, 0.0))
+
+
+def whole_tail(tail):
+    return tail + pltpu.roll(tail, tail.shape[1] - BC, 1)
+
+
+def fetch(pairs, sems):
+    copies = [pltpu.make_async_copy(a, b, sems.at[i]) for i, (a, b) in enumerate(pairs)]
+    for copy in copies:
+        copy.start()
+    return copies
+
+
+def pack_kernel(tab, entries_hbm, q_hbm, cache_hbm, out_ref, entries, q_ref, cache_ref, sems):
+    copies = fetch([(entries_hbm, entries), (q_hbm, q_ref), (cache_hbm, cache_ref)], sems)
+    for copy in copies:
+        copy.wait()
     for p in range(REQ):
         for k in range(2):
             slot = tab[k * REQ + p]
@@ -42,16 +66,50 @@
             out_ref[p, 2 * NEW + k * NS : 2 * NEW + (k + 1) * NS, :] = cache_ref[entry].astype(BF)
 
 
-def project_kernel(place, x_ref, w_ref, own_ref, *sent):
+def project_kernel(place, x_ref, w_ref, after, own_ref, *sent):
     for d in range(4):
         first = pl.multiple_of((place[0] ^ d) * CHUNK, CHUNK)
         rows = x_ref[pl.ds(first, CHUNK), :]
         low = jnp.dot(rows, w_ref[:, :RANK], preferred_element_type=F32)
         rest = jnp.dot(rows, w_ref[:, RANK:], preferred_element_type=F32)
-        out = own_ref if d == 0 else sent[d - 1]
-        out[:, :RANK] = low.astype(out.dtype)
-        pad = jnp.zeros((CHUNK, COLS - RANK - rest.shape[1]), F32)
-        out[:, RANK:] = jnp.concatenate([rest, pad], axis=1).astype(out.dtype)
+        rest = jnp.concatenate([rest, jnp.zeros((CHUNK, COLS - RANK - BC), F32)], axis=1)
+        if d == 0:
+            own_ref[:, :RANK] = low
+            own_ref[:, RANK:] = rest
+        else:
+            sent[d - 1][:, :RANK] = low.astype(BF)
+            sent[d - 1][:, RANK:] = tail_of(rest).astype(BF)
+
+
+def add_four_kernel(own_hbm, h1, h2, h3, after, out_ref, own_ref, r1, r2, r3, sems):
+    for copy in fetch([(own_hbm, own_ref), (h1, r1), (h2, r2), (h3, r3)], sems):
+        copy.wait()
+    low = own_ref[:, :RANK]
+    tail = jnp.zeros((CHUNK, COLS - RANK), F32)
+    for r in (r1, r2, r3):
+        low = low + r[:, :RANK].astype(F32)
+        tail = tail + r[:, RANK:].astype(F32)
+    rest = own_ref[:, RANK:] + whole_tail(tail)
+    low = low.astype(BF)
+    tail = tail_of(rest).astype(BF)
+    for k in range(CHUNK // SUB):
+        out_ref[k, :, :RANK] = low[k * SUB : (k + 1) * SUB]
+        out_ref[k, :, RANK:] = tail[k * SUB : (k + 1) * SUB]
+
+
+def add_eight_kernel(parts, after, out_ref):
+    total = parts[0].astype(F32)
+    for k in range(1, CHUNK // SUB):
+        total = total + parts[k].astype(F32)
+    low = total[:, :RANK].astype(BF)
+    tail = tail_of(whole_tail(total[:, RANK:])).astype(BF)
+    for k in range(CHUNK // SUB):
+        out_ref[k, :, :RANK] = low
+        out_ref[k, :, RANK:] = tail
+
+
+def gate_kernel(partial, a, b, c, out):
+    pass
 
 
 def heads_down(block):
@@ -70,7 +128,7 @@
             stats = []
             for k in range(2):
                 slot = p * REQ + tab[(2 + k) * REQ + p]
-                pages = [pool_ref[table[slot * PAGES + t] - base] for t in range(PAGES)]
+                pages = [pool_ref[table[t * REQ * REQ + slot] - base] for t in range(PAGES)]
                 rows = jnp.concatenate(pages, axis=0)
                 q = heads_down(got_ref[p, k * NEW : (k + 1) * NEW, :])
                 s = lax.dot_general(
@@ -100,17 +158,14 @@
     lax.fori_loop(0, REQ, one_peer, 0)
 
 
-def combine_kernel(tab, fresh_len, q_ref, kv_ref, got_ref, out_ref):
+def fresh_kernel(q_ref, kv_ref, out_ref, stat_ref):
     row = lax.broadcasted_iota(jnp.int32, (2 * NEW, HD), 0)
     lane = lax.broadcasted_iota(jnp.int32, (2 * NEW, HD), 1)
     query = lax.broadcasted_iota(jnp.int32, (2 * NEW, NEW), 0) & (NEW - 1)
     key = lax.broadcasted_iota(jnp.int32, (2 * NEW, NEW), 1)
-    place = lax.broadcasted_iota(jnp.int32, (NEW, 2 * HD), 0)
 
     def one_slot(i, carry):
         first = pl.multiple_of(i * NEW, NEW)
-        owner = tab[5 * REQ + i]
-        second = (tab[REQ + owner] == i).astype(jnp.int32)
         q = heads_down(q_ref[pl.ds(first, NEW), :])
         rows = kv_ref[pl.ds(first, NEW), :]
         s = lax.dot_general(
@@ -120,55 +175,84 @@
         top = jnp.max(s, axis=1, keepdims=True)
         w = jnp.exp(s - top)
         total = jnp.sum(w, axis=1, keepdims=True)
-        o = jnp.dot(w.astype(BF), rows[:, HD:], preferred_element_type=F32)
+        out_ref[i] = jnp.dot(w.astype(BF), rows[:, HD:], preferred_element_type=F32) / total
+        lse = top + jnp.log(total)
+        flat = jnp.sum(jnp.where(row == lane, lse, 0.0), axis=0, keepdims=True)
+        stat_ref[i] = jnp.broadcast_to(flat, (8, HD))
+        return carry
+
+    lax.fori_loop(0, REQ, one_slot, 0, unroll=4)
+
+
+def combine_kernel(place, tab, entries, fresh_len, part_ref, stat_ref, got_ref, after, out_ref):
+    row = lax.broadcasted_iota(jnp.int32, (2 * NEW, HD), 0)
+    lane = lax.broadcasted_iota(jnp.int32, (2 * NEW, HD), 1)
+    spot = lax.broadcasted_iota(jnp.int32, (NEW, 2 * HD), 0)
+
+    def one_slot(i, carry):
+        first = pl.multiple_of(i * NEW, NEW)
+        owner = entries[place[1] * REQ + i] // REQ
+        second = (tab[REQ + owner] == i).astype(jnp.int32)
         old = heads_down(
             got_ref[owner, pl.ds(pl.multiple_of(second * NEW, NEW), NEW), :]
         ).astype(F32)
         stats = got_ref[owner, STAT:RET, :].astype(F32)
         exact = stats[0:2, :HD] + stats[0:2, HD:] + stats[2:4, :HD]
-        flat = jnp.where(second > 0, exact[1:2], exact[0:1])
-        lse = jnp.sum(jnp.where(row == lane, flat, 0.0), axis=1, keepdims=True)
-        most = jnp.maximum(lse, top)
-        share_old = jnp.exp(lse - most)
-        share = jnp.exp(top - most)
-        o = (old * share_old + o * share) / (share_old + total * share)
+        lse_old = jnp.where(second > 0, exact[1:2], exact[0:1])
+        lse = stat_ref[i, 0:1, :]
+        most = jnp.maximum(lse_old, lse)
+        weight_old = jnp.exp(lse_old - most)
+        weight = jnp.exp(lse - most)
+        share_old = weight_old / (weight_old + weight)
+        share_old = jnp.sum(jnp.where(row == lane, share_old, 0.0), axis=1, keepdims=True)
+        share = weight / (weight_old + weight)
+        share = jnp.sum(jnp.where(row == lane, share, 0.0), axis=1, keepdims=True)
+        o = old * share_old + part_ref[i] * share
         o = jnp.concatenate([o[:NEW], o[NEW:]], axis=1)
-        out_ref[pl.ds(first, NEW), :] = jnp.where(place < fresh_len[i], o, 0.0).astype(BF)
+        live = spot < fresh_len[place[1] * REQ + i]
+        out_ref[pl.ds(first, NEW), :] = jnp.where(live, o, 0.0).astype(BF)
         return carry
 
-    lax.fori_loop(0, REQ, one_slot, 0, unroll=2)
+    lax.fori_loop(0, REQ, one_slot, 0, unroll=4)
 
 
 def scan_kernel(
-    tab, place, fresh_len, p0, p1, p2, p3, wdt_ref, b_ref, a_ref, d_ref, x_ref, g_ref, got_ref,
-    out_ref, state_ref, dt_s, u_s, bc_s, y_s, a_s, h_s,
+    place, tab, entries, fresh_len, p0, p1, p2, p3, wdt_hbm, b_ref, a_ref, d_ref, x_hbm, g_hbm, got_hbm,
+    out_ref, state_ref, done_ref, dt_s, u_s, bc_s, y_s, a_s, h_s, wdt_ref, x_ref, g_ref, got_ref, sems,
 ):
+    copies = fetch(
+        [(wdt_hbm, wdt_ref), (x_hbm, x_ref), (got_hbm, got_ref), (g_hbm, g_ref)], sems
+    )
+    done_ref[...] = jnp.zeros(done_ref.shape, F32)
     channels = x_ref.shape[1]
     halves = [slice(c * HD, (c + 1) * HD) for c in range(channels // HD)]
     step = lax.broadcasted_iota(jnp.int32, (NEW, channels), 0)
+    for n in range(NS):
+        a_s[n * 8 : (n + 1) * 8, :] = jnp.broadcast_to(a_ref[n : n + 1, :] * (-LOG2E), (8, channels))
+    copies[0].wait()
+    copies[1].wait()
     for d, part in enumerate((p0, p1, p2, p3)):
         member = place[0] ^ d
         first = pl.multiple_of(member * CHUNK, CHUNK)
         pre = jnp.dot(part[:, :RANK], wdt_ref[...], preferred_element_type=F32) + b_ref[...]
         dt = jnp.maximum(pre, 0.0) + jnp.log1p(jnp.exp(-jnp.abs(pre)))
-        bc_s[pl.ds(first, CHUNK), :] = part[:, RANK:].astype(F32)
+        bc_s[pl.ds(first, CHUNK), :] = whole_tail(part[:, RANK:].astype(F32))
         for j in range(CHUNK // NEW):
             here = pl.multiple_of(first + j * NEW, NEW)
-            live = step < fresh_len[member * (CHUNK // NEW) + j]
+            live = step < fresh_len[place[1] * REQ + member * (CHUNK // NEW) + j]
             masked = jnp.where(live, dt[j * NEW : (j + 1) * NEW], 0.0)
             drive = masked * x_ref[pl.ds(here, NEW), :].astype(F32)
             for c, half in enumerate(halves):
                 dt_s[c, pl.ds(here, NEW), :] = masked[:, half]
                 u_s[c, pl.ds(here, NEW), :] = drive[:, half]
+    copies[2].wait()
     for i in range(REQ):
-        owner = tab[5 * REQ + i]
+        owner = entries[place[1] * REQ + i] // REQ
         second = (tab[REQ + owner] == i).astype(jnp.int32)
         start = pl.multiple_of(2 * NEW + second * NS, NS)
         state = got_ref[owner, pl.ds(start, NS), :].astype(F32)
         for c, half in enumerate(halves):
             h_s[c, i * NS : (i + 1) * NS, :] = state[:, half]
-    for n in range(NS):
-        a_s[n * 8 : (n + 1) * 8, :] = jnp.broadcast_to(a_ref[n : n + 1, :] * (-LOG2E), (8, channels))
     for g in range(2):
         begin = g * 8 * NS
         h0 = tuple(
@@ -197,19 +281,20 @@
                 y_s[c, rows, :] = y[c]
             return tuple(new)
 
-        hs = lax.fori_loop(0, NEW, one_step, h0)
+        hs = lax.fori_loop(0, NEW, one_step, h0, unroll=8)
         for n in range(NS):
             for c in range(len(halves)):
                 h_s[c, pl.ds(begin + n, 8, stride=NS), :] = hs[n][c]
     for c, half in enumerate(halves):
         state_ref[:, half] = h_s[c]
+    copies[3].wait()
     for i in range(REQ):
         rows = slice(i * NEW, (i + 1) * NEW)
         for c, half in enumerate(halves):
             gate = g_ref[rows, half].astype(F32)
             y = y_s[c, rows, :] + d_ref[:, half] * x_ref[rows, half].astype(F32)
             y = y * (gate * jax.nn.sigmoid(gate))
-            out_ref[rows, half] = jnp.where(step[:, half] < fresh_len[i], y, 0.0).astype(BF)
+            out_ref[rows, half] = jnp.where(step[:, half] < fresh_len[place[1] * REQ + i], y, 0.0).astype(BF)
 
 
 def on_device(
@@ -223,25 +308,30 @@
     member = (at // zs) * 2 + (at & 1)
     place = jnp.stack([member, me]).astype(jnp.int32)
 
-    owners = cache_index.reshape(REQ, REQ) // REQ
-    mine = lax.dynamic_slice_in_dim(owners, me, 1, 0)
-    ids = jnp.arange(REQ, dtype=jnp.int32)
+    slots = jnp.arange(REQ * REQ, dtype=jnp.int32)[None, :]
+    peers = jnp.arange(REQ, dtype=jnp.int32)[:, None]
+    owners = (cache_index // REQ)[None, :]
 
     def ends(match):
-        first = jnp.min(jnp.where(match, ids[None, :], REQ), axis=1)
-        last = jnp.max(jnp.where(match, ids[None, :], -1), axis=1)
-        return jnp.minimum(first, REQ - 1), jnp.maximum(last, 0), last >= 0
-
-    q_first, q_last, _ = ends(mine == ids[:, None])
-    s_first, s_last, active = ends(owners == me)
-    tab = jnp.concatenate([q_first, q_last, s_first, s_last, active.astype(jnp.int32), mine[0]])
-    fresh_len = lax.dynamic_slice_in_dim(new_len, me * REQ, REQ, 0)
+        first = jnp.min(jnp.where(match, slots & (REQ - 1), REQ - 1), axis=1)
+        last = jnp.max(jnp.where(match, slots & (REQ - 1), -1), axis=1)
+        return first, jnp.maximum(last, 0), (last >= 0).astype(jnp.int32)
+
+    q_first, q_last, _ = ends((owners == peers) & (slots // REQ == me))
+    s_first, s_last, active = ends((owners == me) & (slots // REQ == peers))
+    tab = jnp.concatenate([q_first, q_last, s_first, s_last, active])
 
     packed = pl.pallas_call(
         pack_kernel,
         out_shape=jax.ShapeDtypeStruct((REQ, SEND, channels), BF),
-        in_specs=[SMEM, SMEM, VMEM, VMEM],
+        in_specs=[SMEM, HBM, HBM, HBM],
         out_specs=VMEM,
+        scratch_shapes=[
+            pltpu.SMEM(cache_index.shape, jnp.int32),
+            pltpu.VMEM(queries.shape, BF),
+            pltpu.VMEM(ssm_cache.shape, F32),
+            pltpu.SemaphoreType.DMA((3,)),
+        ],
         compiler_params=PARAMS,
         name="pack",
     )(tab, cache_index, queries, ssm_cache)
@@ -251,11 +341,11 @@
     own, *sent = pl.pallas_call(
         project_kernel,
         out_shape=[jax.ShapeDtypeStruct((CHUNK, COLS), F32), chunk, chunk, chunk],
-        in_specs=[SMEM, VMEM, VMEM],
+        in_specs=[SMEM, VMEM, VMEM, ANY],
         out_specs=[VMEM] * 4,
         compiler_params=PARAMS,
         name="project",
-    )(place, mixer_in, w_x)
+    )(place, mixer_in, w_x, packed)
 
     def swap(array, d):
         pairs = []
@@ -265,17 +355,20 @@
         return lax.ppermute(array, "mp", pairs)
 
     groups = [[y * zs + 2 * k + b for k in range(zs // 2)] for y in range(2) for b in range(2)]
-    for d in (1, 2, 3):
-        own = own + swap(sent[d - 1], d).astype(F32)
-    parts = lax.all_to_all(
-        own.astype(BF).reshape(-1, SUB, COLS), "mp", 0, 0, tiled=True, axis_index_groups=groups
-    )
-    summed = jnp.sum(parts.astype(F32), axis=0, keepdims=True).astype(BF)
-    whole = lax.all_to_all(
-        jnp.broadcast_to(summed, parts.shape), "mp", 0, 0, tiled=True, axis_index_groups=groups
-    ).reshape(CHUNK, COLS)
-    others = [swap(whole, d) for d in (1, 2, 3)]
-
+    received = [swap(sent[d - 1], d) for d in (1, 2, 3)]
+    split = jax.ShapeDtypeStruct((CHUNK // SUB, SUB, COLS), BF)
+    added = pl.pallas_call(
+        add_four_kernel,
+        out_shape=split,
+        in_specs=[HBM] * 4 + [ANY],
+        out_specs=VMEM,
+        scratch_shapes=[pltpu.VMEM((CHUNK, COLS), F32)]
+        + [pltpu.VMEM((CHUNK, COLS), BF)] * 3
+        + [pltpu.SemaphoreType.DMA((4,))],
+        compiler_params=PARAMS,
+        name="add_four",
+    )(own, *received, got)
+    token = jax.ShapeDtypeStruct((8, HD), F32)
     partial = pl.pallas_call(
         cached_kernel,
         out_shape=jax.ShapeDtypeStruct((REQ, RET, channels), BF),
@@ -283,17 +376,49 @@
         out_specs=VMEM,
         compiler_params=PARAMS,
         name="cached",
-    )(tab, place, page_table.reshape(-1), kept_len, got, kv_pool.reshape(-1, PAGE, channels))
+    )(tab, place, page_table.T.reshape(-1), kept_len, got, kv_pool.reshape(-1, PAGE, channels))
+    block = jax.ShapeDtypeStruct((REQ, 2 * NEW, HD), F32)
+    fresh = pl.pallas_call(
+        fresh_kernel,
+        out_shape=[block, jax.ShapeDtypeStruct((REQ, 8, HD), F32)],
+        in_specs=[VMEM] * 2,
+        out_specs=[VMEM] * 2,
+        compiler_params=PARAMS,
+        name="fresh",
+    )(queries, kv_new.reshape(rows, channels))
+    parts = lax.all_to_all(added, "mp", 0, 0, tiled=True, axis_index_groups=groups)
+    summed = pl.pallas_call(
+        add_eight_kernel,
+        out_shape=split,
+        in_specs=[VMEM, ANY],
+        out_specs=VMEM,
+        compiler_params=PARAMS,
+        name="add_eight",
+    )(parts, fresh[1])
+    whole = lax.all_to_all(summed, "mp", 0, 0, tiled=True, axis_index_groups=groups)
+    whole = whole.reshape(CHUNK, COLS)
+    others = [swap(whole, d) for d in (1, 2, 3)]
+
+    partial = pl.pallas_call(
+        gate_kernel,
+        out_shape=jax.ShapeDtypeStruct(partial.shape, BF),
+        in_specs=[ANY] * 4,
+        out_specs=ANY,
+        input_output_aliases={0: 0},
+        compiler_params=PARAMS,
+        name="gate",
+    )(partial, *others)
     back = lax.all_to_all(partial, "req", 0, 0, tiled=True)
 
-    mixer_out, state_out = pl.pallas_call(
+    mixer_out, state_out, done = pl.pallas_call(
         scan_kernel,
         out_shape=[
             jax.ShapeDtypeStruct((rows, channels), BF),
             jax.ShapeDtypeStruct((REQ * NS, channels), F32),
+            token,
         ],
-        in_specs=[SMEM] * 3 + [VMEM] * 11,
-        out_specs=[VMEM] * 2,
+        in_specs=[SMEM] * 4 + [VMEM] * 4 + [HBM] + [VMEM] * 3 + [HBM] * 3,
+        out_specs=[VMEM] * 3,
         scratch_shapes=[
             pltpu.VMEM((channels // HD, rows, HD), F32),
             pltpu.VMEM((channels // HD, rows, HD), F32),
@@ -301,21 +426,26 @@
             pltpu.VMEM((channels // HD, rows, HD), F32),
             pltpu.VMEM((NS * 8, channels), F32),
             pltpu.VMEM((channels // HD, REQ * NS, HD), F32),
+            pltpu.VMEM(w_dt.shape, BF),
+            pltpu.VMEM((rows, channels), BF),
+            pltpu.VMEM((rows, channels), BF),
+            pltpu.VMEM(got.shape, BF),
+            pltpu.SemaphoreType.DMA((4,)),
         ],
         compiler_params=PARAMS,
         name="scan",
     )(
-        tab, place, fresh_len, whole, *others, w_dt, b_dt.reshape(1, -1), a_rate,
+        place, tab, cache_index, new_len, whole, *others, w_dt, b_dt.reshape(1, -1), a_rate,
         d_skip.reshape(1, -1), mixer_in, gate_in, got,
     )
     attn_out = pl.pallas_call(
         combine_kernel,
         out_shape=jax.ShapeDtypeStruct((rows, channels), BF),
-        in_specs=[SMEM, SMEM, VMEM, VMEM, VMEM],
+        in_specs=[SMEM] * 4 + [VMEM] * 3 + [ANY],
         out_specs=VMEM,
         compiler_params=PARAMS,
         name="combine",
-    )(tab, fresh_len, queries, kv_new.reshape(rows, channels), back)
+    )(place, tab, cache_index, new_len, *fresh, back, done)
     return attn_out, mixer_out, state_out.reshape(REQ, NS, channels)
 
 

time: 127 us -> 131 us (1.031)
  blocking collectives: 0 us -> 19.9 us
  waiting for transfers between devices: 38.3 us -> 18.9 us
  Pallas kernels: 25.9 us -> 31.8 us
  starting transfers between devices: 53.7 us -> 50.8 us
    all_to_all x0 -> x1, blocking collectives: none -> 19.9 us  [on_device(): lax.all_to_all(summed, 'mp', 0, 0, tiled=True, axis_index_groups=groups)]
    all_to_all x1, waiting for transfers between devices: 13.2 us -> 0.01 us  [on_device(): got = lax.all_to_all(packed, 'req', 0, 0, tiled=True)]
    all_to_all x2 -> x1, waiting for transfers between devices: 18.5 us -> 9.75 us  [on_device(): lax.all_to_all(added, 'mp', 0, 0, tiled=True, axis_index_groups=groups)]
    pallas_call x0 -> x4, Pallas kernels: none -> 7.92 us  [the longest x1 4.12 us: on_device(): pl.pallas_call(fresh_kernel, out_shape=[block, jax.ShapeDtypeStruct((REQ,...]
    all_to_all x2 -> x1, starting transfers between devices: 17.4 us -> 14.3 us  [on_device(): lax.all_to_all(added, 'mp', 0, 0, tiled=True, axis_index_groups=groups)]
    pallas_call x1, Pallas kernels: 5.63 us -> 2.7 us  [on_device(): pl.pallas_call(combine_kernel, out_shape=jax.ShapeDtypeStruct((rows, chan...]
    ppermute x6, waiting for transfers between devices: 3.41 us -> 6.04 us  [swap(): return lax.ppermute(array, 'mp', pairs)]
    pallas_call x1, Pallas kernels: 11.1 us -> 8.52 us  [on_device(): pl.pallas_call(scan_kernel, out_shape=[jax.ShapeDtypeStruct((rows, channe...]
  transfers between devices with their start and end apart: 10 -> 9, of which waited for: 6 -> 3; matrix products, arithmetic and copies ran while one was open for 2% -> 2% of each run, Pallas kernels for 11% -> 17%
where the time goes in v1:
time: 131 us; the launch traced here: 130 us
  starting transfers between devices  50.8 us (39%)
  Pallas kernels  31.8 us (24%)
  blocking collectives  19.9 us (15%)
  waiting for transfers between devices  18.9 us (14%)
  local copies, waits for them, and re-layouts  6.02 us (5%)
  other arithmetic  1.49 us (1%)
    all_to_all x1, blocking collectives, on_device(): lax.all_to_all(summed, 'mp', 0, 0, tiled=True, axis_index_groups=groups)  19.9 us
    ppermute x6, starting transfers between devices, swap(): return lax.ppermute(array, 'mp', pairs)  16.7 us
    all_to_all x1, starting transfers between devices, on_device(): lax.all_to_all(added, 'mp', 0, 0, tiled=True, axis_index_groups=groups)  14.3 us
    all_to_all x1, starting transfers between devices, on_device(): got = lax.all_to_all(packed, 'req', 0, 0, tiled=True)  10.3 us
    all_to_all x1, waiting for transfers between devices, on_device(): lax.all_to_all(added, 'mp', 0, 0, tiled=True, axis_index_groups=groups)  9.75 us
    all_to_all x1, starting transfers between devices, on_device(): back = lax.all_to_all(partial, 'req', 0, 0, tiled=True)  9.52 us
    pallas_call x1, Pallas kernels, on_device(): pl.pallas_call(scan_kernel, out_shape=[jax.ShapeDtypeStruct((rows, channe...  8.52 us
    pallas_call x1, Pallas kernels, on_device(): pl.pallas_call(cached_kernel, out_shape=jax.ShapeDtypeStruct((REQ, RET, c...  7.79 us
  transfers between devices with their start and end apart: 9, of which 3 were waited for; matrix products, arithmetic and copies ran while one was open for 2% of the time, Pallas kernels for 17%

profile of v1, /device:TPU:1, one launch (start us, length us, event | category | flops | bytes accessed | tf_op | source)
XLA Modules:
  0.0 129.8 jit_solution(14022347535439415091)
XLA Ops:
  0.7 0.7 broadcast_compare_fusion
  1.6 0.7 concatenate.3.tab
  2.3 2.7 %pack.1.after = bf16[16,96,256]{2,1,0:T(8,128)(2,1)} custom-call(s32[80]{0:T(128)} %concatenate.3.tab, s32[256]{0:T(256)} %entries.3, bf16[512,256]{1,0:T(8,128)(2,1)} %q_hbm.1, f32[16,16,256]{2,1,0:T(8,128)} %cache_hbm.1), custom_call_target="tpu_custom_call" | custom-call | tf_op jit(solution)/shard_map/pack/pallas_call | solution.py:324
  5.0 10.3 %all-to-all-start = ((bf16[16,96,256]{2,1,0:T(8,128)(2,1)}), bf16[16,96,256]{2,1,0:T(8,128)(2,1)S(1)}, u32[]{:S(2)}, u32[]{:S(2)}) async-start(bf16[16,96,256]{2,1,0:T(8,128)(2,1)} %pack.1.after), calls=%async_computation | async-start | bytes 1572864 | tf_op jit(solution)/shard_map/all_to_all | solution.py:338
  15.2 0.9 copy.20.w_ref
  16.2 0.6 pad_add_fusion.place
  16.7 2.2 %project.1 = (f32[128,640]{1,0:T(8,128)}, bf16[128,640]{1,0:T(8,128)(2,1)}, bf16[128,640]{1,0:T(8,128)(2,1)}, bf16[128,640]{1,0:T(8,128)(2,1)}) custom-call(s32[2]{0:T(128)} %pad_add_fusion.place, bf16[512,256]{1,0:T(8,128)(2,1)} %x_hbm.1, bf16[256,544]{1,0:T(8,128)(2,1)} %copy.20.w_ref, bf16[16,96,256]{2,1,0:T(8,128)(2,1)} %pack.1.after), custom_call_target="tpu_custom_call" | custom-call | tf_op jit(solution)/shard_map/project/pallas_call | solution.py:341
  19.0 1.9 %collective-permute-start = (bf16[128,640]{1,0:T(8,128)(2,1)}, bf16[128,640]{1,0:T(8,128)(2,1)S(1)}, u32[]{:S(2)}, u32[]{:S(2)}) collective-permute-start(bf16[128,640]{1,0:T(8,128)(2,1)} %get-tuple-element.15), channel_id=1, source_target_pairs={{0,1},{1,0},{2,3},{3,2},{4,5},{5,4},{6,7},{7,6},{8,9},{9,8},{10,11... | collective-permute-start | bytes 491528 | tf_op jit(solution)/shard_map/ppermute | solution.py:355
  20.9 2.1 %collective-permute-start.1 = (bf16[128,640]{1,0:T(8,128)(2,1)}, bf16[128,640]{1,0:T(8,128)(2,1)S(1)}, u32[]{:S(2)}, u32[]{:S(2)}) collective-permute-start(bf16[128,640]{1,0:T(8,128)(2,1)} %get-tuple-element.16), channel_id=1, source_target_pairs={{0,16},{1,17},{2,18},{3,19},{4,20},{5,21},{6,22},{7,23},{8,24},{9,... | collective-permute-start | bytes 491528 | tf_op jit(solution)/shard_map/ppermute | solution.py:355
  23.0 4.4 %collective-permute-start.2 = (bf16[128,640]{1,0:T(8,128)(2,1)}, bf16[128,640]{1,0:T(8,128)(2,1)S(1)}, u32[]{:S(2)}, u32[]{:S(2)}) collective-permute-start(bf16[128,640]{1,0:T(8,128)(2,1)} %get-tuple-element.17), channel_id=1, source_target_pairs={{0,17},{1,16},{2,19},{3,18},{4,21},{5,20},{6,23},{7,22},{8,25},{9,... | collective-permute-start | bytes 491528 | tf_op jit(solution)/shard_map/ppermute | solution.py:355
  27.4 6.0 %collective-permute-done.1.h2 = bf16[128,640]{1,0:T(8,128)(2,1)S(1)} collective-permute-done((bf16[128,640]{1,0:T(8,128)(2,1)}, bf16[128,640]{1,0:T(8,128)(2,1)S(1)}, u32[]{:S(2)}, u32[]{:S(2)}) %collective-permute-start.1) | collective-permute-done | bytes 163872 | tf_op jit(solution)/shard_map/ppermute | solution.py:355
  33.4 0.6 copy-done.9
  34.1 0.3 copy-done
  34.4 2.1 %add_four.1 = bf16[8,16,640]{2,1,0:T(8,128)(2,1)} custom-call(f32[128,640]{1,0:T(8,128)} %get-tuple-element.14.own_hbm, bf16[128,640]{1,0:T(8,128)(2,1)} %copy-done.8, bf16[128,640]{1,0:T(8,128)(2,1)} %copy-done.9, bf16[128,640]{1,0:T(8,128)(2,1)} %copy-done.10, bf16[16,96,256]{2,1,0:T(8,128)(2,1)} %copy-done), custom_call_target="tpu_custom_call" | custom-call | tf_op jit(solution)/shard_map/add_four/pallas_call | solution.py:360
  36.5 14.3 %all-to-all-start.1 = ((bf16[8,16,640]{2,1,0:T(8,128)(2,1)}), bf16[8,16,640]{2,1,0:T(8,128)(2,1)S(1)}, u32[]{:S(2)}, u32[]{:S(2)}) async-start(bf16[8,16,640]{2,1,0:T(8,128)(2,1)} %add_four.1), calls=%async_computation.1 | async-start | bytes 327680 | tf_op jit(solution)/shard_map/all_to_all | solution.py:389
  50.7 4.1 %fresh.1 = (f32[16,64,128]{2,1,0:T(8,128)}, f32[16,8,128]{2,1,0:T(8,128)}) custom-call(bf16[512,256]{1,0:T(8,128)(2,1)} %q_hbm.1, bf16[512,256]{1,0:T(8,128)(2,1)} %bitcast.16), custom_call_target="tpu_custom_call" | custom-call | tf_op jit(solution)/shard_map/fresh/pallas_call | solution.py:381
  54.8 9.8 %all-to-all-done.1.parts = bf16[8,16,640]{2,1,0:T(8,128)(2,1)S(1)} async-done(((bf16[8,16,640]{2,1,0:T(8,128)(2,1)}), bf16[8,16,640]{2,1,0:T(8,128)(2,1)S(1)}, u32[]{:S(2)}, u32[]{:S(2)}) %all-to-all-start.1) | async-done | bytes 163872 | tf_op jit(solution)/shard_map/all_to_all | solution.py:389
  64.6 0.7 copy-done.6
  65.3 1.7 %add_eight.1 = bf16[8,16,640]{2,1,0:T(8,128)(2,1)} custom-call(bf16[8,16,640]{2,1,0:T(8,128)(2,1)} %copy-done.6, f32[16,8,128]{2,1,0:T(8,128)} %get-tuple-element.13.after.stat_ref), custom_call_target="tpu_custom_call" | custom-call | tf_op jit(solution)/shard_map/add_eight/pallas_call | solution.py:390
  67.0 19.9 %all_to_all.20 = bf16[8,16,640]{2,1,0:T(8,128)(2,1)S(1)} all-to-all(bf16[8,16,640]{2,1,0:T(8,128)(2,1)} %add_eight.1), channel_id=1, replica_groups={{0,2,4,6,8,10,12,14},{1,3,5,7,9,11,13,15},{16,18,20,22,24,26,28,30},{17..., dimensions={0} | all-to-all | bytes 327680 | tf_op jit(solution)/shard_map/all_to_all | solution.py:398
  86.9 2.8 %collective-permute-start.3 = (bf16[128,640]{1,0:T(8,128)(2,1)S(1)}, bf16[128,640]{1,0:T(8,128)(2,1)S(1)}, u32[]{:S(2)}, u32[]{:S(2)}) collective-permute-start(bf16[128,640]{1,0:T(8,128)(2,1)S(1)} %bitcast.12), channel_id=1, source_target_pairs={{0,1},{1,0},{2,3},{3,2},{4,5},{5,4},{6,7},{7,6},{8,9},{9,8},{10,11... | collective-permute-start | bytes 491528 | tf_op jit(solution)/shard_map/ppermute | solution.py:355
  89.7 3.4 %collective-permute-start.4 = (bf16[128,640]{1,0:T(8,128)(2,1)S(1)}, bf16[128,640]{1,0:T(8,128)(2,1)S(1)}, u32[]{:S(2)}, u32[]{:S(2)}) collective-permute-start(bf16[128,640]{1,0:T(8,128)(2,1)S(1)} %bitcast.13), channel_id=1, source_target_pairs={{0,16},{1,17},{2,18},{3,19},{4,20},{5,21},{6,22},{7,23},{8,24},{9,... | collective-permute-start | bytes 491528 | tf_op jit(solution)/shard_map/ppermute | solution.py:355
  93.1 2.1 %collective-permute-start.5 = (bf16[128,640]{1,0:T(8,128)(2,1)S(1)}, bf16[128,640]{1,0:T(8,128)(2,1)S(1)}, u32[]{:S(2)}, u32[]{:S(2)}) collective-permute-start(bf16[128,640]{1,0:T(8,128)(2,1)S(1)} %bitcast.14), channel_id=1, source_target_pairs={{0,17},{1,16},{2,19},{3,18},{4,21},{5,20},{6,23},{7,22},{8,25},{9,... | collective-permute-start | bytes 491528 | tf_op jit(solution)/shard_map/ppermute | solution.py:355
  95.3 0.6 copy.21
  95.9 7.8 %cached.1.partial = bf16[16,72,256]{2,1,0:T(8,128)(2,1)} custom-call(s32[80]{0:T(128)} %concatenate.3.tab, s32[2]{0:T(128)} %pad_add_fusion.place, s32[4096]{0:T(1024)} %bitcast.17, s32[256]{0:T(256)} %kept.1, bf16[16,96,256]{2,1,0:T(8,128)(2,1)} %copy-done, bf16[256,16,256]{2,1,0:T(8,128)(2,1)} %bitcast.11), custom_call_target="tpu_custom_call" | custom-call | tf_op jit(solution)/shard_map/cached/pallas_call | solution.py:372
  103.7 0.6 copy-done.2
  104.4 0.7 copy-done.4
  105.0 9.5 %all-to-all-start.3 = ((bf16[16,72,256]{2,1,0:T(8,128)(2,1)}), bf16[16,72,256]{2,1,0:T(8,128)(2,1)S(1)}, u32[]{:S(2)}, u32[]{:S(2)}) async-start(bf16[16,72,256]{2,1,0:T(8,128)(2,1)} %gate.1), calls=%async_computation.3 | async-start | bytes 1179648 | tf_op jit(solution)/shard_map/all_to_all | solution.py:411
  114.6 8.5 %scan.1 = (bf16[512,256]{1,0:T(8,128)(2,1)}, f32[256,256]{1,0:T(8,128)}, f32[8,128]{1,0:T(8,128)}) custom-call(s32[2]{0:T(128)} %pad_add_fusion.place, s32[80]{0:T(128)} %concatenate.3.tab, s32[256]{0:T(256)} %entries.3, s32[256]{0:T(256)} %fresh_len.3, bf16[128,640]{1,0:T(8,128)(2,1)} %bitcast.15, bf16[128,640]{1,0:T(8,128)(2,1)} %copy-done.2, ...), custom_call_target="tpu_custom_call" | custom-call | tf_op jit(solution)/shard_map/scan/pallas_call | solution.py:413
  123.1 3.1 %all-to-all-done.3.got_ref = bf16[16,72,256]{2,1,0:T(8,128)(2,1)S(1)} async-done(((bf16[16,72,256]{2,1,0:T(8,128)(2,1)}), bf16[16,72,256]{2,1,0:T(8,128)(2,1)S(1)}, u32[]{:S(2)}, u32[]{:S(2)}) %all-to-all-start.3) | async-done | bytes 589856 | tf_op jit(solution)/shard_map/all_to_all | solution.py:411
  126.2 0.8 copy-done.1
  127.1 2.7 %combine.1 = bf16[512,256]{1,0:T(8,128)(2,1)} custom-call(s32[2]{0:T(128)} %pad_add_fusion.place, s32[80]{0:T(128)} %concatenate.3.tab, s32[256]{0:T(256)} %entries.3, s32[256]{0:T(256)} %fresh_len.3, f32[16,64,128]{2,1,0:T(8,128)} %get-tuple-element.12.part_ref, f32[16,8,128]{2,1,0:T(8,128)} %get-tuple-element.13.after.stat_ref, ...), custom_call_target="tpu_custom_call" | custom-call | tf_op jit(solution)/shard_map/combine/pallas_call | solution.py:441
  (30 shorter events, 0.3 us)
Async XLA Ops:
  0.6 14.6 %copy-start.7 = (bf16[256,544]{0,1:T(8,128)(2,1)S(1)}, bf16[256,544]{0,1:T(8,128)(2,1)}, u32[]{:S(2)}) copy-start(bf16[256,544]{0,1:T(8,128)(2,1)} %param.21) | copy-start | bytes 835588
  5.0 28.5 %all-to-all-start = ((bf16[16,96,256]{2,1,0:T(8,128)(2,1)}), bf16[16,96,256]{2,1,0:T(8,128)(2,1)S(1)}, u32[]{:S(2)}, u32[]{:S(2)}) async-start(bf16[16,96,256]{2,1,0:T(8,128)(2,1)} %pack.1.after), calls=%async_computation | async-start | bytes 1572864 | tf_op jit(solution)/shard_map/all_to_all | solution.py:338
  16.7 78.5 %copy-start.11 = (s32[256,16]{0,1:T(8,128)S(1)}, s32[256,16]{0,1:T(8,128)}, u32[]{:S(2)}) copy-start(s32[256,16]{0,1:T(8,128)} %param.29) | copy-start | bytes 49156
  19.0 8.4 %collective-permute-start = (bf16[128,640]{1,0:T(8,128)(2,1)}, bf16[128,640]{1,0:T(8,128)(2,1)S(1)}, u32[]{:S(2)}, u32[]{:S(2)}) collective-permute-start(bf16[128,640]{1,0:T(8,128)(2,1)} %get-tuple-element.15), channel_id=1, source_target_pairs={{0,1},{1,0},{2,3},{3,2},{4,5},{5,4},{6,7},{7,6},{8,9},{9,8},{10,11... | collective-permute-start | bytes 491528 | tf_op jit(solution)/shard_map/ppermute | solution.py:355
  20.9 12.5 %collective-permute-start.1 = (bf16[128,640]{1,0:T(8,128)(2,1)}, bf16[128,640]{1,0:T(8,128)(2,1)S(1)}, u32[]{:S(2)}, u32[]{:S(2)}) collective-permute-start(bf16[128,640]{1,0:T(8,128)(2,1)} %get-tuple-element.16), channel_id=1, source_target_pairs={{0,16},{1,17},{2,18},{3,19},{4,20},{5,21},{6,22},{7,23},{8,24},{9,... | collective-permute-start | bytes 491528 | tf_op jit(solution)/shard_map/ppermute | solution.py:355
  23.0 10.4 %collective-permute-start.2 = (bf16[128,640]{1,0:T(8,128)(2,1)}, bf16[128,640]{1,0:T(8,128)(2,1)S(1)}, u32[]{:S(2)}, u32[]{:S(2)}) collective-permute-start(bf16[128,640]{1,0:T(8,128)(2,1)} %get-tuple-element.17), channel_id=1, source_target_pairs={{0,17},{1,16},{2,19},{3,18},{4,21},{5,20},{6,23},{7,22},{8,25},{9,... | collective-permute-start | bytes 491528 | tf_op jit(solution)/shard_map/ppermute | solution.py:355
  27.4 6.1 %copy-start.8 = (bf16[128,640]{1,0:T(8,128)(2,1)}, bf16[128,640]{1,0:T(8,128)(2,1)S(1)}, u32[]{:S(2)}) copy-start(bf16[128,640]{1,0:T(8,128)(2,1)S(1)} %collective-permute-done.h1) | copy-start | bytes 491524
  33.4 0.7 copy-start.9
  33.4 0.7 copy-start.10
  33.4 1.0 copy-start
  36.5 28.1 %all-to-all-start.1 = ((bf16[8,16,640]{2,1,0:T(8,128)(2,1)}), bf16[8,16,640]{2,1,0:T(8,128)(2,1)S(1)}, u32[]{:S(2)}, u32[]{:S(2)}) async-start(bf16[8,16,640]{2,1,0:T(8,128)(2,1)} %add_four.1), calls=%async_computation.1 | async-start | bytes 327680 | tf_op jit(solution)/shard_map/all_to_all | solution.py:389
  64.6 0.7 copy-start.6
  86.9 18.2 %copy-start.5 = (bf16[8,16,640]{2,1,0:T(8,128)(2,1)}, bf16[8,16,640]{2,1,0:T(8,128)(2,1)S(1)}, u32[]{:S(2)}) copy-start(bf16[8,16,640]{2,1,0:T(8,128)(2,1)S(1)} %all_to_all.20) | copy-start | bytes 491524
  86.9 16.8 %collective-permute-start.3 = (bf16[128,640]{1,0:T(8,128)(2,1)S(1)}, bf16[128,640]{1,0:T(8,128)(2,1)S(1)}, u32[]{:S(2)}, u32[]{:S(2)}) collective-permute-start(bf16[128,640]{1,0:T(8,128)(2,1)S(1)} %bitcast.12), channel_id=1, source_target_pairs={{0,1},{1,0},{2,3},{3,2},{4,5},{5,4},{6,7},{7,6},{8,9},{9,8},{10,11... | collective-permute-start | bytes 491528 | tf_op jit(solution)/shard_map/ppermute | solution.py:355
  89.7 14.0 %collective-permute-start.4 = (bf16[128,640]{1,0:T(8,128)(2,1)S(1)}, bf16[128,640]{1,0:T(8,128)(2,1)S(1)}, u32[]{:S(2)}, u32[]{:S(2)}) collective-permute-start(bf16[128,640]{1,0:T(8,128)(2,1)S(1)} %bitcast.13), channel_id=1, source_target_pairs={{0,16},{1,17},{2,18},{3,19},{4,20},{5,21},{6,22},{7,23},{8,24},{9,... | collective-permute-start | bytes 491528 | tf_op jit(solution)/shard_map/ppermute | solution.py:355
  93.1 10.6 %collective-permute-start.5 = (bf16[128,640]{1,0:T(8,128)(2,1)S(1)}, bf16[128,640]{1,0:T(8,128)(2,1)S(1)}, u32[]{:S(2)}, u32[]{:S(2)}) collective-permute-start(bf16[128,640]{1,0:T(8,128)(2,1)S(1)} %bitcast.14), channel_id=1, source_target_pairs={{0,17},{1,16},{2,19},{3,18},{4,21},{5,20},{6,23},{7,22},{8,25},{9,... | collective-permute-start | bytes 491528 | tf_op jit(solution)/shard_map/ppermute | solution.py:355
  103.7 0.7 copy-start.2
  103.7 0.7 copy-start.3
  104.4 0.7 copy-start.4
  105.0 21.2 %all-to-all-start.3 = ((bf16[16,72,256]{2,1,0:T(8,128)(2,1)}), bf16[16,72,256]{2,1,0:T(8,128)(2,1)S(1)}, u32[]{:S(2)}, u32[]{:S(2)}) async-start(bf16[16,72,256]{2,1,0:T(8,128)(2,1)} %gate.1), calls=%async_computation.3 | async-start | bytes 1179648 | tf_op jit(solution)/shard_map/all_to_all | solution.py:411
  126.2 0.8 copy-start.1

commit v2 on v1

--- a/solution.py
+++ b/solution.py
@@ -31,6 +31,7 @@
 ANY = pl.BlockSpec(memory_space=pl.ANY)
 HBM = pl.BlockSpec(memory_space=pltpu.HBM)
 SMEM = pl.BlockSpec(memory_space=pltpu.SMEM)
+SMALL = pltpu.CompilerParams(vmem_limit_bytes=12 * 1024 * 1024)
 PARAMS = pltpu.CompilerParams(vmem_limit_bytes=60 * 1024 * 1024)
 
 
@@ -81,7 +82,7 @@
             sent[d - 1][:, RANK:] = tail_of(rest).astype(BF)
 
 
-def add_four_kernel(own_hbm, h1, h2, h3, after, out_ref, own_ref, r1, r2, r3, sems):
+def add_four_kernel(own_hbm, h1, h2, h3, after, also, out_ref, own_ref, r1, r2, r3, sems):
     for copy in fetch([(own_hbm, own_ref), (h1, r1), (h2, r2), (h3, r3)], sems):
         copy.wait()
     low = own_ref[:, :RANK]
@@ -108,7 +109,7 @@
         out_ref[k, :, RANK:] = tail
 
 
-def gate_kernel(partial, a, b, c, out):
+def gate_kernel(partial, after, out):
     pass
 
 
@@ -116,7 +117,8 @@
     return jnp.concatenate([block[:, :HD], block[:, HD:]], axis=0)
 
 
-def cached_kernel(tab, place, table, kept, got_ref, pool_ref, out_ref):
+def cached_kernel(tab, place, table, kept, got_ref, pool_ref, out_ref, done_ref):
+    done_ref[...] = jnp.zeros(done_ref.shape, F32)
     row = lax.broadcasted_iota(jnp.int32, (2 * NEW, HD), 0)
     lane = lax.broadcasted_iota(jnp.int32, (2 * NEW, HD), 1)
     key = lax.broadcasted_iota(jnp.int32, (2 * NEW, KEEP), 1)
@@ -217,7 +219,7 @@
 
 
 def scan_kernel(
-    place, tab, entries, fresh_len, p0, p1, p2, p3, wdt_hbm, b_ref, a_ref, d_ref, x_hbm, g_hbm, got_hbm,
+    place, tab, entries, fresh_len, low_ref, wdt_hbm, b_ref, a_ref, d_ref, x_hbm, g_hbm, got_hbm,
     out_ref, state_ref, done_ref, dt_s, u_s, bc_s, y_s, a_s, h_s, wdt_ref, x_ref, g_ref, got_ref, sems,
 ):
     copies = fetch(
@@ -231,14 +233,14 @@
         a_s[n * 8 : (n + 1) * 8, :] = jnp.broadcast_to(a_ref[n : n + 1, :] * (-LOG2E), (8, channels))
     copies[0].wait()
     copies[1].wait()
-    for d, part in enumerate((p0, p1, p2, p3)):
-        member = place[0] ^ d
-        first = pl.multiple_of(member * CHUNK, CHUNK)
+    for member in range(4):
+        part = low_ref[member]
+        first = member * CHUNK
         pre = jnp.dot(part[:, :RANK], wdt_ref[...], preferred_element_type=F32) + b_ref[...]
         dt = jnp.maximum(pre, 0.0) + jnp.log1p(jnp.exp(-jnp.abs(pre)))
         bc_s[pl.ds(first, CHUNK), :] = whole_tail(part[:, RANK:].astype(F32))
         for j in range(CHUNK // NEW):
-            here = pl.multiple_of(first + j * NEW, NEW)
+            here = first + j * NEW
             live = step < fresh_len[place[1] * REQ + member * (CHUNK // NEW) + j]
             masked = jnp.where(live, dt[j * NEW : (j + 1) * NEW], 0.0)
             drive = masked * x_ref[pl.ds(here, NEW), :].astype(F32)
@@ -354,29 +356,10 @@
             pairs.append((i, (y ^ (d >> 1)) * zs + (z ^ (d & 1))))
         return lax.ppermute(array, "mp", pairs)
 
+    quads = [[y * zs + 2 * k + b for y in range(2) for b in range(2)] for k in range(zs // 2)]
     groups = [[y * zs + 2 * k + b for k in range(zs // 2)] for y in range(2) for b in range(2)]
     received = [swap(sent[d - 1], d) for d in (1, 2, 3)]
     split = jax.ShapeDtypeStruct((CHUNK // SUB, SUB, COLS), BF)
-    added = pl.pallas_call(
-        add_four_kernel,
-        out_shape=split,
-        in_specs=[HBM] * 4 + [ANY],
-        out_specs=VMEM,
-        scratch_shapes=[pltpu.VMEM((CHUNK, COLS), F32)]
-        + [pltpu.VMEM((CHUNK, COLS), BF)] * 3
-        + [pltpu.SemaphoreType.DMA((4,))],
-        compiler_params=PARAMS,
-        name="add_four",
-    )(own, *received, got)
-    token = jax.ShapeDtypeStruct((8, HD), F32)
-    partial = pl.pallas_call(
-        cached_kernel,
-        out_shape=jax.ShapeDtypeStruct((REQ, RET, channels), BF),
-        in_specs=[SMEM, SMEM, SMEM, SMEM, VMEM, VMEM],
-        out_specs=VMEM,
-        compiler_params=PARAMS,
-        name="cached",
-    )(tab, place, page_table.T.reshape(-1), kept_len, got, kv_pool.reshape(-1, PAGE, channels))
     block = jax.ShapeDtypeStruct((REQ, 2 * NEW, HD), F32)
     fresh = pl.pallas_call(
         fresh_kernel,
@@ -386,28 +369,48 @@
         compiler_params=PARAMS,
         name="fresh",
     )(queries, kv_new.reshape(rows, channels))
+    added = pl.pallas_call(
+        add_four_kernel,
+        out_shape=split,
+        in_specs=[HBM] * 4 + [ANY] * 2,
+        out_specs=VMEM,
+        scratch_shapes=[pltpu.VMEM((CHUNK, COLS), F32)]
+        + [pltpu.VMEM((CHUNK, COLS), BF)] * 3
+        + [pltpu.SemaphoreType.DMA((4,))],
+        compiler_params=PARAMS,
+        name="add_four",
+    )(own, *received, got, fresh[1])
+    token = jax.ShapeDtypeStruct((8, HD), F32)
+    partial, cached = pl.pallas_call(
+        cached_kernel,
+        out_shape=[jax.ShapeDtypeStruct((REQ, RET, channels), BF), token],
+        in_specs=[SMEM, SMEM, SMEM, SMEM, VMEM, VMEM],
+        out_specs=[VMEM] * 2,
+        compiler_params=SMALL,
+        name="cached",
+    )(tab, place, page_table.T.reshape(-1), kept_len, got, kv_pool.reshape(-1, PAGE, channels))
     parts = lax.all_to_all(added, "mp", 0, 0, tiled=True, axis_index_groups=groups)
     summed = pl.pallas_call(
         add_eight_kernel,
         out_shape=split,
         in_specs=[VMEM, ANY],
         out_specs=VMEM,
-        compiler_params=PARAMS,
+        compiler_params=SMALL,
         name="add_eight",
-    )(parts, fresh[1])
+    )(parts, cached)
     whole = lax.all_to_all(summed, "mp", 0, 0, tiled=True, axis_index_groups=groups)
-    whole = whole.reshape(CHUNK, COLS)
-    others = [swap(whole, d) for d in (1, 2, 3)]
+    whole = jnp.broadcast_to(whole.reshape(1, CHUNK, COLS), (4, CHUNK, COLS))
+    whole = lax.all_to_all(whole, "mp", 0, 0, tiled=True, axis_index_groups=quads)
 
     partial = pl.pallas_call(
         gate_kernel,
         out_shape=jax.ShapeDtypeStruct(partial.shape, BF),
-        in_specs=[ANY] * 4,
+        in_specs=[ANY] * 2,
         out_specs=ANY,
         input_output_aliases={0: 0},
         compiler_params=PARAMS,
         name="gate",
-    )(partial, *others)
+    )(partial, whole)
     back = lax.all_to_all(partial, "req", 0, 0, tiled=True)
 
     mixer_out, state_out, done = pl.pallas_call(
@@ -417,7 +420,7 @@
             jax.ShapeDtypeStruct((REQ * NS, channels), F32),
             token,
         ],
-        in_specs=[SMEM] * 4 + [VMEM] * 4 + [HBM] + [VMEM] * 3 + [HBM] * 3,
+        in_specs=[SMEM] * 4 + [VMEM, HBM] + [VMEM] * 3 + [HBM] * 3,
         out_specs=[VMEM] * 3,
         scratch_shapes=[
             pltpu.VMEM((channels // HD, rows, HD), F32),
@@ -435,7 +438,7 @@
         compiler_params=PARAMS,
         name="scan",
     )(
-        place, tab, cache_index, new_len, whole, *others, w_dt, b_dt.reshape(1, -1), a_rate,
+        place, tab, cache_index, new_len, whole, w_dt, b_dt.reshape(1, -1), a_rate,
         d_skip.reshape(1, -1), mixer_in, gate_in, got,
     )
     attn_out = pl.pallas_call(

time: 131 us -> 120 us (0.916)
  blocking collectives: 19.9 us -> 30.1 us
  starting transfers between devices: 50.8 us -> 42 us
  waiting for transfers between devices: 18.9 us -> 11.1 us
  Pallas kernels: 31.8 us -> 28.4 us
    all_to_all x0 -> x1, blocking collectives: none -> 10.4 us  [on_device(): lax.all_to_all(whole, 'mp', 0, 0, tiled=True, axis_index_groups=quads)]
    ppermute x6 -> x3, starting transfers between devices: 16.7 us -> 8.36 us  [swap(): return lax.ppermute(array, 'mp', pairs)]
    ppermute x6 -> x3, waiting for transfers between devices: 6.04 us -> 1.96 us  [swap(): return lax.ppermute(array, 'mp', pairs)]
    all_to_all x1, waiting for transfers between devices: 9.75 us -> 5.89 us  [on_device(): lax.all_to_all(added, 'mp', 0, 0, tiled=True, axis_index_groups=groups)]
    pallas_call x1, Pallas kernels: 7.79 us -> 5.95 us  [on_device(): pl.pallas_call(cached_kernel, out_shape=[jax.ShapeDtypeStruct((REQ, RET,...]
    pallas_call x1, Pallas kernels: 1.74 us -> 0.17 us  [on_device(): pl.pallas_call(add_eight_kernel, out_shape=split, in_specs=[VMEM, ANY], o...]
    unnamed x26 -> x28, local copies, waits for them, and re-layouts: 5.34 us -> 4.68 us
  transfers between devices with their start and end apart: 9 -> 6, of which waited for: 3 -> 3; matrix products, arithmetic and copies ran while one was open for 2% -> 1% of each run, Pallas kernels for 17% -> 17%
where the time goes in v2:
time: 120 us; the launch traced here: 119 us
  starting transfers between devices  42 us (35%)
  blocking collectives  30.1 us (25%)
  Pallas kernels  28.4 us (24%)
  waiting for transfers between devices  11.1 us (9%)
  local copies, waits for them, and re-layouts  5.35 us (4%)
  other arithmetic  1.48 us (1%)
    all_to_all x1, blocking collectives, on_device(): lax.all_to_all(summed, 'mp', 0, 0, tiled=True, axis_index_groups=groups)  19.7 us
    all_to_all x1, starting transfers between devices, on_device(): lax.all_to_all(added, 'mp', 0, 0, tiled=True, axis_index_groups=groups)  14.1 us
    all_to_all x1, blocking collectives, on_device(): lax.all_to_all(whole, 'mp', 0, 0, tiled=True, axis_index_groups=quads)  10.4 us
    all_to_all x1, starting transfers between devices, on_device(): got = lax.all_to_all(packed, 'req', 0, 0, tiled=True)  10.3 us
    all_to_all x1, starting transfers between devices, on_device(): back = lax.all_to_all(partial, 'req', 0, 0, tiled=True)  9.26 us
    pallas_call x1, Pallas kernels, on_device(): pl.pallas_call(scan_kernel, out_shape=[jax.ShapeDtypeStruct((rows, channe...  8.43 us
    ppermute x3, starting transfers between devices, swap(): return lax.ppermute(array, 'mp', pairs)  8.36 us
    pallas_call x1, Pallas kernels, on_device(): pl.pallas_call(cached_kernel, out_shape=[jax.ShapeDtypeStruct((REQ, RET,...  5.95 us
  transfers between devices with their start and end apart: 6, of which 3 were waited for; matrix products, arithmetic and copies ran while one was open for 1% of the time, Pallas kernels for 17%

profile of v2, /device:TPU:1, one launch (start us, length us, event | category | flops | bytes accessed | tf_op | source)
XLA Modules:
  0.0 119.3 jit_solution(8946675803473149460)
XLA Ops:
  0.7 0.7 broadcast_compare_fusion
  1.4 0.2 select_reduce_fusion
  1.6 0.6 concatenate.3.tab
  2.2 2.7 %pack.1.after = bf16[16,96,256]{2,1,0:T(8,128)(2,1)} custom-call(s32[80]{0:T(128)} %concatenate.3.tab, s32[256]{0:T(256)} %entries.3, bf16[512,256]{1,0:T(8,128)(2,1)} %q_hbm.1, f32[16,16,256]{2,1,0:T(8,128)} %cache_hbm.1), custom_call_target="tpu_custom_call" | custom-call | tf_op jit(solution)/shard_map/pack/pallas_call | solution.py:326
  4.9 10.3 %all-to-all-start = ((bf16[16,96,256]{2,1,0:T(8,128)(2,1)}), bf16[16,96,256]{2,1,0:T(8,128)(2,1)S(1)}, u32[]{:S(2)}, u32[]{:S(2)}) async-start(bf16[16,96,256]{2,1,0:T(8,128)(2,1)} %pack.1.after), calls=%async_computation | async-start | bytes 1572864 | tf_op jit(solution)/shard_map/all_to_all | solution.py:340
  15.2 0.9 copy.20.w_ref
  16.1 0.6 pad_add_fusion.place
  16.7 2.3 %project.1 = (f32[128,640]{1,0:T(8,128)}, bf16[128,640]{1,0:T(8,128)(2,1)}, bf16[128,640]{1,0:T(8,128)(2,1)}, bf16[128,640]{1,0:T(8,128)(2,1)}) custom-call(s32[2]{0:T(128)} %pad_add_fusion.place, bf16[512,256]{1,0:T(8,128)(2,1)} %x_hbm.1, bf16[256,544]{1,0:T(8,128)(2,1)} %copy.20.w_ref, bf16[16,96,256]{2,1,0:T(8,128)(2,1)} %pack.1.after), custom_call_target="tpu_custom_call" | custom-call | tf_op jit(solution)/shard_map/project/pallas_call | solution.py:343
  19.0 1.9 %collective-permute-start = (bf16[128,640]{1,0:T(8,128)(2,1)}, bf16[128,640]{1,0:T(8,128)(2,1)S(1)}, u32[]{:S(2)}, u32[]{:S(2)}) collective-permute-start(bf16[128,640]{1,0:T(8,128)(2,1)} %get-tuple-element.18), channel_id=1, source_target_pairs={{0,1},{1,0},{2,3},{3,2},{4,5},{5,4},{6,7},{7,6},{8,9},{9,8},{10,11... | collective-permute-start | bytes 491528 | tf_op jit(solution)/shard_map/ppermute | solution.py:357
  20.9 2.1 %collective-permute-start.1 = (bf16[128,640]{1,0:T(8,128)(2,1)}, bf16[128,640]{1,0:T(8,128)(2,1)S(1)}, u32[]{:S(2)}, u32[]{:S(2)}) collective-permute-start(bf16[128,640]{1,0:T(8,128)(2,1)} %get-tuple-element.19), channel_id=1, source_target_pairs={{0,16},{1,17},{2,18},{3,19},{4,20},{5,21},{6,22},{7,23},{8,24},{9,... | collective-permute-start | bytes 491528 | tf_op jit(solution)/shard_map/ppermute | solution.py:357
  23.0 4.3 %collective-permute-start.2 = (bf16[128,640]{1,0:T(8,128)(2,1)}, bf16[128,640]{1,0:T(8,128)(2,1)S(1)}, u32[]{:S(2)}, u32[]{:S(2)}) collective-permute-start(bf16[128,640]{1,0:T(8,128)(2,1)} %get-tuple-element.20), channel_id=1, source_target_pairs={{0,17},{1,16},{2,19},{3,18},{4,21},{5,20},{6,23},{7,22},{8,25},{9,... | collective-permute-start | bytes 491528 | tf_op jit(solution)/shard_map/ppermute | solution.py:357
  27.3 4.1 %fresh.1 = (f32[16,64,128]{2,1,0:T(8,128)}, f32[16,8,128]{2,1,0:T(8,128)}) custom-call(bf16[512,256]{1,0:T(8,128)(2,1)} %q_hbm.1, bf16[512,256]{1,0:T(8,128)(2,1)} %bitcast.14), custom_call_target="tpu_custom_call" | custom-call | tf_op jit(solution)/shard_map/fresh/pallas_call | solution.py:364
  31.5 0.0 collective-permute-done.h1
  31.5 2.0 %collective-permute-done.1.h2 = bf16[128,640]{1,0:T(8,128)(2,1)S(1)} collective-permute-done((bf16[128,640]{1,0:T(8,128)(2,1)}, bf16[128,640]{1,0:T(8,128)(2,1)S(1)}, u32[]{:S(2)}, u32[]{:S(2)}) %collective-permute-start.1) | collective-permute-done | bytes 163872 | tf_op jit(solution)/shard_map/ppermute | solution.py:357
  33.5 0.6 copy-done.10
  34.1 0.1 copy-done.11
  34.2 0.3 copy-done
  34.4 2.0 %add_four.1 = bf16[8,16,640]{2,1,0:T(8,128)(2,1)} custom-call(f32[128,640]{1,0:T(8,128)} %get-tuple-element.17.own_hbm, bf16[128,640]{1,0:T(8,128)(2,1)} %copy-done.9, bf16[128,640]{1,0:T(8,128)(2,1)} %copy-done.10, bf16[128,640]{1,0:T(8,128)(2,1)} %copy-done.11, bf16[16,96,256]{2,1,0:T(8,128)(2,1)} %copy-done, f32[16,8,128]{2,1,0:T(8,128)} %get-tuple-element.15.also.stat_ref), custom_call_target="tpu_custom_call" | custom-call | tf_op jit(solution)/shard_map/add_four/pallas_call | solution.py:372
  36.5 14.1 %all-to-all-start.1 = ((bf16[8,16,640]{2,1,0:T(8,128)(2,1)}), bf16[8,16,640]{2,1,0:T(8,128)(2,1)S(1)}, u32[]{:S(2)}, u32[]{:S(2)}) async-start(bf16[8,16,640]{2,1,0:T(8,128)(2,1)} %add_four.1), calls=%async_computation.1 | async-start | bytes 327680 | tf_op jit(solution)/shard_map/all_to_all | solution.py:392
  50.7 1.1 copy-done.1
  51.8 5.9 %cached.1 = (bf16[16,72,256]{2,1,0:T(8,128)(2,1)S(1)}, f32[8,128]{1,0:T(8,128)S(1)}) custom-call(s32[80]{0:T(128)S(1)} %copy-done.4, s32[2]{0:T(128)S(1)} %copy-done.5, s32[4096]{0:T(1024)S(1)} %bitcast.12, s32[256]{0:T(256)S(1)} %copy-done.6, bf16[16,96,256]{2,1,0:T(8,128)(2,1)S(1)} %copy-done.1, bf16[256,16,256]{2,1,0:T(8,128)(2,1)S(1)} %bitcast.11), custom_call_target="tpu_custom_call" | custom-call | tf_op jit(solution)/shard_map/cached/pallas_call | solution.py:384
  57.8 0.8 copy-done.2
  58.6 5.9 %all-to-all-done.1.parts = bf16[8,16,640]{2,1,0:T(8,128)(2,1)S(1)} async-done(((bf16[8,16,640]{2,1,0:T(8,128)(2,1)}), bf16[8,16,640]{2,1,0:T(8,128)(2,1)S(1)}, u32[]{:S(2)}, u32[]{:S(2)}) %all-to-all-start.1) | async-done | bytes 163872 | tf_op jit(solution)/shard_map/all_to_all | solution.py:392
  64.5 0.2 add_eight.1
  64.7 19.7 %all_to_all.25 = bf16[8,16,640]{2,1,0:T(8,128)(2,1)S(1)} all-to-all(bf16[8,16,640]{2,1,0:T(8,128)(2,1)S(1)} %add_eight.1), channel_id=1, replica_groups={{0,2,4,6,8,10,12,14},{1,3,5,7,9,11,13,15},{16,18,20,22,24,26,28,30},{17..., dimensions={0} | all-to-all | bytes 327680 | tf_op jit(solution)/shard_map/all_to_all | solution.py:401
  84.4 0.1 broadcast_in_dim.46
  84.4 10.4 %all_to_all.26.after.low_ref = bf16[4,128,640]{2,1,0:T(8,128)(2,1)} all-to-all(bf16[4,128,640]{2,1,0:T(8,128)(2,1)S(1)} %broadcast_in_dim.46), channel_id=1, replica_groups={{0,1,16,17},{2,3,18,19},{4,5,20,21},{6,7,22,23},{8,9,24,25},{10,11,26,2..., dimensions={0} | all-to-all | bytes 1310720 | tf_op jit(solution)/shard_map/all_to_all | solution.py:403
  94.8 9.3 %all-to-all-start.4 = ((bf16[16,72,256]{2,1,0:T(8,128)(2,1)}), bf16[16,72,256]{2,1,0:T(8,128)(2,1)S(1)}, u32[]{:S(2)}, u32[]{:S(2)}) async-start(bf16[16,72,256]{2,1,0:T(8,128)(2,1)} %gate.1), calls=%async_computation.4 | async-start | bytes 1179648 | tf_op jit(solution)/shard_map/all_to_all | solution.py:414
  104.1 8.4 %scan.1 = (bf16[512,256]{1,0:T(8,128)(2,1)}, f32[256,256]{1,0:T(8,128)}, f32[8,128]{1,0:T(8,128)}) custom-call(s32[2]{0:T(128)} %pad_add_fusion.place, s32[80]{0:T(128)} %concatenate.3.tab, s32[256]{0:T(256)} %entries.3, s32[256]{0:T(256)} %fresh_len.3, bf16[4,128,640]{2,1,0:T(8,128)(2,1)} %all_to_all.26.after.low_ref, bf16[512,256]{1,0:T(8,128)(2,1)} %wdt_hbm.1, ...), custom_call_target="tpu_custom_call" | custom-call | tf_op jit(solution)/shard_map/scan/pallas_call | solution.py:416
  112.5 3.2 %all-to-all-done.4.got_ref = bf16[16,72,256]{2,1,0:T(8,128)(2,1)S(1)} async-done(((bf16[16,72,256]{2,1,0:T(8,128)(2,1)}), bf16[16,72,256]{2,1,0:T(8,128)(2,1)S(1)}, u32[]{:S(2)}, u32[]{:S(2)}) %all-to-all-start.4) | async-done | bytes 589856 | tf_op jit(solution)/shard_map/all_to_all | solution.py:414
  115.7 0.8 copy-done.7
  116.6 2.7 %combine.1 = bf16[512,256]{1,0:T(8,128)(2,1)} custom-call(s32[2]{0:T(128)} %pad_add_fusion.place, s32[80]{0:T(128)} %concatenate.3.tab, s32[256]{0:T(256)} %entries.3, s32[256]{0:T(256)} %fresh_len.3, f32[16,64,128]{2,1,0:T(8,128)} %get-tuple-element.14.part_ref, f32[16,8,128]{2,1,0:T(8,128)} %get-tuple-element.15.also.stat_ref, ...), custom_call_target="tpu_custom_call" | custom-call | tf_op jit(solution)/shard_map/combine/pallas_call | solution.py:444
  (28 shorter events, 0.1 us)
Async XLA Ops:
  0.6 14.6 %copy-start.8 = (bf16[256,544]{0,1:T(8,128)(2,1)S(1)}, bf16[256,544]{0,1:T(8,128)(2,1)}, u32[]{:S(2)}) copy-start(bf16[256,544]{0,1:T(8,128)(2,1)} %param.21) | copy-start | bytes 835588
  4.9 28.6 %all-to-all-start = ((bf16[16,96,256]{2,1,0:T(8,128)(2,1)}), bf16[16,96,256]{2,1,0:T(8,128)(2,1)S(1)}, u32[]{:S(2)}, u32[]{:S(2)}) async-start(bf16[16,96,256]{2,1,0:T(8,128)(2,1)} %pack.1.after), calls=%async_computation | async-start | bytes 1572864 | tf_op jit(solution)/shard_map/all_to_all | solution.py:340
  16.1 34.5 %copy-start.12 = (s32[256,16]{0,1:T(8,128)S(1)}, s32[256,16]{0,1:T(8,128)}, u32[]{:S(2)}) copy-start(s32[256,16]{0,1:T(8,128)} %param.29) | copy-start | bytes 49156
  16.1 34.6 %copy-start.3 = (bf16[256,16,1,256]{3,1,2,0:T(8,128)(2,1)S(1)}, bf16[256,16,1,256]{3,1,2,0:T(8,128)(2,1)}, u32[]{:S(2)}) copy-start(bf16[256,16,1,256]{3,1,2,0:T(8,128)(2,1)} %param.17) | copy-start | bytes 6291460
  16.1 34.6 %copy-start.4 = (s32[80]{0:T(128)S(1)}, s32[80]{0:T(128)}, u32[]{:S(2)}) copy-start(s32[80]{0:T(128)} %concatenate.3.tab) | copy-start | bytes 964
  16.1 34.6 %copy-start.6 = (s32[256]{0:T(256)S(1)}, s32[256]{0:T(256)}, u32[]{:S(2)}) copy-start(s32[256]{0:T(256)} %kept.1) | copy-start | bytes 3076
  16.7 34.0 %copy-start.5 = (s32[2]{0:T(128)S(1)}, s32[2]{0:T(128)}, u32[]{:S(2)}) copy-start(s32[2]{0:T(128)} %pad_add_fusion.place) | copy-start | bytes 28
  19.0 12.5 %collective-permute-start = (bf16[128,640]{1,0:T(8,128)(2,1)}, bf16[128,640]{1,0:T(8,128)(2,1)S(1)}, u32[]{:S(2)}, u32[]{:S(2)}) collective-permute-start(bf16[128,640]{1,0:T(8,128)(2,1)} %get-tuple-element.18), channel_id=1, source_target_pairs={{0,1},{1,0},{2,3},{3,2},{4,5},{5,4},{6,7},{7,6},{8,9},{9,8},{10,11... | collective-permute-start | bytes 491528 | tf_op jit(solution)/shard_map/ppermute | solution.py:357
  20.9 12.6 %collective-permute-start.1 = (bf16[128,640]{1,0:T(8,128)(2,1)}, bf16[128,640]{1,0:T(8,128)(2,1)S(1)}, u32[]{:S(2)}, u32[]{:S(2)}) collective-permute-start(bf16[128,640]{1,0:T(8,128)(2,1)} %get-tuple-element.19), channel_id=1, source_target_pairs={{0,16},{1,17},{2,18},{3,19},{4,20},{5,21},{6,22},{7,23},{8,24},{9,... | collective-permute-start | bytes 491528 | tf_op jit(solution)/shard_map/ppermute | solution.py:357
  23.0 10.4 %collective-permute-start.2 = (bf16[128,640]{1,0:T(8,128)(2,1)}, bf16[128,640]{1,0:T(8,128)(2,1)S(1)}, u32[]{:S(2)}, u32[]{:S(2)}) collective-permute-start(bf16[128,640]{1,0:T(8,128)(2,1)} %get-tuple-element.20), channel_id=1, source_target_pairs={{0,17},{1,16},{2,19},{3,18},{4,21},{5,20},{6,23},{7,22},{8,25},{9,... | collective-permute-start | bytes 491528 | tf_op jit(solution)/shard_map/ppermute | solution.py:357
  31.5 2.0 %copy-start.9 = (bf16[128,640]{1,0:T(8,128)(2,1)}, bf16[128,640]{1,0:T(8,128)(2,1)S(1)}, u32[]{:S(2)}) copy-start(bf16[128,640]{1,0:T(8,128)(2,1)S(1)} %collective-permute-done.h1) | copy-start | bytes 491524
  33.4 0.7 copy-start.10
  33.4 0.7 copy-start.11
  33.5 1.0 copy-start
  36.5 28.0 %all-to-all-start.1 = ((bf16[8,16,640]{2,1,0:T(8,128)(2,1)}), bf16[8,16,640]{2,1,0:T(8,128)(2,1)S(1)}, u32[]{:S(2)}, u32[]{:S(2)}) async-start(bf16[8,16,640]{2,1,0:T(8,128)(2,1)} %add_four.1), calls=%async_computation.1 | async-start | bytes 327680 | tf_op jit(solution)/shard_map/all_to_all | solution.py:392
  50.7 1.1 copy-start.1
  57.8 0.8 copy-start.2
  94.8 20.9 %all-to-all-start.4 = ((bf16[16,72,256]{2,1,0:T(8,128)(2,1)}), bf16[16,72,256]{2,1,0:T(8,128)(2,1)S(1)}, u32[]{:S(2)}, u32[]{:S(2)}) async-start(bf16[16,72,256]{2,1,0:T(8,128)(2,1)} %gate.1), calls=%async_computation.4 | async-start | bytes 1179648 | tf_op jit(solution)/shard_map/all_to_all | solution.py:414
  115.7 0.8 copy-start.7

commit v3 on v2

--- a/solution.py
+++ b/solution.py
@@ -26,6 +26,7 @@
 STAT = 64
 RET = 72
 SEND = 96
+TABLE = 6 * REQ
 
 VMEM = pl.BlockSpec(memory_space=pltpu.VMEM)
 ANY = pl.BlockSpec(memory_space=pl.ANY)
@@ -53,10 +54,30 @@
     return copies
 
 
-def pack_kernel(tab, entries_hbm, q_hbm, cache_hbm, out_ref, entries, q_ref, cache_ref, sems):
+def pack_kernel(entries_hbm, q_hbm, cache_hbm, out_ref, tab, entries, q_ref, cache_ref, sems):
     copies = fetch([(entries_hbm, entries), (q_hbm, q_ref), (cache_hbm, cache_ref)], sems)
-    for copy in copies:
-        copy.wait()
+    me = lax.axis_index("req")
+    for i in range(TABLE):
+        tab[i] = 0
+    copies[0].wait()
+    for i in range(REQ):
+        owner = entries[me * REQ + i] // REQ
+        count = tab[5 * REQ + owner]
+        tab[jnp.minimum(count, 1) * REQ + owner] = i
+        tab[5 * REQ + owner] = count + 1
+
+    def one_peer(p, carry):
+        count = jnp.int32(0)
+        for i in range(REQ):
+            match = entries[p * REQ + i] // REQ == me
+            tab[jnp.where(match, (2 + jnp.minimum(count, 1)) * REQ, 5 * REQ) + p] = i
+            count = count + match.astype(jnp.int32)
+        tab[4 * REQ + p] = count
+        return carry
+
+    lax.fori_loop(0, REQ, one_peer, 0)
+    copies[1].wait()
+    copies[2].wait()
     for p in range(REQ):
         for k in range(2):
             slot = tab[k * REQ + p]
@@ -67,9 +88,11 @@
             out_ref[p, 2 * NEW + k * NS : 2 * NEW + (k + 1) * NS, :] = cache_ref[entry].astype(BF)
 
 
-def project_kernel(place, x_ref, w_ref, after, own_ref, *sent):
+def project_kernel(x_ref, w_ref, after, own_ref, *sent):
+    at = lax.axis_index("mp")
+    member = (at // (lax.axis_size("mp") // 2)) * 2 + (at & 1)
     for d in range(4):
-        first = pl.multiple_of((place[0] ^ d) * CHUNK, CHUNK)
+        first = pl.multiple_of((member ^ d) * CHUNK, CHUNK)
         rows = x_ref[pl.ds(first, CHUNK), :]
         low = jnp.dot(rows, w_ref[:, :RANK], preferred_element_type=F32)
         rest = jnp.dot(rows, w_ref[:, RANK:], preferred_element_type=F32)
@@ -82,9 +105,7 @@
             sent[d - 1][:, RANK:] = tail_of(rest).astype(BF)
 
 
-def add_four_kernel(own_hbm, h1, h2, h3, after, also, out_ref, own_ref, r1, r2, r3, sems):
-    for copy in fetch([(own_hbm, own_ref), (h1, r1), (h2, r2), (h3, r3)], sems):
-        copy.wait()
+def add_four_kernel(own_ref, r1, r2, r3, after, out_ref):
     low = own_ref[:, :RANK]
     tail = jnp.zeros((CHUNK, COLS - RANK), F32)
     for r in (r1, r2, r3):
@@ -117,12 +138,12 @@
     return jnp.concatenate([block[:, :HD], block[:, HD:]], axis=0)
 
 
-def cached_kernel(tab, place, table, kept, got_ref, pool_ref, out_ref, done_ref):
+def cached_kernel(tab, table, kept, got_ref, pool_ref, out_ref, done_ref):
     done_ref[...] = jnp.zeros(done_ref.shape, F32)
     row = lax.broadcasted_iota(jnp.int32, (2 * NEW, HD), 0)
     lane = lax.broadcasted_iota(jnp.int32, (2 * NEW, HD), 1)
     key = lax.broadcasted_iota(jnp.int32, (2 * NEW, KEEP), 1)
-    base = place[1] * (REQ * PAGES)
+    base = lax.axis_index("req") * (REQ * PAGES)
 
     def one_peer(p, carry):
         @pl.when(tab[4 * REQ + p] > 0)
@@ -186,14 +207,15 @@
     lax.fori_loop(0, REQ, one_slot, 0, unroll=4)
 
 
-def combine_kernel(place, tab, entries, fresh_len, part_ref, stat_ref, got_ref, after, out_ref):
+def combine_kernel(tab, entries, fresh_len, part_ref, stat_ref, got_ref, after, out_ref):
+    base = lax.axis_index("req") * REQ
     row = lax.broadcasted_iota(jnp.int32, (2 * NEW, HD), 0)
     lane = lax.broadcasted_iota(jnp.int32, (2 * NEW, HD), 1)
     spot = lax.broadcasted_iota(jnp.int32, (NEW, 2 * HD), 0)
 
     def one_slot(i, carry):
         first = pl.multiple_of(i * NEW, NEW)
-        owner = entries[place[1] * REQ + i] // REQ
+        owner = entries[base + i] // REQ
         second = (tab[REQ + owner] == i).astype(jnp.int32)
         old = heads_down(
             got_ref[owner, pl.ds(pl.multiple_of(second * NEW, NEW), NEW), :]
@@ -211,7 +233,7 @@
         share = jnp.sum(jnp.where(row == lane, share, 0.0), axis=1, keepdims=True)
         o = old * share_old + part_ref[i] * share
         o = jnp.concatenate([o[:NEW], o[NEW:]], axis=1)
-        live = spot < fresh_len[place[1] * REQ + i]
+        live = spot < fresh_len[base + i]
         out_ref[pl.ds(first, NEW), :] = jnp.where(live, o, 0.0).astype(BF)
         return carry
 
@@ -219,13 +241,14 @@
 
 
 def scan_kernel(
-    place, tab, entries, fresh_len, low_ref, wdt_hbm, b_ref, a_ref, d_ref, x_hbm, g_hbm, got_hbm,
+    tab, entries, fresh_len, low_ref, wdt_hbm, b_ref, a_ref, d_ref, x_hbm, g_hbm, got_hbm,
     out_ref, state_ref, done_ref, dt_s, u_s, bc_s, y_s, a_s, h_s, wdt_ref, x_ref, g_ref, got_ref, sems,
 ):
     copies = fetch(
         [(wdt_hbm, wdt_ref), (x_hbm, x_ref), (got_hbm, got_ref), (g_hbm, g_ref)], sems
     )
     done_ref[...] = jnp.zeros(done_ref.shape, F32)
+    base = lax.axis_index("req") * REQ
     channels = x_ref.shape[1]
     halves = [slice(c * HD, (c + 1) * HD) for c in range(channels // HD)]
     step = lax.broadcasted_iota(jnp.int32, (NEW, channels), 0)
@@ -241,7 +264,7 @@
         bc_s[pl.ds(first, CHUNK), :] = whole_tail(part[:, RANK:].astype(F32))
         for j in range(CHUNK // NEW):
             here = first + j * NEW
-            live = step < fresh_len[place[1] * REQ + member * (CHUNK // NEW) + j]
+            live = step < fresh_len[base + member * (CHUNK // NEW) + j]
             masked = jnp.where(live, dt[j * NEW : (j + 1) * NEW], 0.0)
             drive = masked * x_ref[pl.ds(here, NEW), :].astype(F32)
             for c, half in enumerate(halves):
@@ -249,7 +272,7 @@
                 u_s[c, pl.ds(here, NEW), :] = drive[:, half]
     copies[2].wait()
     for i in range(REQ):
-        owner = entries[place[1] * REQ + i] // REQ
+        owner = entries[base + i] // REQ
         second = (tab[REQ + owner] == i).astype(jnp.int32)
         start = pl.multiple_of(2 * NEW + second * NS, NS)
         state = got_ref[owner, pl.ds(start, NS), :].astype(F32)
@@ -296,7 +319,7 @@
             gate = g_ref[rows, half].astype(F32)
             y = y_s[c, rows, :] + d_ref[:, half] * x_ref[rows, half].astype(F32)
             y = y * (gate * jax.nn.sigmoid(gate))
-            out_ref[rows, half] = jnp.where(step[:, half] < fresh_len[place[1] * REQ + i], y, 0.0).astype(BF)
+            out_ref[rows, half] = jnp.where(step[:, half] < fresh_len[base + i], y, 0.0).astype(BF)
 
 
 def on_device(
@@ -304,30 +327,16 @@
     kept_len, new_len, cache_index, page_table,
 ):
     rows, channels = mixer_in.shape
-    me = lax.axis_index("req")
-    at = lax.axis_index("mp")
     zs = lax.axis_size("mp") // 2
-    member = (at // zs) * 2 + (at & 1)
-    place = jnp.stack([member, me]).astype(jnp.int32)
-
-    slots = jnp.arange(REQ * REQ, dtype=jnp.int32)[None, :]
-    peers = jnp.arange(REQ, dtype=jnp.int32)[:, None]
-    owners = (cache_index // REQ)[None, :]
-
-    def ends(match):
-        first = jnp.min(jnp.where(match, slots & (REQ - 1), REQ - 1), axis=1)
-        last = jnp.max(jnp.where(match, slots & (REQ - 1), -1), axis=1)
-        return first, jnp.maximum(last, 0), (last >= 0).astype(jnp.int32)
-
-    q_first, q_last, _ = ends((owners == peers) & (slots // REQ == me))
-    s_first, s_last, active = ends((owners == me) & (slots // REQ == peers))
-    tab = jnp.concatenate([q_first, q_last, s_first, s_last, active])
-
-    packed = pl.pallas_call(
+
+    packed, tab = pl.pallas_call(
         pack_kernel,
-        out_shape=jax.ShapeDtypeStruct((REQ, SEND, channels), BF),
-        in_specs=[SMEM, HBM, HBM, HBM],
-        out_specs=VMEM,
+        out_shape=[
+            jax.ShapeDtypeStruct((REQ, SEND, channels), BF),
+            jax.ShapeDtypeStruct((TABLE,), jnp.int32),
+        ],
+        in_specs=[HBM, HBM, HBM],
+        out_specs=[VMEM, SMEM],
         scratch_shapes=[
             pltpu.SMEM(cache_index.shape, jnp.int32),
             pltpu.VMEM(queries.shape, BF),
@@ -336,18 +345,18 @@
         ],
         compiler_params=PARAMS,
         name="pack",
-    )(tab, cache_index, queries, ssm_cache)
+    )(cache_index, queries, ssm_cache)
     got = lax.all_to_all(packed, "req", 0, 0, tiled=True)
 
     chunk = jax.ShapeDtypeStruct((CHUNK, COLS), BF)
     own, *sent = pl.pallas_call(
         project_kernel,
         out_shape=[jax.ShapeDtypeStruct((CHUNK, COLS), F32), chunk, chunk, chunk],
-        in_specs=[SMEM, VMEM, VMEM, ANY],
+        in_specs=[VMEM, VMEM, ANY],
         out_specs=[VMEM] * 4,
-        compiler_params=PARAMS,
+        compiler_params=SMALL,
         name="project",
-    )(place, mixer_in, w_x, packed)
+    )(mixer_in, w_x, packed)
 
     def swap(array, d):
         pairs = []
@@ -366,29 +375,26 @@
         out_shape=[block, jax.ShapeDtypeStruct((REQ, 8, HD), F32)],
         in_specs=[VMEM] * 2,
         out_specs=[VMEM] * 2,
-        compiler_params=PARAMS,
+        compiler_params=SMALL,
         name="fresh",
     )(queries, kv_new.reshape(rows, channels))
     added = pl.pallas_call(
         add_four_kernel,
         out_shape=split,
-        in_specs=[HBM] * 4 + [ANY] * 2,
+        in_specs=[VMEM] * 4 + [ANY],
         out_specs=VMEM,
-        scratch_shapes=[pltpu.VMEM((CHUNK, COLS), F32)]
-        + [pltpu.VMEM((CHUNK, COLS), BF)] * 3
-        + [pltpu.SemaphoreType.DMA((4,))],
-        compiler_params=PARAMS,
+        compiler_params=SMALL,
         name="add_four",
-    )(own, *received, got, fresh[1])
+    )(own, *received, fresh[1])
     token = jax.ShapeDtypeStruct((8, HD), F32)
     partial, cached = pl.pallas_call(
         cached_kernel,
         out_shape=[jax.ShapeDtypeStruct((REQ, RET, channels), BF), token],
-        in_specs=[SMEM, SMEM, SMEM, SMEM, VMEM, VMEM],
+        in_specs=[SMEM, SMEM, SMEM, VMEM, VMEM],
         out_specs=[VMEM] * 2,
         compiler_params=SMALL,
         name="cached",
-    )(tab, place, page_table.T.reshape(-1), kept_len, got, kv_pool.reshape(-1, PAGE, channels))
+    )(tab, page_table.T.reshape(-1), kept_len, got, kv_pool.reshape(-1, PAGE, channels))
     parts = lax.all_to_all(added, "mp", 0, 0, tiled=True, axis_index_groups=groups)
     summed = pl.pallas_call(
         add_eight_kernel,
@@ -420,7 +426,7 @@
             jax.ShapeDtypeStruct((REQ * NS, channels), F32),
             token,
         ],
-        in_specs=[SMEM] * 4 + [VMEM, HBM] + [VMEM] * 3 + [HBM] * 3,
+        in_specs=[SMEM] * 3 + [VMEM, HBM] + [VMEM] * 3 + [HBM] * 3,
         out_specs=[VMEM] * 3,
         scratch_shapes=[
             pltpu.VMEM((channels // HD, rows, HD), F32),
@@ -438,17 +444,17 @@
         compiler_params=PARAMS,
         name="scan",
     )(
-        place, tab, cache_index, new_len, whole, w_dt, b_dt.reshape(1, -1), a_rate,
+        tab, cache_index, new_len, whole, w_dt, b_dt.reshape(1, -1), a_rate,
         d_skip.reshape(1, -1), mixer_in, gate_in, got,
     )
     attn_out = pl.pallas_call(
         combine_kernel,
         out_shape=jax.ShapeDtypeStruct((rows, channels), BF),
-        in_specs=[SMEM] * 4 + [VMEM] * 3 + [ANY],
+        in_specs=[SMEM] * 3 + [VMEM] * 3 + [ANY],
         out_specs=VMEM,
-        compiler_params=PARAMS,
+        compiler_params=SMALL,
         name="combine",
-    )(place, tab, cache_index, new_len, *fresh, back, done)
+    )(tab, cache_index, new_len, *fresh, back, done)
     return attn_out, mixer_out, state_out.reshape(REQ, NS, channels)
 
 

time: 120 us -> 118 us (0.983)
  Pallas kernels: 28.4 us -> 24.3 us
  waiting for transfers between devices: 11.1 us -> 14.6 us
  starting transfers between devices: 42 us -> 44.6 us
  local copies, waits for them, and re-layouts: 5.35 us -> 3.4 us
  other arithmetic: 1.48 us -> 0 us
    ppermute x3, waiting for transfers between devices: 1.96 us -> 5.92 us  [swap(): return lax.ppermute(array, 'mp', pairs)]
    all_to_all x1, starting transfers between devices: 9.26 us -> 11.5 us  [on_device(): back = lax.all_to_all(partial, 'req', 0, 0, tiled=True)]
    pallas_call x1, Pallas kernels: 4.13 us -> 2.27 us  [on_device(): pl.pallas_call(fresh_kernel, out_shape=[block, jax.ShapeDtypeStruct((REQ,...]
    pallas_call x1, Pallas kernels: 2.26 us -> 0.45 us  [on_device(): pl.pallas_call(project_kernel, out_shape=[jax.ShapeDtypeStruct((CHUNK, CO...]
    unnamed x28 -> x32, local copies, waits for them, and re-layouts: 4.68 us -> 3.35 us
  transfers between devices with their start and end apart: 6 -> 6, of which waited for: 3 -> 3; matrix products, arithmetic and copies ran while one was open for 1% -> 0% of each run, Pallas kernels for 17% -> 15%
where the time goes in v3:
time: 118 us; the launch traced here: 117 us
  starting transfers between devices  44.6 us (38%)
  blocking collectives  29.7 us (25%)
  Pallas kernels  24.3 us (21%)
  waiting for transfers between devices  14.6 us (12%)
  local copies, waits for them, and re-layouts  3.4 us (3%)
    all_to_all x1, blocking collectives, on_device(): lax.all_to_all(summed, 'mp', 0, 0, tiled=True, axis_index_groups=groups)  19.5 us
    all_to_all x1, starting transfers between devices, on_device(): lax.all_to_all(added, 'mp', 0, 0, tiled=True, axis_index_groups=groups)  14.3 us
    all_to_all x1, starting transfers between devices, on_device(): back = lax.all_to_all(partial, 'req', 0, 0, tiled=True)  11.5 us
    all_to_all x1, starting transfers between devices, on_device(): got = lax.all_to_all(packed, 'req', 0, 0, tiled=True)  10.4 us
    all_to_all x1, blocking collectives, on_device(): lax.all_to_all(whole, 'mp', 0, 0, tiled=True, axis_index_groups=quads)  10.2 us
    pallas_call x1, Pallas kernels, on_device(): pl.pallas_call(scan_kernel, out_shape=[jax.ShapeDtypeStruct((rows, channe...  8.42 us
    ppermute x3, starting transfers between devices, swap(): return lax.ppermute(array, 'mp', pairs)  8.37 us
    pallas_call x1, Pallas kernels, on_device(): pl.pallas_call(cached_kernel, out_shape=[jax.ShapeDtypeStruct((REQ, RET,...  5.94 us
  transfers between devices with their start and end apart: 6, of which 3 were waited for; matrix products, arithmetic and copies ran while one was open for 0% of the time, Pallas kernels for 15%

profile of v3, /device:TPU:1, one launch (start us, length us, event | category | flops | bytes accessed | tf_op | source)
XLA Modules:
  0.0 117.5 jit_solution(10793785757421291871)
XLA Ops:
  0.7 0.0 copy-start.5
  0.7 4.2 %pack.1 = (bf16[16,96,256]{2,1,0:T(8,128)(2,1)}, s32[96]{0:T(128)}) custom-call(s32[256]{0:T(256)} %entries.3, bf16[512,256]{1,0:T(8,128)(2,1)} %q_ref.1, f32[16,16,256]{2,1,0:T(8,128)} %cache_hbm.1), custom_call_target="tpu_custom_call" | custom-call | tf_op jit(solution)/shard_map/pack/pallas_call | solution.py:332
  4.9 10.4 %all-to-all-start = ((bf16[16,96,256]{2,1,0:T(8,128)(2,1)}), bf16[16,96,256]{2,1,0:T(8,128)(2,1)S(1)}, u32[]{:S(2)}, u32[]{:S(2)}) async-start(bf16[16,96,256]{2,1,0:T(8,128)(2,1)} %get-tuple-element.19.after), calls=%async_computation | async-start | bytes 1572864 | tf_op jit(solution)/shard_map/all_to_all | solution.py:349
  15.3 0.0 copy-start.14
  15.4 0.0 copy-start.12
  15.4 0.2 copy.19.w_ref
  15.6 0.5 project.1
  16.1 1.9 %collective-permute-start = (bf16[128,640]{1,0:T(8,128)(2,1)S(1)}, bf16[128,640]{1,0:T(8,128)(2,1)S(1)}, u32[]{:S(2)}, u32[]{:S(2)}) collective-permute-start(bf16[128,640]{1,0:T(8,128)(2,1)S(1)} %get-tuple-element.22), channel_id=1, source_target_pairs={{0,1},{1,0},{2,3},{3,2},{4,5},{5,4},{6,7},{7,6},{8,9},{9,8},{10,11... | collective-permute-start | bytes 491528 | tf_op jit(solution)/shard_map/ppermute | solution.py:366
  18.0 2.1 %collective-permute-start.1 = (bf16[128,640]{1,0:T(8,128)(2,1)S(1)}, bf16[128,640]{1,0:T(8,128)(2,1)S(1)}, u32[]{:S(2)}, u32[]{:S(2)}) collective-permute-start(bf16[128,640]{1,0:T(8,128)(2,1)S(1)} %get-tuple-element.23), channel_id=1, source_target_pairs={{0,16},{1,17},{2,18},{3,19},{4,20},{5,21},{6,22},{7,23},{8,24},{9,... | collective-permute-start | bytes 491528 | tf_op jit(solution)/shard_map/ppermute | solution.py:366
  20.1 4.3 %collective-permute-start.2 = (bf16[128,640]{1,0:T(8,128)(2,1)S(1)}, bf16[128,640]{1,0:T(8,128)(2,1)S(1)}, u32[]{:S(2)}, u32[]{:S(2)}) collective-permute-start(bf16[128,640]{1,0:T(8,128)(2,1)S(1)} %get-tuple-element.24), channel_id=1, source_target_pairs={{0,17},{1,16},{2,19},{3,18},{4,21},{5,20},{6,23},{7,22},{8,25},{9,... | collective-permute-start | bytes 491528 | tf_op jit(solution)/shard_map/ppermute | solution.py:366
  24.5 2.3 %fresh.1 = (f32[16,64,128]{2,1,0:T(8,128)S(1)}, f32[16,8,128]{2,1,0:T(8,128)S(1)}) custom-call(bf16[512,256]{1,0:T(8,128)(2,1)S(1)} %copy-done.4, bf16[512,256]{1,0:T(8,128)(2,1)S(1)} %bitcast.10), custom_call_target="tpu_custom_call" | custom-call | tf_op jit(solution)/shard_map/fresh/pallas_call | solution.py:373
  26.7 0.0 collective-permute-done.r1
  26.8 5.9 %collective-permute-done.1.r2 = bf16[128,640]{1,0:T(8,128)(2,1)S(1)} collective-permute-done((bf16[128,640]{1,0:T(8,128)(2,1)S(1)}, bf16[128,640]{1,0:T(8,128)(2,1)S(1)}, u32[]{:S(2)}, u32[]{:S(2)}) %collective-permute-start.1) | collective-permute-done | bytes 163872 | tf_op jit(solution)/shard_map/ppermute | solution.py:366
  32.7 0.0 collective-permute-done.2.r3
  32.7 0.8 add_four.1
  33.5 0.0 all-to-all-done.got_ref.got_hbm
  33.5 14.3 %all-to-all-start.1 = ((bf16[8,16,640]{2,1,0:T(8,128)(2,1)}), bf16[8,16,640]{2,1,0:T(8,128)(2,1)S(1)}, u32[]{:S(2)}, u32[]{:S(2)}) async-start(bf16[8,16,640]{2,1,0:T(8,128)(2,1)} %add_four.1), calls=%async_computation.1 | async-start | bytes 327680 | tf_op jit(solution)/shard_map/all_to_all | solution.py:398
  47.8 0.0 copy-start.3
  47.8 1.6 %copy-done.3 = bf16[256,16,1,256]{3,1,2,0:T(8,128)(2,1)S(1)} copy-done((bf16[256,16,1,256]{3,1,2,0:T(8,128)(2,1)S(1)}, bf16[256,16,1,256]{3,1,2,0:T(8,128)(2,1)}, u32[]{:S(2)}) %copy-start.3) | copy-done | bytes 2097176
  49.4 5.9 %cached.1 = (bf16[16,72,256]{2,1,0:T(8,128)(2,1)S(1)}, f32[8,128]{1,0:T(8,128)S(1)}) custom-call(s32[96]{0:T(128)S(1)} %copy-done.8, s32[4096]{0:T(1024)S(1)} %bitcast.11, s32[256]{0:T(256)S(1)} %copy-done.12, bf16[16,96,256]{2,1,0:T(8,128)(2,1)S(1)} %all-to-all-done.got_ref.got_hbm, bf16[256,16,256]{2,1,0:T(8,128)(2,1)S(1)} %bitcast.9), custom_call_target="tpu_custom_call" | custom-call | tf_op jit(solution)/shard_map/cached/pallas_call | solution.py:390
  55.4 0.8 copy-done.2
  56.2 5.4 %all-to-all-done.1.parts = bf16[8,16,640]{2,1,0:T(8,128)(2,1)S(1)} async-done(((bf16[8,16,640]{2,1,0:T(8,128)(2,1)}), bf16[8,16,640]{2,1,0:T(8,128)(2,1)S(1)}, u32[]{:S(2)}, u32[]{:S(2)}) %all-to-all-start.1) | async-done | bytes 163872 | tf_op jit(solution)/shard_map/all_to_all | solution.py:398
  61.6 0.2 add_eight.1
  61.8 19.5 %all_to_all.25 = bf16[8,16,640]{2,1,0:T(8,128)(2,1)S(1)} all-to-all(bf16[8,16,640]{2,1,0:T(8,128)(2,1)S(1)} %add_eight.1), channel_id=1, replica_groups={{0,2,4,6,8,10,12,14},{1,3,5,7,9,11,13,15},{16,18,20,22,24,26,28,30},{17..., dimensions={0} | all-to-all | bytes 327680 | tf_op jit(solution)/shard_map/all_to_all | solution.py:407
  81.3 0.1 broadcast_in_dim.8
  81.4 10.2 %all_to_all.26.after.low_ref = bf16[4,128,640]{2,1,0:T(8,128)(2,1)} all-to-all(bf16[4,128,640]{2,1,0:T(8,128)(2,1)S(1)} %broadcast_in_dim.8), channel_id=1, replica_groups={{0,1,16,17},{2,3,18,19},{4,5,20,21},{6,7,22,23},{8,9,24,25},{10,11,26,2..., dimensions={0} | all-to-all | bytes 1310720 | tf_op jit(solution)/shard_map/all_to_all | solution.py:409
  91.6 11.5 %all-to-all-start.4 = ((bf16[16,72,256]{2,1,0:T(8,128)(2,1)}), bf16[16,72,256]{2,1,0:T(8,128)(2,1)S(1)}, u32[]{:S(2)}, u32[]{:S(2)}) async-start(bf16[16,72,256]{2,1,0:T(8,128)(2,1)} %gate.1), calls=%async_computation.4 | async-start | bytes 1179648 | tf_op jit(solution)/shard_map/all_to_all | solution.py:420
  103.1 8.4 %scan.1 = (bf16[512,256]{1,0:T(8,128)(2,1)}, f32[256,256]{1,0:T(8,128)}, f32[8,128]{1,0:T(8,128)}) custom-call(s32[96]{0:T(128)} %get-tuple-element.16.tab, s32[256]{0:T(256)} %entries.3, s32[256]{0:T(256)} %fresh_len.3, bf16[4,128,640]{2,1,0:T(8,128)(2,1)} %all_to_all.26.after.low_ref, bf16[512,256]{1,0:T(8,128)(2,1)} %wdt_hbm.1, f32[1,256]{1,0:T(1,128)} %bitcast.14, ...), custom_call_target="tpu_custom_call" | custom-call | tf_op jit(solution)/shard_map/scan/pallas_call | solution.py:422
  111.6 3.2 %all-to-all-done.4.got_ref = bf16[16,72,256]{2,1,0:T(8,128)(2,1)S(1)} async-done(((bf16[16,72,256]{2,1,0:T(8,128)(2,1)}), bf16[16,72,256]{2,1,0:T(8,128)(2,1)S(1)}, u32[]{:S(2)}, u32[]{:S(2)}) %all-to-all-start.4) | async-done | bytes 589856 | tf_op jit(solution)/shard_map/all_to_all | solution.py:420
  114.8 0.0 copy-start.11
  114.8 0.7 copy-done.11
  115.5 2.0 %combine.1 = bf16[512,256]{1,0:T(8,128)(2,1)} custom-call(s32[96]{0:T(128)S(1)} %copy-done.9, s32[256]{0:T(256)S(1)} %copy-done.7, s32[256]{0:T(256)S(1)} %copy-done.10, f32[16,64,128]{2,1,0:T(8,128)S(1)} %get-tuple-element.17.part_ref, f32[16,8,128]{2,1,0:T(8,128)S(1)} %get-tuple-element.18.after.stat_ref, bf16[16,72,256]{2,1,0:T(8,128)(2,1)S(1)} %all-to-all-done.4.got_ref, ...), custom_call_target="tpu_custom_call" | custom-call | tf_op jit(solution)/shard_map/combine/pallas_call | solution.py:450
  (24 shorter events, 0.1 us)
Async XLA Ops:
  0.6 23.8 %copy-start.4 = (bf16[512,256]{1,0:T(8,128)(2,1)S(1)}, bf16[512,256]{1,0:T(8,128)(2,1)}, u32[]{:S(2)}) copy-start(bf16[512,256]{1,0:T(8,128)(2,1)} %q_ref.1) | copy-start | bytes 786436
  0.6 14.7 %copy-start.13 = (bf16[256,544]{0,1:T(8,128)(2,1)S(1)}, bf16[256,544]{0,1:T(8,128)(2,1)}, u32[]{:S(2)}) copy-start(bf16[256,544]{0,1:T(8,128)(2,1)} %param.21) | copy-start | bytes 835588
  0.7 14.9 %copy-start.5 = (bf16[512,256]{1,0:T(8,128)(2,1)S(1)}, bf16[512,256]{1,0:T(8,128)(2,1)}, u32[]{:S(2)}) copy-start(bf16[512,256]{1,0:T(8,128)(2,1)} %x_hbm.1) | copy-start | bytes 786436
  0.7 23.8 %copy-start.6 = (bf16[512,1,256]{2,0,1:T(8,128)(2,1)S(1)}, bf16[512,1,256]{2,0,1:T(8,128)(2,1)}, u32[]{:S(2)}) copy-start(bf16[512,1,256]{2,0,1:T(8,128)(2,1)} %param.16) | copy-start | bytes 786436
  4.9 10.7 %copy-start.1 = (bf16[16,96,256]{2,1,0:T(8,128)(2,1)S(1)}, bf16[16,96,256]{2,1,0:T(8,128)(2,1)}, u32[]{:S(2)}) copy-start(bf16[16,96,256]{2,1,0:T(8,128)(2,1)} %get-tuple-element.19.after) | copy-start | bytes 2359300
  4.9 28.6 %all-to-all-start = ((bf16[16,96,256]{2,1,0:T(8,128)(2,1)}), bf16[16,96,256]{2,1,0:T(8,128)(2,1)S(1)}, u32[]{:S(2)}, u32[]{:S(2)}) async-start(bf16[16,96,256]{2,1,0:T(8,128)(2,1)} %get-tuple-element.19.after), calls=%async_computation | async-start | bytes 1572864 | tf_op jit(solution)/shard_map/all_to_all | solution.py:349
  15.3 32.5 %copy-start.14 = (s32[256,16]{0,1:T(8,128)S(1)}, s32[256,16]{0,1:T(8,128)}, u32[]{:S(2)}) copy-start(s32[256,16]{0,1:T(8,128)} %param.29) | copy-start | bytes 49156
  15.3 32.5 %copy-start.8 = (s32[96]{0:T(128)S(1)}, s32[96]{0:T(128)}, u32[]{:S(2)}) copy-start(s32[96]{0:T(128)} %get-tuple-element.16.tab) | copy-start | bytes 1156
  15.4 32.5 %copy-start.12 = (s32[256]{0:T(256)S(1)}, s32[256]{0:T(256)}, u32[]{:S(2)}) copy-start(s32[256]{0:T(256)} %kept.1) | copy-start | bytes 3076
  16.1 10.7 %collective-permute-start = (bf16[128,640]{1,0:T(8,128)(2,1)S(1)}, bf16[128,640]{1,0:T(8,128)(2,1)S(1)}, u32[]{:S(2)}, u32[]{:S(2)}) collective-permute-start(bf16[128,640]{1,0:T(8,128)(2,1)S(1)} %get-tuple-element.22), channel_id=1, source_target_pairs={{0,1},{1,0},{2,3},{3,2},{4,5},{5,4},{6,7},{7,6},{8,9},{9,8},{10,11... | collective-permute-start | bytes 491528 | tf_op jit(solution)/shard_map/ppermute | solution.py:366
  18.0 14.7 %collective-permute-start.1 = (bf16[128,640]{1,0:T(8,128)(2,1)S(1)}, bf16[128,640]{1,0:T(8,128)(2,1)S(1)}, u32[]{:S(2)}, u32[]{:S(2)}) collective-permute-start(bf16[128,640]{1,0:T(8,128)(2,1)S(1)} %get-tuple-element.23), channel_id=1, source_target_pairs={{0,16},{1,17},{2,18},{3,19},{4,20},{5,21},{6,22},{7,23},{8,24},{9,... | collective-permute-start | bytes 491528 | tf_op jit(solution)/shard_map/ppermute | solution.py:366
  20.1 12.6 %collective-permute-start.2 = (bf16[128,640]{1,0:T(8,128)(2,1)S(1)}, bf16[128,640]{1,0:T(8,128)(2,1)S(1)}, u32[]{:S(2)}, u32[]{:S(2)}) collective-permute-start(bf16[128,640]{1,0:T(8,128)(2,1)S(1)} %get-tuple-element.24), channel_id=1, source_target_pairs={{0,17},{1,16},{2,19},{3,18},{4,21},{5,20},{6,23},{7,22},{8,25},{9,... | collective-permute-start | bytes 491528 | tf_op jit(solution)/shard_map/ppermute | solution.py:366
  33.5 47.9 %copy-start = (bf16[16,96,256]{2,1,0:T(8,128)(2,1)}, bf16[16,96,256]{2,1,0:T(8,128)(2,1)S(1)}, u32[]{:S(2)}) copy-start(bf16[16,96,256]{2,1,0:T(8,128)(2,1)S(1)} %all-to-all-done.got_ref.got_hbm) | copy-start | bytes 2359300
  33.5 28.1 %all-to-all-start.1 = ((bf16[8,16,640]{2,1,0:T(8,128)(2,1)}), bf16[8,16,640]{2,1,0:T(8,128)(2,1)S(1)}, u32[]{:S(2)}, u32[]{:S(2)}) async-start(bf16[8,16,640]{2,1,0:T(8,128)(2,1)} %add_four.1), calls=%async_computation.1 | async-start | bytes 327680 | tf_op jit(solution)/shard_map/all_to_all | solution.py:398
  47.8 1.6 %copy-start.3 = (bf16[256,16,1,256]{3,1,2,0:T(8,128)(2,1)S(1)}, bf16[256,16,1,256]{3,1,2,0:T(8,128)(2,1)}, u32[]{:S(2)}) copy-start(bf16[256,16,1,256]{3,1,2,0:T(8,128)(2,1)} %param.17) | copy-start | bytes 6291460
  55.4 0.8 copy-start.2
  91.6 23.2 %copy-start.7 = (s32[256]{0:T(256)S(1)}, s32[256]{0:T(256)}, u32[]{:S(2)}) copy-start(s32[256]{0:T(256)} %entries.3) | copy-start | bytes 3076
  91.6 23.2 %copy-start.9 = (s32[96]{0:T(128)S(1)}, s32[96]{0:T(128)}, u32[]{:S(2)}) copy-start(s32[96]{0:T(128)} %get-tuple-element.16.tab) | copy-start | bytes 1156
  91.6 23.2 %copy-start.10 = (s32[256]{0:T(256)S(1)}, s32[256]{0:T(256)}, u32[]{:S(2)}) copy-start(s32[256]{0:T(256)} %fresh_len.3) | copy-start | bytes 3076
  91.6 23.2 %all-to-all-start.4 = ((bf16[16,72,256]{2,1,0:T(8,128)(2,1)}), bf16[16,72,256]{2,1,0:T(8,128)(2,1)S(1)}, u32[]{:S(2)}, u32[]{:S(2)}) async-start(bf16[16,72,256]{2,1,0:T(8,128)(2,1)} %gate.1), calls=%async_computation.4 | async-start | bytes 1179648 | tf_op jit(solution)/shard_map/all_to_all | solution.py:420
  114.8 0.7 copy-start.11

commit v4 on v3

--- a/solution.py
+++ b/solution.py
@@ -27,6 +27,9 @@
 RET = 72
 SEND = 96
 TABLE = 6 * REQ
+SHIFT = REQ.bit_length() - 1
+TILES = RANK // HD
+BLOCK = TILES * SUB + SUB // 2
 
 VMEM = pl.BlockSpec(memory_space=pltpu.VMEM)
 ANY = pl.BlockSpec(memory_space=pl.ANY)
@@ -45,6 +48,18 @@
 
 def whole_tail(tail):
     return tail + pltpu.roll(tail, tail.shape[1] - BC, 1)
+
+
+def store_block(ref, k, low, rest):
+    for t in range(TILES):
+        ref[k, t * SUB : (t + 1) * SUB, :] = low[:, t * HD : (t + 1) * HD].astype(BF)
+    tail = tail_of(rest)
+    both = tail[: SUB // 2] + pltpu.roll(tail[SUB // 2 :], HD // 2, 1)
+    ref[k, TILES * SUB : BLOCK, :] = both.astype(BF)
+
+
+def rest_of(both):
+    return whole_tail(jnp.concatenate([both, pltpu.roll(both, HD // 2, 1)], axis=0))
 
 
 def fetch(pairs, sems):
@@ -61,21 +76,23 @@
         tab[i] = 0
     copies[0].wait()
     for i in range(REQ):
-        owner = entries[me * REQ + i] // REQ
+        owner = entries[me * REQ + i] >> SHIFT
         count = tab[5 * REQ + owner]
         tab[jnp.minimum(count, 1) * REQ + owner] = i
         tab[5 * REQ + owner] = count + 1
 
     def one_peer(p, carry):
-        count = jnp.int32(0)
+        first, last = jnp.int32(REQ - 1), jnp.int32(-1)
         for i in range(REQ):
-            match = entries[p * REQ + i] // REQ == me
-            tab[jnp.where(match, (2 + jnp.minimum(count, 1)) * REQ, 5 * REQ) + p] = i
-            count = count + match.astype(jnp.int32)
-        tab[4 * REQ + p] = count
+            match = entries[p * REQ + i] >> SHIFT == me
+            first = jnp.minimum(first, jnp.where(match, i, REQ - 1))
+            last = jnp.where(match, i, last)
+        tab[2 * REQ + p] = first
+        tab[3 * REQ + p] = jnp.maximum(last, 0)
+        tab[4 * REQ + p] = (last >= 0).astype(jnp.int32)
         return carry
 
-    lax.fori_loop(0, REQ, one_peer, 0)
+    lax.fori_loop(0, REQ, one_peer, 0, unroll=2)
     copies[1].wait()
     copies[2].wait()
     for p in range(REQ):
@@ -101,33 +118,28 @@
             own_ref[:, :RANK] = low
             own_ref[:, RANK:] = rest
         else:
-            sent[d - 1][:, :RANK] = low.astype(BF)
-            sent[d - 1][:, RANK:] = tail_of(rest).astype(BF)
+            for k in range(CHUNK // SUB):
+                some = slice(k * SUB, (k + 1) * SUB)
+                store_block(sent[d - 1], k, low[some], rest[some])
 
 
 def add_four_kernel(own_ref, r1, r2, r3, after, out_ref):
-    low = own_ref[:, :RANK]
-    tail = jnp.zeros((CHUNK, COLS - RANK), F32)
-    for r in (r1, r2, r3):
-        low = low + r[:, :RANK].astype(F32)
-        tail = tail + r[:, RANK:].astype(F32)
-    rest = own_ref[:, RANK:] + whole_tail(tail)
-    low = low.astype(BF)
-    tail = tail_of(rest).astype(BF)
     for k in range(CHUNK // SUB):
-        out_ref[k, :, :RANK] = low[k * SUB : (k + 1) * SUB]
-        out_ref[k, :, RANK:] = tail[k * SUB : (k + 1) * SUB]
+        some = slice(k * SUB, (k + 1) * SUB)
+        block = r1[k].astype(F32) + r2[k].astype(F32) + r3[k].astype(F32)
+        tiles = [block[t * SUB : (t + 1) * SUB] for t in range(TILES)]
+        low = own_ref[some, :RANK] + jnp.concatenate(tiles, axis=1)
+        store_block(out_ref, k, low, own_ref[some, RANK:] + rest_of(block[TILES * SUB :]))
 
 
 def add_eight_kernel(parts, after, out_ref):
-    total = parts[0].astype(F32)
+    block = parts[0].astype(F32)
     for k in range(1, CHUNK // SUB):
-        total = total + parts[k].astype(F32)
-    low = total[:, :RANK].astype(BF)
-    tail = tail_of(whole_tail(total[:, RANK:])).astype(BF)
+        block = block + parts[k].astype(F32)
+    low = jnp.concatenate([block[t * SUB : (t + 1) * SUB] for t in range(TILES)], axis=1)
+    rest = rest_of(block[TILES * SUB :])
     for k in range(CHUNK // SUB):
-        out_ref[k, :, :RANK] = low
-        out_ref[k, :, RANK:] = tail
+        store_block(out_ref, k, low, rest)
 
 
 def gate_kernel(partial, after, out):
@@ -215,7 +227,7 @@
 
     def one_slot(i, carry):
         first = pl.multiple_of(i * NEW, NEW)
-        owner = entries[base + i] // REQ
+        owner = entries[base + i] >> SHIFT
         second = (tab[REQ + owner] == i).astype(jnp.int32)
         old = heads_down(
             got_ref[owner, pl.ds(pl.multiple_of(second * NEW, NEW), NEW), :]
@@ -257,11 +269,18 @@
     copies[0].wait()
     copies[1].wait()
     for member in range(4):
-        part = low_ref[member]
         first = member * CHUNK
-        pre = jnp.dot(part[:, :RANK], wdt_ref[...], preferred_element_type=F32) + b_ref[...]
+        low = []
+        for k in range(CHUNK // SUB):
+            at = member * (CHUNK // SUB) + k
+            tiles = [low_ref[at, t * SUB : (t + 1) * SUB, :] for t in range(TILES)]
+            low.append(jnp.concatenate(tiles, axis=1))
+            bc_s[first + k * SUB : first + (k + 1) * SUB, :] = rest_of(
+                low_ref[at, TILES * SUB : BLOCK, :].astype(F32)
+            )
+        low = jnp.concatenate(low, axis=0)
+        pre = jnp.dot(low, wdt_ref[...], preferred_element_type=F32) + b_ref[...]
         dt = jnp.maximum(pre, 0.0) + jnp.log1p(jnp.exp(-jnp.abs(pre)))
-        bc_s[pl.ds(first, CHUNK), :] = whole_tail(part[:, RANK:].astype(F32))
         for j in range(CHUNK // NEW):
             here = first + j * NEW
             live = step < fresh_len[base + member * (CHUNK // NEW) + j]
@@ -272,7 +291,7 @@
                 u_s[c, pl.ds(here, NEW), :] = drive[:, half]
     copies[2].wait()
     for i in range(REQ):
-        owner = entries[base + i] // REQ
+        owner = entries[base + i] >> SHIFT
         second = (tab[REQ + owner] == i).astype(jnp.int32)
         start = pl.multiple_of(2 * NEW + second * NS, NS)
         state = got_ref[owner, pl.ds(start, NS), :].astype(F32)
@@ -348,7 +367,7 @@
     )(cache_index, queries, ssm_cache)
     got = lax.all_to_all(packed, "req", 0, 0, tiled=True)
 
-    chunk = jax.ShapeDtypeStruct((CHUNK, COLS), BF)
+    chunk = jax.ShapeDtypeStruct((CHUNK // SUB, BLOCK, HD), BF)
     own, *sent = pl.pallas_call(
         project_kernel,
         out_shape=[jax.ShapeDtypeStruct((CHUNK, COLS), F32), chunk, chunk, chunk],
@@ -368,7 +387,6 @@
     quads = [[y * zs + 2 * k + b for y in range(2) for b in range(2)] for k in range(zs // 2)]
     groups = [[y * zs + 2 * k + b for k in range(zs // 2)] for y in range(2) for b in range(2)]
     received = [swap(sent[d - 1], d) for d in (1, 2, 3)]
-    split = jax.ShapeDtypeStruct((CHUNK // SUB, SUB, COLS), BF)
     block = jax.ShapeDtypeStruct((REQ, 2 * NEW, HD), F32)
     fresh = pl.pallas_call(
         fresh_kernel,
@@ -380,7 +398,7 @@
     )(queries, kv_new.reshape(rows, channels))
     added = pl.pallas_call(
         add_four_kernel,
-        out_shape=split,
+        out_shape=chunk,
         in_specs=[VMEM] * 4 + [ANY],
         out_specs=VMEM,
         compiler_params=SMALL,
@@ -398,14 +416,14 @@
     parts = lax.all_to_all(added, "mp", 0, 0, tiled=True, axis_index_groups=groups)
     summed = pl.pallas_call(
         add_eight_kernel,
-        out_shape=split,
+        out_shape=chunk,
         in_specs=[VMEM, ANY],
         out_specs=VMEM,
         compiler_params=SMALL,
         name="add_eight",
     )(parts, cached)
     whole = lax.all_to_all(summed, "mp", 0, 0, tiled=True, axis_index_groups=groups)
-    whole = jnp.broadcast_to(whole.reshape(1, CHUNK, COLS), (4, CHUNK, COLS))
+    whole = jnp.concatenate([whole] * 4, axis=0)
     whole = lax.all_to_all(whole, "mp", 0, 0, tiled=True, axis_index_groups=quads)
 
     partial = pl.pallas_call(

time: 118 us -> 115 us (0.975)
  Pallas kernels: 24.3 us -> 22.9 us
    pallas_call x1, Pallas kernels: 4.22 us -> 2.63 us  [on_device(): pl.pallas_call(pack_kernel, out_shape=[jax.ShapeDtypeStruct((REQ, SEND, c...]
  transfers between devices with their start and end apart: 6 -> 6, of which waited for: 3 -> 3; matrix products, arithmetic and copies ran while one was open for 0% -> 0% of each run, Pallas kernels for 15% -> 16%
where the time goes in v4:
time: 115 us; the launch traced here: 114 us
  starting transfers between devices  44.6 us (39%)
  blocking collectives  29 us (25%)
  Pallas kernels  22.9 us (20%)
  waiting for transfers between devices  13.5 us (12%)
  local copies, waits for them, and re-layouts  3.37 us (3%)
    all_to_all x1, blocking collectives, on_device(): lax.all_to_all(summed, 'mp', 0, 0, tiled=True, axis_index_groups=groups)  19.4 us
    all_to_all x1, starting transfers between devices, on_device(): lax.all_to_all(added, 'mp', 0, 0, tiled=True, axis_index_groups=groups)  14.3 us
    all_to_all x1, starting transfers between devices, on_device(): back = lax.all_to_all(partial, 'req', 0, 0, tiled=True)  11.5 us
    all_to_all x1, starting transfers between devices, on_device(): got = lax.all_to_all(packed, 'req', 0, 0, tiled=True)  10.4 us
    all_to_all x1, blocking collectives, on_device(): lax.all_to_all(whole, 'mp', 0, 0, tiled=True, axis_index_groups=quads)  9.59 us
    ppermute x3, starting transfers between devices, swap(): return lax.ppermute(array, 'mp', pairs)  8.37 us
    pallas_call x1, Pallas kernels, on_device(): pl.pallas_call(scan_kernel, out_shape=[jax.ShapeDtypeStruct((rows, channe...  8.35 us
    pallas_call x1, Pallas kernels, on_device(): pl.pallas_call(cached_kernel, out_shape=[jax.ShapeDtypeStruct((REQ, RET,...  5.94 us
  transfers between devices with their start and end apart: 6, of which 3 were waited for; matrix products, arithmetic and copies ran while one was open for 0% of the time, Pallas kernels for 16%

profile of v4, /device:TPU:1, one launch (start us, length us, event | category | flops | bytes accessed | tf_op | source)
XLA Modules:
  0.0 114.4 jit_solution(16845105691969855410)
XLA Ops:
  0.7 0.0 copy-start.5
  0.7 2.6 %pack.1 = (bf16[16,96,256]{2,1,0:T(8,128)(2,1)}, s32[96]{0:T(128)}) custom-call(s32[256]{0:T(256)} %entries.3, bf16[512,256]{1,0:T(8,128)(2,1)} %q_ref.1, f32[16,16,256]{2,1,0:T(8,128)} %cache_hbm.1), custom_call_target="tpu_custom_call" | custom-call | tf_op jit(solution)/shard_map/pack/pallas_call | solution.py:351
  3.3 10.4 %all-to-all-start = ((bf16[16,96,256]{2,1,0:T(8,128)(2,1)}), bf16[16,96,256]{2,1,0:T(8,128)(2,1)S(1)}, u32[]{:S(2)}, u32[]{:S(2)}) async-start(bf16[16,96,256]{2,1,0:T(8,128)(2,1)} %get-tuple-element.19.after), calls=%async_computation | async-start | bytes 1572864 | tf_op jit(solution)/shard_map/all_to_all | solution.py:368
  13.8 0.0 copy-start.14
  13.8 0.0 copy-start.12
  13.8 0.2 copy.19.w_ref
  14.0 0.5 project.1
  14.5 1.9 %collective-permute-start = (bf16[8,72,128]{2,1,0:T(8,128)(2,1)S(1)}, bf16[8,72,128]{2,1,0:T(8,128)(2,1)S(1)}, u32[]{:S(2)}, u32[]{:S(2)}) collective-permute-start(bf16[8,72,128]{2,1,0:T(8,128)(2,1)S(1)} %get-tuple-element.22), channel_id=1, source_target_pairs={{0,1},{1,0},{2,3},{3,2},{4,5},{5,4},{6,7},{7,6},{8,9},{9,8},{10,11... | collective-permute-start | bytes 442376 | tf_op jit(solution)/shard_map/ppermute | solution.py:385
  16.5 2.1 %collective-permute-start.1 = (bf16[8,72,128]{2,1,0:T(8,128)(2,1)S(1)}, bf16[8,72,128]{2,1,0:T(8,128)(2,1)S(1)}, u32[]{:S(2)}, u32[]{:S(2)}) collective-permute-start(bf16[8,72,128]{2,1,0:T(8,128)(2,1)S(1)} %get-tuple-element.23), channel_id=1, source_target_pairs={{0,16},{1,17},{2,18},{3,19},{4,20},{5,21},{6,22},{7,23},{8,24},{9,... | collective-permute-start | bytes 442376 | tf_op jit(solution)/shard_map/ppermute | solution.py:385
  18.6 4.3 %collective-permute-start.2 = (bf16[8,72,128]{2,1,0:T(8,128)(2,1)S(1)}, bf16[8,72,128]{2,1,0:T(8,128)(2,1)S(1)}, u32[]{:S(2)}, u32[]{:S(2)}) collective-permute-start(bf16[8,72,128]{2,1,0:T(8,128)(2,1)S(1)} %get-tuple-element.24), channel_id=1, source_target_pairs={{0,17},{1,16},{2,19},{3,18},{4,21},{5,20},{6,23},{7,22},{8,25},{9,... | collective-permute-start | bytes 442376 | tf_op jit(solution)/shard_map/ppermute | solution.py:385
  22.9 2.3 %fresh.1 = (f32[16,64,128]{2,1,0:T(8,128)S(1)}, f32[16,8,128]{2,1,0:T(8,128)S(1)}) custom-call(bf16[512,256]{1,0:T(8,128)(2,1)S(1)} %copy-done.4, bf16[512,256]{1,0:T(8,128)(2,1)S(1)} %bitcast.9), custom_call_target="tpu_custom_call" | custom-call | tf_op jit(solution)/shard_map/fresh/pallas_call | solution.py:391
  25.2 0.0 collective-permute-done.r1
  25.2 5.1 %collective-permute-done.1.r2 = bf16[8,72,128]{2,1,0:T(8,128)(2,1)S(1)} collective-permute-done((bf16[8,72,128]{2,1,0:T(8,128)(2,1)S(1)}, bf16[8,72,128]{2,1,0:T(8,128)(2,1)S(1)}, u32[]{:S(2)}, u32[]{:S(2)}) %collective-permute-start.1) | collective-permute-done | bytes 147488 | tf_op jit(solution)/shard_map/ppermute | solution.py:385
  30.4 0.0 collective-permute-done.2.r3
  30.4 1.0 add_four.1
  31.3 0.0 all-to-all-done.got_ref.got_hbm
  31.4 14.3 %all-to-all-start.1 = ((bf16[8,72,128]{2,1,0:T(8,128)(2,1)}), bf16[8,72,128]{2,1,0:T(8,128)(2,1)S(1)}, u32[]{:S(2)}, u32[]{:S(2)}) async-start(bf16[8,72,128]{2,1,0:T(8,128)(2,1)} %add_four.1), calls=%async_computation.1 | async-start | bytes 294912 | tf_op jit(solution)/shard_map/all_to_all | solution.py:416
  45.7 0.0 copy-start.3
  45.7 1.6 %copy-done.3 = bf16[256,16,1,256]{3,1,2,0:T(8,128)(2,1)S(1)} copy-done((bf16[256,16,1,256]{3,1,2,0:T(8,128)(2,1)S(1)}, bf16[256,16,1,256]{3,1,2,0:T(8,128)(2,1)}, u32[]{:S(2)}) %copy-start.3) | copy-done | bytes 2097176
  47.3 5.9 %cached.1 = (bf16[16,72,256]{2,1,0:T(8,128)(2,1)S(1)}, f32[8,128]{1,0:T(8,128)S(1)}) custom-call(s32[96]{0:T(128)S(1)} %copy-done.8, s32[4096]{0:T(1024)S(1)} %bitcast.10, s32[256]{0:T(256)S(1)} %copy-done.12, bf16[16,96,256]{2,1,0:T(8,128)(2,1)S(1)} %all-to-all-done.got_ref.got_hbm, bf16[256,16,256]{2,1,0:T(8,128)(2,1)S(1)} %bitcast.8), custom_call_target="tpu_custom_call" | custom-call | tf_op jit(solution)/shard_map/cached/pallas_call | solution.py:408
  53.3 0.8 copy-done.2
  54.1 5.1 %all-to-all-done.1.parts = bf16[8,72,128]{2,1,0:T(8,128)(2,1)S(1)} async-done(((bf16[8,72,128]{2,1,0:T(8,128)(2,1)}), bf16[8,72,128]{2,1,0:T(8,128)(2,1)S(1)}, u32[]{:S(2)}, u32[]{:S(2)}) %all-to-all-start.1) | async-done | bytes 147488 | tf_op jit(solution)/shard_map/all_to_all | solution.py:416
  59.2 0.3 add_eight.1
  59.5 19.4 %all_to_all.25 = bf16[8,72,128]{2,1,0:T(8,128)(2,1)S(1)} all-to-all(bf16[8,72,128]{2,1,0:T(8,128)(2,1)S(1)} %add_eight.1), channel_id=1, replica_groups={{0,2,4,6,8,10,12,14},{1,3,5,7,9,11,13,15},{16,18,20,22,24,26,28,30},{17..., dimensions={0} | all-to-all | bytes 294912 | tf_op jit(solution)/shard_map/all_to_all | solution.py:425
  78.9 0.1 pad_maximum_fusion
  79.0 9.6 %all_to_all.26.after.low_ref = bf16[32,72,128]{2,1,0:T(8,128)(2,1)} all-to-all(bf16[32,72,128]{2,1,0:T(8,128)(2,1)S(1)} %pad_maximum_fusion), channel_id=1, replica_groups={{0,1,16,17},{2,3,18,19},{4,5,20,21},{6,7,22,23},{8,9,24,25},{10,11,26,2..., dimensions={0} | all-to-all | bytes 1179648 | tf_op jit(solution)/shard_map/all_to_all | solution.py:427
  88.6 11.5 %all-to-all-start.4 = ((bf16[16,72,256]{2,1,0:T(8,128)(2,1)}), bf16[16,72,256]{2,1,0:T(8,128)(2,1)S(1)}, u32[]{:S(2)}, u32[]{:S(2)}) async-start(bf16[16,72,256]{2,1,0:T(8,128)(2,1)} %gate.1), calls=%async_computation.4 | async-start | bytes 1179648 | tf_op jit(solution)/shard_map/all_to_all | solution.py:438
  100.0 8.3 %scan.1 = (bf16[512,256]{1,0:T(8,128)(2,1)}, f32[256,256]{1,0:T(8,128)}, f32[8,128]{1,0:T(8,128)}) custom-call(s32[96]{0:T(128)} %get-tuple-element.16.tab, s32[256]{0:T(256)} %entries.3, s32[256]{0:T(256)} %fresh_len.3, bf16[32,72,128]{2,1,0:T(8,128)(2,1)} %all_to_all.26.after.low_ref, bf16[512,256]{1,0:T(8,128)(2,1)} %wdt_hbm.1, f32[1,256]{1,0:T(1,128)} %bitcast.12, ...), custom_call_target="tpu_custom_call" | custom-call | tf_op jit(solution)/shard_map/scan/pallas_call | solution.py:440
  108.4 3.3 %all-to-all-done.4.got_ref = bf16[16,72,256]{2,1,0:T(8,128)(2,1)S(1)} async-done(((bf16[16,72,256]{2,1,0:T(8,128)(2,1)}), bf16[16,72,256]{2,1,0:T(8,128)(2,1)S(1)}, u32[]{:S(2)}, u32[]{:S(2)}) %all-to-all-start.4) | async-done | bytes 589856 | tf_op jit(solution)/shard_map/all_to_all | solution.py:438
  111.7 0.0 copy-start.11
  111.7 0.7 copy-done.11
  112.4 2.0 %combine.1 = bf16[512,256]{1,0:T(8,128)(2,1)} custom-call(s32[96]{0:T(128)S(1)} %copy-done.9, s32[256]{0:T(256)S(1)} %copy-done.7, s32[256]{0:T(256)S(1)} %copy-done.10, f32[16,64,128]{2,1,0:T(8,128)S(1)} %get-tuple-element.17.part_ref, f32[16,8,128]{2,1,0:T(8,128)S(1)} %get-tuple-element.18.after.stat_ref, bf16[16,72,256]{2,1,0:T(8,128)(2,1)S(1)} %all-to-all-done.4.got_ref, ...), custom_call_target="tpu_custom_call" | custom-call | tf_op jit(solution)/shard_map/combine/pallas_call | solution.py:468
  (24 shorter events, 0.1 us)
Async XLA Ops:
  0.6 22.3 %copy-start.4 = (bf16[512,256]{1,0:T(8,128)(2,1)S(1)}, bf16[512,256]{1,0:T(8,128)(2,1)}, u32[]{:S(2)}) copy-start(bf16[512,256]{1,0:T(8,128)(2,1)} %q_ref.1) | copy-start | bytes 786436
  0.6 13.1 %copy-start.13 = (bf16[256,544]{0,1:T(8,128)(2,1)S(1)}, bf16[256,544]{0,1:T(8,128)(2,1)}, u32[]{:S(2)}) copy-start(bf16[256,544]{0,1:T(8,128)(2,1)} %param.21) | copy-start | bytes 835588
  0.7 13.3 %copy-start.5 = (bf16[512,256]{1,0:T(8,128)(2,1)S(1)}, bf16[512,256]{1,0:T(8,128)(2,1)}, u32[]{:S(2)}) copy-start(bf16[512,256]{1,0:T(8,128)(2,1)} %x_hbm.1) | copy-start | bytes 786436
  0.7 22.3 %copy-start.6 = (bf16[512,1,256]{2,0,1:T(8,128)(2,1)S(1)}, bf16[512,1,256]{2,0,1:T(8,128)(2,1)}, u32[]{:S(2)}) copy-start(bf16[512,1,256]{2,0,1:T(8,128)(2,1)} %param.16) | copy-start | bytes 786436
  3.3 10.7 %copy-start.1 = (bf16[16,96,256]{2,1,0:T(8,128)(2,1)S(1)}, bf16[16,96,256]{2,1,0:T(8,128)(2,1)}, u32[]{:S(2)}) copy-start(bf16[16,96,256]{2,1,0:T(8,128)(2,1)} %get-tuple-element.19.after) | copy-start | bytes 2359300
  3.3 28.0 %all-to-all-start = ((bf16[16,96,256]{2,1,0:T(8,128)(2,1)}), bf16[16,96,256]{2,1,0:T(8,128)(2,1)S(1)}, u32[]{:S(2)}, u32[]{:S(2)}) async-start(bf16[16,96,256]{2,1,0:T(8,128)(2,1)} %get-tuple-element.19.after), calls=%async_computation | async-start | bytes 1572864 | tf_op jit(solution)/shard_map/all_to_all | solution.py:368
  13.8 31.9 %copy-start.14 = (s32[256,16]{0,1:T(8,128)S(1)}, s32[256,16]{0,1:T(8,128)}, u32[]{:S(2)}) copy-start(s32[256,16]{0,1:T(8,128)} %param.29) | copy-start | bytes 49156
  13.8 31.9 %copy-start.8 = (s32[96]{0:T(128)S(1)}, s32[96]{0:T(128)}, u32[]{:S(2)}) copy-start(s32[96]{0:T(128)} %get-tuple-element.16.tab) | copy-start | bytes 1156
  13.8 31.9 %copy-start.12 = (s32[256]{0:T(256)S(1)}, s32[256]{0:T(256)}, u32[]{:S(2)}) copy-start(s32[256]{0:T(256)} %kept.1) | copy-start | bytes 3076
  14.5 10.7 %collective-permute-start = (bf16[8,72,128]{2,1,0:T(8,128)(2,1)S(1)}, bf16[8,72,128]{2,1,0:T(8,128)(2,1)S(1)}, u32[]{:S(2)}, u32[]{:S(2)}) collective-permute-start(bf16[8,72,128]{2,1,0:T(8,128)(2,1)S(1)} %get-tuple-element.22), channel_id=1, source_target_pairs={{0,1},{1,0},{2,3},{3,2},{4,5},{5,4},{6,7},{7,6},{8,9},{9,8},{10,11... | collective-permute-start | bytes 442376 | tf_op jit(solution)/shard_map/ppermute | solution.py:385
  16.5 13.9 %collective-permute-start.1 = (bf16[8,72,128]{2,1,0:T(8,128)(2,1)S(1)}, bf16[8,72,128]{2,1,0:T(8,128)(2,1)S(1)}, u32[]{:S(2)}, u32[]{:S(2)}) collective-permute-start(bf16[8,72,128]{2,1,0:T(8,128)(2,1)S(1)} %get-tuple-element.23), channel_id=1, source_target_pairs={{0,16},{1,17},{2,18},{3,19},{4,20},{5,21},{6,22},{7,23},{8,24},{9,... | collective-permute-start | bytes 442376 | tf_op jit(solution)/shard_map/ppermute | solution.py:385
  18.6 11.8 %collective-permute-start.2 = (bf16[8,72,128]{2,1,0:T(8,128)(2,1)S(1)}, bf16[8,72,128]{2,1,0:T(8,128)(2,1)S(1)}, u32[]{:S(2)}, u32[]{:S(2)}) collective-permute-start(bf16[8,72,128]{2,1,0:T(8,128)(2,1)S(1)} %get-tuple-element.24), channel_id=1, source_target_pairs={{0,17},{1,16},{2,19},{3,18},{4,21},{5,20},{6,23},{7,22},{8,25},{9,... | collective-permute-start | bytes 442376 | tf_op jit(solution)/shard_map/ppermute | solution.py:385
  31.3 47.6 %copy-start = (bf16[16,96,256]{2,1,0:T(8,128)(2,1)}, bf16[16,96,256]{2,1,0:T(8,128)(2,1)S(1)}, u32[]{:S(2)}) copy-start(bf16[16,96,256]{2,1,0:T(8,128)(2,1)S(1)} %all-to-all-done.got_ref.got_hbm) | copy-start | bytes 2359300
  31.4 27.8 %all-to-all-start.1 = ((bf16[8,72,128]{2,1,0:T(8,128)(2,1)}), bf16[8,72,128]{2,1,0:T(8,128)(2,1)S(1)}, u32[]{:S(2)}, u32[]{:S(2)}) async-start(bf16[8,72,128]{2,1,0:T(8,128)(2,1)} %add_four.1), calls=%async_computation.1 | async-start | bytes 294912 | tf_op jit(solution)/shard_map/all_to_all | solution.py:416
  45.7 1.6 %copy-start.3 = (bf16[256,16,1,256]{3,1,2,0:T(8,128)(2,1)S(1)}, bf16[256,16,1,256]{3,1,2,0:T(8,128)(2,1)}, u32[]{:S(2)}) copy-start(bf16[256,16,1,256]{3,1,2,0:T(8,128)(2,1)} %param.17) | copy-start | bytes 6291460
  53.3 0.8 copy-start.2
  88.5 23.2 %copy-start.7 = (s32[256]{0:T(256)S(1)}, s32[256]{0:T(256)}, u32[]{:S(2)}) copy-start(s32[256]{0:T(256)} %entries.3) | copy-start | bytes 3076
  88.5 23.2 %copy-start.9 = (s32[96]{0:T(128)S(1)}, s32[96]{0:T(128)}, u32[]{:S(2)}) copy-start(s32[96]{0:T(128)} %get-tuple-element.16.tab) | copy-start | bytes 1156
  88.5 23.2 %copy-start.10 = (s32[256]{0:T(256)S(1)}, s32[256]{0:T(256)}, u32[]{:S(2)}) copy-start(s32[256]{0:T(256)} %fresh_len.3) | copy-start | bytes 3076
  88.6 23.1 %all-to-all-start.4 = ((bf16[16,72,256]{2,1,0:T(8,128)(2,1)}), bf16[16,72,256]{2,1,0:T(8,128)(2,1)S(1)}, u32[]{:S(2)}, u32[]{:S(2)}) async-start(bf16[16,72,256]{2,1,0:T(8,128)(2,1)} %gate.1), calls=%async_computation.4 | async-start | bytes 1179648 | tf_op jit(solution)/shard_map/all_to_all | solution.py:438
  111.7 0.7 copy-start.11

commit v5 on v4

--- a/solution.py
+++ b/solution.py
@@ -36,6 +36,7 @@
 HBM = pl.BlockSpec(memory_space=pltpu.HBM)
 SMEM = pl.BlockSpec(memory_space=pltpu.SMEM)
 SMALL = pltpu.CompilerParams(vmem_limit_bytes=12 * 1024 * 1024)
+MIDDLE = pltpu.CompilerParams(vmem_limit_bytes=32 * 1024 * 1024)
 PARAMS = pltpu.CompilerParams(vmem_limit_bytes=60 * 1024 * 1024)
 
 
@@ -266,6 +267,8 @@
     step = lax.broadcasted_iota(jnp.int32, (NEW, channels), 0)
     for n in range(NS):
         a_s[n * 8 : (n + 1) * 8, :] = jnp.broadcast_to(a_ref[n : n + 1, :] * (-LOG2E), (8, channels))
+    for at in range(low_ref.shape[0]):
+        bc_s[at * SUB : (at + 1) * SUB, :] = rest_of(low_ref[at, TILES * SUB : BLOCK, :].astype(F32))
     copies[0].wait()
     copies[1].wait()
     for member in range(4):
@@ -275,9 +278,6 @@
             at = member * (CHUNK // SUB) + k
             tiles = [low_ref[at, t * SUB : (t + 1) * SUB, :] for t in range(TILES)]
             low.append(jnp.concatenate(tiles, axis=1))
-            bc_s[first + k * SUB : first + (k + 1) * SUB, :] = rest_of(
-                low_ref[at, TILES * SUB : BLOCK, :].astype(F32)
-            )
         low = jnp.concatenate(low, axis=0)
         pre = jnp.dot(low, wdt_ref[...], preferred_element_type=F32) + b_ref[...]
         dt = jnp.maximum(pre, 0.0) + jnp.log1p(jnp.exp(-jnp.abs(pre)))
@@ -325,7 +325,7 @@
                 y_s[c, rows, :] = y[c]
             return tuple(new)
 
-        hs = lax.fori_loop(0, NEW, one_step, h0, unroll=8)
+        hs = lax.fori_loop(0, NEW, one_step, h0, unroll=16)
         for n in range(NS):
             for c in range(len(halves)):
                 h_s[c, pl.ds(begin + n, 8, stride=NS), :] = hs[n][c]
@@ -459,7 +459,7 @@
             pltpu.VMEM(got.shape, BF),
             pltpu.SemaphoreType.DMA((4,)),
         ],
-        compiler_params=PARAMS,
+        compiler_params=MIDDLE,
         name="scan",
     )(
         tab, cache_index, new_len, whole, w_dt, b_dt.reshape(1, -1), a_rate,

time: 115 us -> 114 us (level)
  Pallas kernels: 22.9 us -> 21.4 us
  waiting for transfers between devices: 13.5 us -> 15 us
    pallas_call x1, Pallas kernels: 8.35 us -> 6.85 us  [on_device(): pl.pallas_call(scan_kernel, out_shape=[jax.ShapeDtypeStruct((rows, channe...]
    all_to_all x1, waiting for transfers between devices: 3.31 us -> 4.73 us  [on_device(): back = lax.all_to_all(partial, 'req', 0, 0, tiled=True)]
    unnamed x32 -> x38, local copies, waits for them, and re-layouts: 3.37 us -> 2.69 us
  transfers between devices with their start and end apart: 6 -> 6, of which waited for: 3 -> 3; matrix products, arithmetic and copies ran while one was open for 0% -> 0% of each run, Pallas kernels for 16% -> 15%
where the time goes in v5:
time: 114 us
  starting transfers between devices  44.6 us (39%)
  blocking collectives  29.1 us (26%)
  Pallas kernels  21.4 us (19%)
  waiting for transfers between devices  15 us (13%)
  local copies, waits for them, and re-layouts  2.69 us (2%)
    all_to_all x1, blocking collectives, on_device(): lax.all_to_all(summed, 'mp', 0, 0, tiled=True, axis_index_groups=groups)  19.4 us
    all_to_all x1, starting transfers between devices, on_device(): lax.all_to_all(added, 'mp', 0, 0, tiled=True, axis_index_groups=groups)  14.3 us
    all_to_all x1, starting transfers between devices, on_device(): back = lax.all_to_all(partial, 'req', 0, 0, tiled=True)  11.5 us
    all_to_all x1, starting transfers between devices, on_device(): got = lax.all_to_all(packed, 'req', 0, 0, tiled=True)  10.4 us
    all_to_all x1, blocking collectives, on_device(): lax.all_to_all(whole, 'mp', 0, 0, tiled=True, axis_index_groups=quads)  9.74 us
    ppermute x3, starting transfers between devices, swap(): return lax.ppermute(array, 'mp', pairs)  8.37 us
    pallas_call x1, Pallas kernels, on_device(): pl.pallas_call(scan_kernel, out_shape=[jax.ShapeDtypeStruct((rows, channe...  6.85 us
    pallas_call x1, Pallas kernels, on_device(): pl.pallas_call(cached_kernel, out_shape=[jax.ShapeDtypeStruct((REQ, RET,...  5.95 us
  transfers between devices with their start and end apart: 6, of which 3 were waited for; matrix products, arithmetic and copies ran while one was open for 0% of the time, Pallas kernels for 15%

profile of v5, /device:TPU:1, one launch (start us, length us, event | category | flops | bytes accessed | tf_op | source)
XLA Modules:
  0.0 113.9 jit_solution(6310299224450613150)
XLA Ops:
  0.7 2.6 %pack.1 = (bf16[16,96,256]{2,1,0:T(8,128)(2,1)}, s32[96]{0:T(128)}) custom-call(s32[256]{0:T(256)} %entries.3, bf16[512,256]{1,0:T(8,128)(2,1)} %q_ref.1, f32[16,16,256]{2,1,0:T(8,128)} %cache_hbm.1), custom_call_target="tpu_custom_call" | custom-call | tf_op jit(solution)/shard_map/pack/pallas_call | solution.py:351
  3.3 10.4 %all-to-all-start = ((bf16[16,96,256]{2,1,0:T(8,128)(2,1)}), bf16[16,96,256]{2,1,0:T(8,128)(2,1)S(1)}, u32[]{:S(2)}, u32[]{:S(2)}) async-start(bf16[16,96,256]{2,1,0:T(8,128)(2,1)} %get-tuple-element.19.after), calls=%async_computation | async-start | bytes 1572864 | tf_op jit(solution)/shard_map/all_to_all | solution.py:368
  13.8 0.0 copy-start.17
  13.8 0.0 copy-start.11
  13.8 0.0 copy-start.15
  13.8 0.2 copy.19.w_ref
  14.0 0.5 project.1
  14.5 1.9 %collective-permute-start = (bf16[8,72,128]{2,1,0:T(8,128)(2,1)S(1)}, bf16[8,72,128]{2,1,0:T(8,128)(2,1)S(1)}, u32[]{:S(2)}, u32[]{:S(2)}) collective-permute-start(bf16[8,72,128]{2,1,0:T(8,128)(2,1)S(1)} %get-tuple-element.22), channel_id=1, source_target_pairs={{0,1},{1,0},{2,3},{3,2},{4,5},{5,4},{6,7},{7,6},{8,9},{9,8},{10,11... | collective-permute-start | bytes 442376 | tf_op jit(solution)/shard_map/ppermute | solution.py:385
  16.5 2.1 %collective-permute-start.1 = (bf16[8,72,128]{2,1,0:T(8,128)(2,1)S(1)}, bf16[8,72,128]{2,1,0:T(8,128)(2,1)S(1)}, u32[]{:S(2)}, u32[]{:S(2)}) collective-permute-start(bf16[8,72,128]{2,1,0:T(8,128)(2,1)S(1)} %get-tuple-element.23), channel_id=1, source_target_pairs={{0,16},{1,17},{2,18},{3,19},{4,20},{5,21},{6,22},{7,23},{8,24},{9,... | collective-permute-start | bytes 442376 | tf_op jit(solution)/shard_map/ppermute | solution.py:385
  18.6 4.3 %collective-permute-start.2 = (bf16[8,72,128]{2,1,0:T(8,128)(2,1)S(1)}, bf16[8,72,128]{2,1,0:T(8,128)(2,1)S(1)}, u32[]{:S(2)}, u32[]{:S(2)}) collective-permute-start(bf16[8,72,128]{2,1,0:T(8,128)(2,1)S(1)} %get-tuple-element.24), channel_id=1, source_target_pairs={{0,17},{1,16},{2,19},{3,18},{4,21},{5,20},{6,23},{7,22},{8,25},{9,... | collective-permute-start | bytes 442376 | tf_op jit(solution)/shard_map/ppermute | solution.py:385
  22.9 2.3 %fresh.1 = (f32[16,64,128]{2,1,0:T(8,128)S(1)}, f32[16,8,128]{2,1,0:T(8,128)S(1)}) custom-call(bf16[512,256]{1,0:T(8,128)(2,1)S(1)} %copy-done.4, bf16[512,256]{1,0:T(8,128)(2,1)S(1)} %bitcast.9), custom_call_target="tpu_custom_call" | custom-call | tf_op jit(solution)/shard_map/fresh/pallas_call | solution.py:391
  25.2 5.1 %collective-permute-done.1.r2 = bf16[8,72,128]{2,1,0:T(8,128)(2,1)S(1)} collective-permute-done((bf16[8,72,128]{2,1,0:T(8,128)(2,1)S(1)}, bf16[8,72,128]{2,1,0:T(8,128)(2,1)S(1)}, u32[]{:S(2)}, u32[]{:S(2)}) %collective-permute-start.1) | collective-permute-done | bytes 147488 | tf_op jit(solution)/shard_map/ppermute | solution.py:385
  30.4 1.0 add_four.1
  31.3 14.3 %all-to-all-start.1 = ((bf16[8,72,128]{2,1,0:T(8,128)(2,1)}), bf16[8,72,128]{2,1,0:T(8,128)(2,1)S(1)}, u32[]{:S(2)}, u32[]{:S(2)}) async-start(bf16[8,72,128]{2,1,0:T(8,128)(2,1)} %add_four.1), calls=%async_computation.1 | async-start | bytes 294912 | tf_op jit(solution)/shard_map/all_to_all | solution.py:416
  45.7 0.0 copy-start.3
  45.7 1.6 %copy-done.3 = bf16[256,16,1,256]{3,1,2,0:T(8,128)(2,1)S(1)} copy-done((bf16[256,16,1,256]{3,1,2,0:T(8,128)(2,1)S(1)}, bf16[256,16,1,256]{3,1,2,0:T(8,128)(2,1)}, u32[]{:S(2)}) %copy-start.3) | copy-done | bytes 2097176
  47.3 5.9 %cached.1 = (bf16[16,72,256]{2,1,0:T(8,128)(2,1)S(1)}, f32[8,128]{1,0:T(8,128)S(1)}) custom-call(s32[96]{0:T(128)S(1)} %copy-done.11, s32[4096]{0:T(1024)S(1)} %bitcast.10, s32[256]{0:T(256)S(1)} %copy-done.15, bf16[16,96,256]{2,1,0:T(8,128)(2,1)S(1)} %all-to-all-done.got_ref.got_hbm, bf16[256,16,256]{2,1,0:T(8,128)(2,1)S(1)} %bitcast.8), custom_call_target="tpu_custom_call" | custom-call | tf_op jit(solution)/shard_map/cached/pallas_call | solution.py:408
  53.3 0.8 copy-done.2
  54.1 5.1 %all-to-all-done.1.parts = bf16[8,72,128]{2,1,0:T(8,128)(2,1)S(1)} async-done(((bf16[8,72,128]{2,1,0:T(8,128)(2,1)}), bf16[8,72,128]{2,1,0:T(8,128)(2,1)S(1)}, u32[]{:S(2)}, u32[]{:S(2)}) %all-to-all-start.1) | async-done | bytes 147488 | tf_op jit(solution)/shard_map/all_to_all | solution.py:416
  59.2 0.3 add_eight.1
  59.5 19.4 %all_to_all.25 = bf16[8,72,128]{2,1,0:T(8,128)(2,1)S(1)} all-to-all(bf16[8,72,128]{2,1,0:T(8,128)(2,1)S(1)} %add_eight.1), channel_id=1, replica_groups={{0,2,4,6,8,10,12,14},{1,3,5,7,9,11,13,15},{16,18,20,22,24,26,28,30},{17..., dimensions={0} | all-to-all | bytes 294912 | tf_op jit(solution)/shard_map/all_to_all | solution.py:425
  78.8 0.1 pad_maximum_fusion
  78.9 0.0 copy-start.6
  78.9 0.0 copy-start.7
  78.9 0.0 copy-start.9
  78.9 0.0 copy-start.10
  79.0 0.0 copy-start.14
  79.0 9.7 %all_to_all.26.after.low_ref = bf16[32,72,128]{2,1,0:T(8,128)(2,1)} all-to-all(bf16[32,72,128]{2,1,0:T(8,128)(2,1)S(1)} %pad_maximum_fusion), channel_id=1, replica_groups={{0,1,16,17},{2,3,18,19},{4,5,20,21},{6,7,22,23},{8,9,24,25},{10,11,26,2..., dimensions={0} | all-to-all | bytes 1179648 | tf_op jit(solution)/shard_map/all_to_all | solution.py:427
  88.7 11.5 %all-to-all-start.4 = ((bf16[16,72,256]{2,1,0:T(8,128)(2,1)}), bf16[16,72,256]{2,1,0:T(8,128)(2,1)S(1)}, u32[]{:S(2)}, u32[]{:S(2)}) async-start(bf16[16,72,256]{2,1,0:T(8,128)(2,1)} %gate.1), calls=%async_computation.4 | async-start | bytes 1179648 | tf_op jit(solution)/shard_map/all_to_all | solution.py:438
  100.3 6.8 %scan.1 = (bf16[512,256]{1,0:T(8,128)(2,1)}, f32[256,256]{1,0:T(8,128)}, f32[8,128]{1,0:T(8,128)S(1)}) custom-call(s32[96]{0:T(128)S(1)} %copy-done.11, s32[256]{0:T(256)S(1)} %copy-done.10, s32[256]{0:T(256)S(1)} %copy-done.12, bf16[32,72,128]{2,1,0:T(8,128)(2,1)S(1)} %copy-done, bf16[512,256]{1,0:T(8,128)(2,1)S(1)} %copy-done.6, f32[1,256]{1,0:T(1,128)S(1)} %bitcast.11, ...), custom_call_target="tpu_custom_call" | custom-call | tf_op jit(solution)/shard_map/scan/pallas_call | solution.py:440
  107.2 4.7 %all-to-all-done.4.got_ref = bf16[16,72,256]{2,1,0:T(8,128)(2,1)S(1)} async-done(((bf16[16,72,256]{2,1,0:T(8,128)(2,1)}), bf16[16,72,256]{2,1,0:T(8,128)(2,1)S(1)}, u32[]{:S(2)}, u32[]{:S(2)}) %all-to-all-start.4) | async-done | bytes 589856 | tf_op jit(solution)/shard_map/all_to_all | solution.py:438
  111.9 2.0 %combine.1 = bf16[512,256]{1,0:T(8,128)(2,1)} custom-call(s32[96]{0:T(128)S(1)} %copy-done.11, s32[256]{0:T(256)S(1)} %copy-done.10, s32[256]{0:T(256)S(1)} %copy-done.12, f32[16,64,128]{2,1,0:T(8,128)S(1)} %get-tuple-element.17.part_ref, f32[16,8,128]{2,1,0:T(8,128)S(1)} %get-tuple-element.18.after.stat_ref, ...), custom_call_target="tpu_custom_call" | custom-call | tf_op jit(solution)/shard_map/combine/pallas_call | solution.py:468
  (30 shorter events, 0.1 us)
Async XLA Ops:
  0.6 22.3 %copy-start.4 = (bf16[512,256]{1,0:T(8,128)(2,1)S(1)}, bf16[512,256]{1,0:T(8,128)(2,1)}, u32[]{:S(2)}) copy-start(bf16[512,256]{1,0:T(8,128)(2,1)} %q_ref.1) | copy-start | bytes 786436
  0.6 13.1 %copy-start.16 = (bf16[256,544]{0,1:T(8,128)(2,1)S(1)}, bf16[256,544]{0,1:T(8,128)(2,1)}, u32[]{:S(2)}) copy-start(bf16[256,544]{0,1:T(8,128)(2,1)} %param.21) | copy-start | bytes 835588
  0.7 13.3 %copy-start.5 = (bf16[512,256]{1,0:T(8,128)(2,1)S(1)}, bf16[512,256]{1,0:T(8,128)(2,1)}, u32[]{:S(2)}) copy-start(bf16[512,256]{1,0:T(8,128)(2,1)} %x_hbm.1) | copy-start | bytes 786436
  0.7 22.3 %copy-start.8 = (bf16[512,1,256]{2,0,1:T(8,128)(2,1)S(1)}, bf16[512,1,256]{2,0,1:T(8,128)(2,1)}, u32[]{:S(2)}) copy-start(bf16[512,1,256]{2,0,1:T(8,128)(2,1)} %param.16) | copy-start | bytes 786436
  3.3 10.7 %copy-start.1 = (bf16[16,96,256]{2,1,0:T(8,128)(2,1)S(1)}, bf16[16,96,256]{2,1,0:T(8,128)(2,1)}, u32[]{:S(2)}) copy-start(bf16[16,96,256]{2,1,0:T(8,128)(2,1)} %get-tuple-element.19.after) | copy-start | bytes 2359300
  3.3 28.0 %all-to-all-start = ((bf16[16,96,256]{2,1,0:T(8,128)(2,1)}), bf16[16,96,256]{2,1,0:T(8,128)(2,1)S(1)}, u32[]{:S(2)}, u32[]{:S(2)}) async-start(bf16[16,96,256]{2,1,0:T(8,128)(2,1)} %get-tuple-element.19.after), calls=%async_computation | async-start | bytes 1572864 | tf_op jit(solution)/shard_map/all_to_all | solution.py:368
  13.8 31.9 %copy-start.17 = (s32[256,16]{0,1:T(8,128)S(1)}, s32[256,16]{0,1:T(8,128)}, u32[]{:S(2)}) copy-start(s32[256,16]{0,1:T(8,128)} %param.29) | copy-start | bytes 49156
  13.8 31.9 %copy-start.11 = (s32[96]{0:T(128)S(1)}, s32[96]{0:T(128)}, u32[]{:S(2)}) copy-start(s32[96]{0:T(128)} %get-tuple-element.16.tab) | copy-start | bytes 1156
  13.8 31.9 %copy-start.15 = (s32[256]{0:T(256)S(1)}, s32[256]{0:T(256)}, u32[]{:S(2)}) copy-start(s32[256]{0:T(256)} %kept.1) | copy-start | bytes 3076
  14.5 10.7 %collective-permute-start = (bf16[8,72,128]{2,1,0:T(8,128)(2,1)S(1)}, bf16[8,72,128]{2,1,0:T(8,128)(2,1)S(1)}, u32[]{:S(2)}, u32[]{:S(2)}) collective-permute-start(bf16[8,72,128]{2,1,0:T(8,128)(2,1)S(1)} %get-tuple-element.22), channel_id=1, source_target_pairs={{0,1},{1,0},{2,3},{3,2},{4,5},{5,4},{6,7},{7,6},{8,9},{9,8},{10,11... | collective-permute-start | bytes 442376 | tf_op jit(solution)/shard_map/ppermute | solution.py:385
  16.5 13.9 %collective-permute-start.1 = (bf16[8,72,128]{2,1,0:T(8,128)(2,1)S(1)}, bf16[8,72,128]{2,1,0:T(8,128)(2,1)S(1)}, u32[]{:S(2)}, u32[]{:S(2)}) collective-permute-start(bf16[8,72,128]{2,1,0:T(8,128)(2,1)S(1)} %get-tuple-element.23), channel_id=1, source_target_pairs={{0,16},{1,17},{2,18},{3,19},{4,20},{5,21},{6,22},{7,23},{8,24},{9,... | collective-permute-start | bytes 442376 | tf_op jit(solution)/shard_map/ppermute | solution.py:385
  18.6 11.8 %collective-permute-start.2 = (bf16[8,72,128]{2,1,0:T(8,128)(2,1)S(1)}, bf16[8,72,128]{2,1,0:T(8,128)(2,1)S(1)}, u32[]{:S(2)}, u32[]{:S(2)}) collective-permute-start(bf16[8,72,128]{2,1,0:T(8,128)(2,1)S(1)} %get-tuple-element.24), channel_id=1, source_target_pairs={{0,17},{1,16},{2,19},{3,18},{4,21},{5,20},{6,23},{7,22},{8,25},{9,... | collective-permute-start | bytes 442376 | tf_op jit(solution)/shard_map/ppermute | solution.py:385
  31.3 27.8 %all-to-all-start.1 = ((bf16[8,72,128]{2,1,0:T(8,128)(2,1)}), bf16[8,72,128]{2,1,0:T(8,128)(2,1)S(1)}, u32[]{:S(2)}, u32[]{:S(2)}) async-start(bf16[8,72,128]{2,1,0:T(8,128)(2,1)} %add_four.1), calls=%async_computation.1 | async-start | bytes 294912 | tf_op jit(solution)/shard_map/all_to_all | solution.py:416
  45.7 1.6 %copy-start.3 = (bf16[256,16,1,256]{3,1,2,0:T(8,128)(2,1)S(1)}, bf16[256,16,1,256]{3,1,2,0:T(8,128)(2,1)}, u32[]{:S(2)}) copy-start(bf16[256,16,1,256]{3,1,2,0:T(8,128)(2,1)} %param.17) | copy-start | bytes 6291460
  53.3 0.8 copy-start.2
  78.9 21.3 %copy-start.6 = (bf16[512,256]{1,0:T(8,128)(2,1)S(1)}, bf16[512,256]{1,0:T(8,128)(2,1)}, u32[]{:S(2)}) copy-start(bf16[512,256]{1,0:T(8,128)(2,1)} %wdt_hbm.1) | copy-start | bytes 786436
  78.9 21.3 %copy-start.7 = (bf16[512,256]{1,0:T(8,128)(2,1)S(1)}, bf16[512,256]{1,0:T(8,128)(2,1)}, u32[]{:S(2)}) copy-start(bf16[512,256]{1,0:T(8,128)(2,1)} %g_hbm.1) | copy-start | bytes 786436
  78.9 21.3 %copy-start.9 = (f32[16,256]{1,0:T(8,128)S(1)}, f32[16,256]{1,0:T(8,128)}, u32[]{:S(2)}) copy-start(f32[16,256]{1,0:T(8,128)} %a_ref.1) | copy-start | bytes 49156
  78.9 21.3 %copy-start.10 = (s32[256]{0:T(256)S(1)}, s32[256]{0:T(256)}, u32[]{:S(2)}) copy-start(s32[256]{0:T(256)} %entries.3) | copy-start | bytes 3076
  79.0 21.3 %copy-start.12 = (s32[256]{0:T(256)S(1)}, s32[256]{0:T(256)}, u32[]{:S(2)}) copy-start(s32[256]{0:T(256)} %fresh_len.3) | copy-start | bytes 3076
  79.0 21.3 %copy-start.13 = (f32[256]{0:T(256)S(1)}, f32[256]{0:T(256)}, u32[]{:S(2)}) copy-start(f32[256]{0:T(256)} %param.23) | copy-start | bytes 3076
  79.0 21.3 %copy-start.14 = (f32[256]{0:T(256)S(1)}, f32[256]{0:T(256)}, u32[]{:S(2)}) copy-start(f32[256]{0:T(256)} %param.25) | copy-start | bytes 3076
  88.7 11.6 %copy-start = (bf16[32,72,128]{2,1,0:T(8,128)(2,1)S(1)}, bf16[32,72,128]{2,1,0:T(8,128)(2,1)}, u32[]{:S(2)}) copy-start(bf16[32,72,128]{2,1,0:T(8,128)(2,1)} %all_to_all.26.after.low_ref) | copy-start | bytes 1769476
  88.7 23.2 %all-to-all-start.4 = ((bf16[16,72,256]{2,1,0:T(8,128)(2,1)}), bf16[16,72,256]{2,1,0:T(8,128)(2,1)S(1)}, u32[]{:S(2)}, u32[]{:S(2)}) async-start(bf16[16,72,256]{2,1,0:T(8,128)(2,1)} %gate.1), calls=%async_computation.4 | async-start | bytes 1179648 | tf_op jit(solution)/shard_map/all_to_all | solution.py:438

commit v6 on v5

--- a/solution.py
+++ b/solution.py
@@ -106,7 +106,7 @@
             out_ref[p, 2 * NEW + k * NS : 2 * NEW + (k + 1) * NS, :] = cache_ref[entry].astype(BF)
 
 
-def project_kernel(x_ref, w_ref, after, own_ref, *sent):
+def project_kernel(x_ref, w_ref, after, own_ref, far_ref, sent):
     at = lax.axis_index("mp")
     member = (at // (lax.axis_size("mp") // 2)) * 2 + (at & 1)
     for d in range(4):
@@ -115,22 +115,31 @@
         low = jnp.dot(rows, w_ref[:, :RANK], preferred_element_type=F32)
         rest = jnp.dot(rows, w_ref[:, RANK:], preferred_element_type=F32)
         rest = jnp.concatenate([rest, jnp.zeros((CHUNK, COLS - RANK - BC), F32)], axis=1)
-        if d == 0:
-            own_ref[:, :RANK] = low
-            own_ref[:, RANK:] = rest
+        if d % 2 == 0:
+            kept = far_ref if d else own_ref
+            kept[:, :RANK] = low
+            kept[:, RANK:] = rest
         else:
             for k in range(CHUNK // SUB):
                 some = slice(k * SUB, (k + 1) * SUB)
-                store_block(sent[d - 1], k, low[some], rest[some])
-
-
-def add_four_kernel(own_ref, r1, r2, r3, after, out_ref):
+                store_block(sent, d // 2 * (CHUNK // SUB) + k, low[some], rest[some])
+
+
+def add_block(kept, k, block, out_ref):
+    some = slice(k * SUB, (k + 1) * SUB)
+    tiles = [block[t * SUB : (t + 1) * SUB] for t in range(TILES)]
+    low = kept[some, :RANK] + jnp.concatenate(tiles, axis=1)
+    store_block(out_ref, k, low, kept[some, RANK:] + rest_of(block[TILES * SUB :]))
+
+
+def add_two_kernel(far_ref, r1, after, out_ref):
     for k in range(CHUNK // SUB):
-        some = slice(k * SUB, (k + 1) * SUB)
-        block = r1[k].astype(F32) + r2[k].astype(F32) + r3[k].astype(F32)
-        tiles = [block[t * SUB : (t + 1) * SUB] for t in range(TILES)]
-        low = own_ref[some, :RANK] + jnp.concatenate(tiles, axis=1)
-        store_block(out_ref, k, low, own_ref[some, RANK:] + rest_of(block[TILES * SUB :]))
+        add_block(far_ref, k, r1[CHUNK // SUB + k].astype(F32), out_ref)
+
+
+def add_four_kernel(own_ref, r1, r2, out_ref):
+    for k in range(CHUNK // SUB):
+        add_block(own_ref, k, r1[k].astype(F32) + r2[k].astype(F32), out_ref)
 
 
 def add_eight_kernel(parts, after, out_ref):
@@ -368,11 +377,15 @@
     got = lax.all_to_all(packed, "req", 0, 0, tiled=True)
 
     chunk = jax.ShapeDtypeStruct((CHUNK // SUB, BLOCK, HD), BF)
-    own, *sent = pl.pallas_call(
+    own, far, sent = pl.pallas_call(
         project_kernel,
-        out_shape=[jax.ShapeDtypeStruct((CHUNK, COLS), F32), chunk, chunk, chunk],
+        out_shape=[
+            jax.ShapeDtypeStruct((CHUNK, COLS), F32),
+            jax.ShapeDtypeStruct((CHUNK, COLS), F32),
+            jax.ShapeDtypeStruct((2 * CHUNK // SUB, BLOCK, HD), BF),
+        ],
         in_specs=[VMEM, VMEM, ANY],
-        out_specs=[VMEM] * 4,
+        out_specs=[VMEM] * 3,
         compiler_params=SMALL,
         name="project",
     )(mixer_in, w_x, packed)
@@ -386,7 +399,6 @@
 
     quads = [[y * zs + 2 * k + b for y in range(2) for b in range(2)] for k in range(zs // 2)]
     groups = [[y * zs + 2 * k + b for k in range(zs // 2)] for y in range(2) for b in range(2)]
-    received = [swap(sent[d - 1], d) for d in (1, 2, 3)]
     block = jax.ShapeDtypeStruct((REQ, 2 * NEW, HD), F32)
     fresh = pl.pallas_call(
         fresh_kernel,
@@ -396,14 +408,24 @@
         compiler_params=SMALL,
         name="fresh",
     )(queries, kv_new.reshape(rows, channels))
+    near = swap(sent, 1)
+    pair = pl.pallas_call(
+        add_two_kernel,
+        out_shape=chunk,
+        in_specs=[VMEM] * 2 + [ANY],
+        out_specs=VMEM,
+        compiler_params=SMALL,
+        name="add_two",
+    )(far, near, fresh[1])
+    across = swap(pair, 2)
     added = pl.pallas_call(
         add_four_kernel,
         out_shape=chunk,
-        in_specs=[VMEM] * 4 + [ANY],
+        in_specs=[VMEM] * 3,
         out_specs=VMEM,
         compiler_params=SMALL,
         name="add_four",
-    )(own, *received, fresh[1])
+    )(own, near, across)
     token = jax.ShapeDtypeStruct((8, HD), F32)
     partial, cached = pl.pallas_call(
         cached_kernel,

time: 114 us -> 113 us (level)
  starting transfers between devices: 44.6 us -> 38.9 us
  waiting for transfers between devices: 15 us -> 20.1 us
    ppermute x3 -> x2, starting transfers between devices: 8.37 us -> 3.97 us  [swap(): return lax.ppermute(array, 'mp', pairs)]
    ppermute x3 -> x2, waiting for transfers between devices: 5.15 us -> 8.57 us  [swap(): return lax.ppermute(array, 'mp', pairs)]
    all_to_all x1, waiting for transfers between devices: 5.09 us -> 6.82 us  [on_device(): lax.all_to_all(added, 'mp', 0, 0, tiled=True, axis_index_groups=groups)]
    unnamed x38 -> x42, local copies, waits for them, and re-layouts: 2.69 us -> 2.86 us
  transfers between devices with their start and end apart: 6 -> 5, of which waited for: 3 -> 4; matrix products, arithmetic and copies ran while one was open for 0% -> 0% of each run, Pallas kernels for 15% -> 15%
where the time goes in v6:
time: 113 us
  starting transfers between devices  38.9 us (34%)
  blocking collectives  28 us (25%)
  Pallas kernels  21.8 us (19%)
  waiting for transfers between devices  20.1 us (18%)
  local copies, waits for them, and re-layouts  2.86 us (3%)
    all_to_all x1, blocking collectives, on_device(): lax.all_to_all(summed, 'mp', 0, 0, tiled=True, axis_index_groups=groups)  18.3 us
    all_to_all x1, starting transfers between devices, on_device(): lax.all_to_all(added, 'mp', 0, 0, tiled=True, axis_index_groups=groups)  13.4 us
    all_to_all x1, starting transfers between devices, on_device(): back = lax.all_to_all(partial, 'req', 0, 0, tiled=True)  11.1 us
    all_to_all x1, starting transfers between devices, on_device(): got = lax.all_to_all(packed, 'req', 0, 0, tiled=True)  10.4 us
    all_to_all x1, blocking collectives, on_device(): lax.all_to_all(whole, 'mp', 0, 0, tiled=True, axis_index_groups=quads)  9.74 us
    ppermute x2, waiting for transfers between devices, swap(): return lax.ppermute(array, 'mp', pairs)  8.57 us
    pallas_call x1, Pallas kernels, on_device(): pl.pallas_call(scan_kernel, out_shape=[jax.ShapeDtypeStruct((rows, channe...  6.85 us
    all_to_all x1, waiting for transfers between devices, on_device(): lax.all_to_all(added, 'mp', 0, 0, tiled=True, axis_index_groups=groups)  6.82 us
  transfers between devices with their start and end apart: 5, of which 4 were waited for; matrix products, arithmetic and copies ran while one was open for 0% of the time, Pallas kernels for 15%

profile of v6, /device:TPU:1, one launch (start us, length us, event | category | flops | bytes accessed | tf_op | source)
XLA Modules:
  0.0 112.6 jit_solution(13193639603433073274)
XLA Ops:
  0.7 2.6 %pack.1 = (bf16[16,96,256]{2,1,0:T(8,128)(2,1)}, s32[96]{0:T(128)}) custom-call(s32[256]{0:T(256)} %entries.3, bf16[512,256]{1,0:T(8,128)(2,1)} %q_ref.1, f32[16,16,256]{2,1,0:T(8,128)} %cache_hbm.1), custom_call_target="tpu_custom_call" | custom-call | tf_op jit(solution)/shard_map/pack/pallas_call | solution.py:360
  3.3 10.4 %all-to-all-start = ((bf16[16,96,256]{2,1,0:T(8,128)(2,1)}), bf16[16,96,256]{2,1,0:T(8,128)(2,1)S(1)}, u32[]{:S(2)}, u32[]{:S(2)}) async-start(bf16[16,96,256]{2,1,0:T(8,128)(2,1)} %get-tuple-element.18.after), calls=%async_computation | async-start | bytes 1572864 | tf_op jit(solution)/shard_map/all_to_all | solution.py:377
  13.7 0.2 copy.19.w_ref
  14.0 0.0 copy-start.19
  14.0 0.0 copy-start.13
  14.0 0.0 copy-start.17
  14.0 0.5 project.1
  14.5 2.1 %collective-permute-start = (bf16[16,72,128]{2,1,0:T(8,128)(2,1)S(1)}, bf16[16,72,128]{2,1,0:T(8,128)(2,1)S(1)}, u32[]{:S(2)}, u32[]{:S(2)}) collective-permute-start(bf16[16,72,128]{2,1,0:T(8,128)(2,1)S(1)} %get-tuple-element.21), channel_id=1, source_target_pairs={{0,1},{1,0},{2,3},{3,2},{4,5},{5,4},{6,7},{7,6},{8,9},{9,8},{10,11... | collective-permute-start | bytes 884744 | tf_op jit(solution)/shard_map/ppermute | solution.py:398
  16.6 0.0 copy-start.10
  16.6 0.9 copy-done.10
  17.6 2.3 %fresh.1 = (f32[16,64,128]{2,1,0:T(8,128)S(1)}, f32[16,8,128]{2,1,0:T(8,128)S(1)}) custom-call(bf16[512,256]{1,0:T(8,128)(2,1)S(1)} %copy-done.4, bf16[512,256]{1,0:T(8,128)(2,1)S(1)} %bitcast.9), custom_call_target="tpu_custom_call" | custom-call | tf_op jit(solution)/shard_map/fresh/pallas_call | solution.py:403
  19.8 0.8 copy-done.6
  20.6 4.3 %collective-permute-done.r1 = bf16[16,72,128]{2,1,0:T(8,128)(2,1)S(1)} collective-permute-done((bf16[16,72,128]{2,1,0:T(8,128)(2,1)S(1)}, bf16[16,72,128]{2,1,0:T(8,128)(2,1)S(1)}, u32[]{:S(2)}, u32[]{:S(2)}) %collective-permute-start) | collective-permute-done | bytes 294944 | tf_op jit(solution)/shard_map/ppermute | solution.py:398
  24.9 0.3 add_two.1
  25.2 1.9 %collective-permute-start.1 = (bf16[8,72,128]{2,1,0:T(8,128)(2,1)S(1)}, bf16[8,72,128]{2,1,0:T(8,128)(2,1)S(1)}, u32[]{:S(2)}, u32[]{:S(2)}) collective-permute-start(bf16[8,72,128]{2,1,0:T(8,128)(2,1)S(1)} %add_two.1), channel_id=1, source_target_pairs={{0,16},{1,17},{2,18},{3,19},{4,20},{5,21},{6,22},{7,23},{8,24},{9,... | collective-permute-start | bytes 442376 | tf_op jit(solution)/shard_map/ppermute | solution.py:398
  27.2 4.3 %collective-permute-done.1.r2 = bf16[8,72,128]{2,1,0:T(8,128)(2,1)S(1)} collective-permute-done((bf16[8,72,128]{2,1,0:T(8,128)(2,1)S(1)}, bf16[8,72,128]{2,1,0:T(8,128)(2,1)S(1)}, u32[]{:S(2)}, u32[]{:S(2)}) %collective-permute-start.1) | collective-permute-done | bytes 147488 | tf_op jit(solution)/shard_map/ppermute | solution.py:398
  31.4 1.0 add_four.1
  32.4 13.4 %all-to-all-start.1 = ((bf16[8,72,128]{2,1,0:T(8,128)(2,1)}), bf16[8,72,128]{2,1,0:T(8,128)(2,1)S(1)}, u32[]{:S(2)}, u32[]{:S(2)}) async-start(bf16[8,72,128]{2,1,0:T(8,128)(2,1)} %add_four.1), calls=%async_computation.1 | async-start | bytes 294912 | tf_op jit(solution)/shard_map/all_to_all | solution.py:438
  45.8 6.0 %cached.1 = (bf16[16,72,256]{2,1,0:T(8,128)(2,1)S(1)}, f32[8,128]{1,0:T(8,128)S(1)}) custom-call(s32[96]{0:T(128)S(1)} %copy-done.13, s32[4096]{0:T(1024)S(1)} %bitcast.10, s32[256]{0:T(256)S(1)} %copy-done.17, bf16[16,96,256]{2,1,0:T(8,128)(2,1)S(1)} %all-to-all-done.got_ref.got_hbm, bf16[256,16,256]{2,1,0:T(8,128)(2,1)S(1)} %bitcast.8), custom_call_target="tpu_custom_call" | custom-call | tf_op jit(solution)/shard_map/cached/pallas_call | solution.py:430
  51.8 0.8 copy-done.2
  52.6 6.8 %all-to-all-done.1.parts = bf16[8,72,128]{2,1,0:T(8,128)(2,1)S(1)} async-done(((bf16[8,72,128]{2,1,0:T(8,128)(2,1)}), bf16[8,72,128]{2,1,0:T(8,128)(2,1)S(1)}, u32[]{:S(2)}, u32[]{:S(2)}) %all-to-all-start.1) | async-done | bytes 147488 | tf_op jit(solution)/shard_map/all_to_all | solution.py:438
  59.4 0.3 add_eight.1
  59.7 18.3 %all_to_all.25 = bf16[8,72,128]{2,1,0:T(8,128)(2,1)S(1)} all-to-all(bf16[8,72,128]{2,1,0:T(8,128)(2,1)S(1)} %add_eight.1), channel_id=1, replica_groups={{0,2,4,6,8,10,12,14},{1,3,5,7,9,11,13,15},{16,18,20,22,24,26,28,30},{17..., dimensions={0} | all-to-all | bytes 294912 | tf_op jit(solution)/shard_map/all_to_all | solution.py:447
  78.0 0.1 pad_maximum_fusion
  78.1 0.0 copy-start.11
  78.1 0.0 copy-start.12
  78.1 0.0 copy-start.16
  78.1 9.7 %all_to_all.26.after.low_ref = bf16[32,72,128]{2,1,0:T(8,128)(2,1)} all-to-all(bf16[32,72,128]{2,1,0:T(8,128)(2,1)S(1)} %pad_maximum_fusion), channel_id=1, replica_groups={{0,1,16,17},{2,3,18,19},{4,5,20,21},{6,7,22,23},{8,9,24,25},{10,11,26,2..., dimensions={0} | all-to-all | bytes 1179648 | tf_op jit(solution)/shard_map/all_to_all | solution.py:449
  87.9 11.1 %all-to-all-start.4 = ((bf16[16,72,256]{2,1,0:T(8,128)(2,1)}), bf16[16,72,256]{2,1,0:T(8,128)(2,1)S(1)}, u32[]{:S(2)}, u32[]{:S(2)}) async-start(bf16[16,72,256]{2,1,0:T(8,128)(2,1)} %gate.1), calls=%async_computation.4 | async-start | bytes 1179648 | tf_op jit(solution)/shard_map/all_to_all | solution.py:460
  99.0 6.8 %scan.1 = (bf16[512,256]{1,0:T(8,128)(2,1)}, f32[256,256]{1,0:T(8,128)}, f32[8,128]{1,0:T(8,128)S(1)}) custom-call(s32[96]{0:T(128)S(1)} %copy-done.13, s32[256]{0:T(256)S(1)} %copy-done.12, s32[256]{0:T(256)S(1)} %copy-done.14, bf16[32,72,128]{2,1,0:T(8,128)(2,1)S(1)} %copy-done, bf16[512,256]{1,0:T(8,128)(2,1)S(1)} %copy-done.8, f32[1,256]{1,0:T(1,128)S(1)} %bitcast.11, ...), custom_call_target="tpu_custom_call" | custom-call | tf_op jit(solution)/shard_map/scan/pallas_call | solution.py:462
  105.9 4.7 %all-to-all-done.4.got_ref = bf16[16,72,256]{2,1,0:T(8,128)(2,1)S(1)} async-done(((bf16[16,72,256]{2,1,0:T(8,128)(2,1)}), bf16[16,72,256]{2,1,0:T(8,128)(2,1)S(1)}, u32[]{:S(2)}, u32[]{:S(2)}) %all-to-all-start.4) | async-done | bytes 589856 | tf_op jit(solution)/shard_map/all_to_all | solution.py:460
  110.6 2.0 %combine.1 = bf16[512,256]{1,0:T(8,128)(2,1)} custom-call(s32[96]{0:T(128)S(1)} %copy-done.13, s32[256]{0:T(256)S(1)} %copy-done.12, s32[256]{0:T(256)S(1)} %copy-done.14, f32[16,64,128]{2,1,0:T(8,128)S(1)} %copy-done.7, f32[16,8,128]{2,1,0:T(8,128)S(1)} %get-tuple-element.17.after.stat_ref, bf16[16,72,256]{2,1,0:T(8,128)(2,1)S(1)} %all-to-all-done.4.got_ref, ...), custom_call_target="tpu_custom_call" | custom-call | tf_op jit(solution)/shard_map/combine/pallas_call | solution.py:490
  (33 shorter events, 0.1 us)
Async XLA Ops:
  0.6 16.0 %copy-start.4 = (bf16[512,256]{1,0:T(8,128)(2,1)S(1)}, bf16[512,256]{1,0:T(8,128)(2,1)}, u32[]{:S(2)}) copy-start(bf16[512,256]{1,0:T(8,128)(2,1)} %q_ref.1) | copy-start | bytes 786436
  0.6 13.1 %copy-start.18 = (bf16[256,544]{0,1:T(8,128)(2,1)S(1)}, bf16[256,544]{0,1:T(8,128)(2,1)}, u32[]{:S(2)}) copy-start(bf16[256,544]{0,1:T(8,128)(2,1)} %param.21) | copy-start | bytes 835588
  0.7 13.3 %copy-start.5 = (bf16[512,256]{1,0:T(8,128)(2,1)S(1)}, bf16[512,256]{1,0:T(8,128)(2,1)}, u32[]{:S(2)}) copy-start(bf16[512,256]{1,0:T(8,128)(2,1)} %x_hbm.1) | copy-start | bytes 786436
  3.3 10.7 %copy-start.1 = (bf16[16,96,256]{2,1,0:T(8,128)(2,1)S(1)}, bf16[16,96,256]{2,1,0:T(8,128)(2,1)}, u32[]{:S(2)}) copy-start(bf16[16,96,256]{2,1,0:T(8,128)(2,1)} %get-tuple-element.18.after) | copy-start | bytes 2359300
  3.3 29.1 %all-to-all-start = ((bf16[16,96,256]{2,1,0:T(8,128)(2,1)}), bf16[16,96,256]{2,1,0:T(8,128)(2,1)S(1)}, u32[]{:S(2)}, u32[]{:S(2)}) async-start(bf16[16,96,256]{2,1,0:T(8,128)(2,1)} %get-tuple-element.18.after), calls=%async_computation | async-start | bytes 1572864 | tf_op jit(solution)/shard_map/all_to_all | solution.py:377
  14.0 31.8 %copy-start.19 = (s32[256,16]{0,1:T(8,128)S(1)}, s32[256,16]{0,1:T(8,128)}, u32[]{:S(2)}) copy-start(s32[256,16]{0,1:T(8,128)} %param.29) | copy-start | bytes 49156
  14.0 31.8 %copy-start.13 = (s32[96]{0:T(128)S(1)}, s32[96]{0:T(128)}, u32[]{:S(2)}) copy-start(s32[96]{0:T(128)} %get-tuple-element.15.tab) | copy-start | bytes 1156
  14.0 31.8 %copy-start.17 = (s32[256]{0:T(256)S(1)}, s32[256]{0:T(256)}, u32[]{:S(2)}) copy-start(s32[256]{0:T(256)} %kept.1) | copy-start | bytes 3076
  14.5 31.3 %copy-start.3 = (bf16[256,16,1,256]{3,1,2,0:T(8,128)(2,1)S(1)}, bf16[256,16,1,256]{3,1,2,0:T(8,128)(2,1)}, u32[]{:S(2)}) copy-start(bf16[256,16,1,256]{3,1,2,0:T(8,128)(2,1)} %param.17) | copy-start | bytes 6291460
  14.5 10.4 %collective-permute-start = (bf16[16,72,128]{2,1,0:T(8,128)(2,1)S(1)}, bf16[16,72,128]{2,1,0:T(8,128)(2,1)S(1)}, u32[]{:S(2)}, u32[]{:S(2)}) collective-permute-start(bf16[16,72,128]{2,1,0:T(8,128)(2,1)S(1)} %get-tuple-element.21), channel_id=1, source_target_pairs={{0,1},{1,0},{2,3},{3,2},{4,5},{5,4},{6,7},{7,6},{8,9},{9,8},{10,11... | collective-permute-start | bytes 884744 | tf_op jit(solution)/shard_map/ppermute | solution.py:398
  16.6 1.0 copy-start.10
  19.8 0.8 copy-start.6
  25.2 6.2 %collective-permute-start.1 = (bf16[8,72,128]{2,1,0:T(8,128)(2,1)S(1)}, bf16[8,72,128]{2,1,0:T(8,128)(2,1)S(1)}, u32[]{:S(2)}, u32[]{:S(2)}) collective-permute-start(bf16[8,72,128]{2,1,0:T(8,128)(2,1)S(1)} %add_two.1), channel_id=1, source_target_pairs={{0,16},{1,17},{2,18},{3,19},{4,20},{5,21},{6,22},{7,23},{8,24},{9,... | collective-permute-start | bytes 442376 | tf_op jit(solution)/shard_map/ppermute | solution.py:398
  32.4 27.0 %all-to-all-start.1 = ((bf16[8,72,128]{2,1,0:T(8,128)(2,1)}), bf16[8,72,128]{2,1,0:T(8,128)(2,1)S(1)}, u32[]{:S(2)}, u32[]{:S(2)}) async-start(bf16[8,72,128]{2,1,0:T(8,128)(2,1)} %add_four.1), calls=%async_computation.1 | async-start | bytes 294912 | tf_op jit(solution)/shard_map/all_to_all | solution.py:438
  51.8 0.8 copy-start.2
  78.0 20.9 %copy-start.8 = (bf16[512,256]{1,0:T(8,128)(2,1)S(1)}, bf16[512,256]{1,0:T(8,128)(2,1)}, u32[]{:S(2)}) copy-start(bf16[512,256]{1,0:T(8,128)(2,1)} %wdt_hbm.1) | copy-start | bytes 786436
  78.0 20.9 %copy-start.9 = (bf16[512,256]{1,0:T(8,128)(2,1)S(1)}, bf16[512,256]{1,0:T(8,128)(2,1)}, u32[]{:S(2)}) copy-start(bf16[512,256]{1,0:T(8,128)(2,1)} %g_hbm.1) | copy-start | bytes 786436
  78.1 20.9 %copy-start.11 = (f32[16,256]{1,0:T(8,128)S(1)}, f32[16,256]{1,0:T(8,128)}, u32[]{:S(2)}) copy-start(f32[16,256]{1,0:T(8,128)} %a_ref.1) | copy-start | bytes 49156
  78.1 20.9 %copy-start.12 = (s32[256]{0:T(256)S(1)}, s32[256]{0:T(256)}, u32[]{:S(2)}) copy-start(s32[256]{0:T(256)} %entries.3) | copy-start | bytes 3076
  78.1 20.9 %copy-start.14 = (s32[256]{0:T(256)S(1)}, s32[256]{0:T(256)}, u32[]{:S(2)}) copy-start(s32[256]{0:T(256)} %fresh_len.3) | copy-start | bytes 3076
  78.1 20.9 %copy-start.15 = (f32[256]{0:T(256)S(1)}, f32[256]{0:T(256)}, u32[]{:S(2)}) copy-start(f32[256]{0:T(256)} %param.23) | copy-start | bytes 3076
  78.1 20.9 %copy-start.16 = (f32[256]{0:T(256)S(1)}, f32[256]{0:T(256)}, u32[]{:S(2)}) copy-start(f32[256]{0:T(256)} %param.25) | copy-start | bytes 3076
  87.9 11.2 %copy-start = (bf16[32,72,128]{2,1,0:T(8,128)(2,1)S(1)}, bf16[32,72,128]{2,1,0:T(8,128)(2,1)}, u32[]{:S(2)}) copy-start(bf16[32,72,128]{2,1,0:T(8,128)(2,1)} %all_to_all.26.after.low_ref) | copy-start | bytes 1769476
  87.9 22.8 %copy-start.7 = (f32[16,64,128]{2,1,0:T(8,128)S(1)}, f32[16,64,128]{2,1,0:T(8,128)}, u32[]{:S(2)}) copy-start(f32[16,64,128]{2,1,0:T(8,128)} %copy-done.6) | copy-start | bytes 1572868
  87.9 22.8 %all-to-all-start.4 = ((bf16[16,72,256]{2,1,0:T(8,128)(2,1)}), bf16[16,72,256]{2,1,0:T(8,128)(2,1)S(1)}, u32[]{:S(2)}, u32[]{:S(2)}) async-start(bf16[16,72,256]{2,1,0:T(8,128)(2,1)} %gate.1), calls=%async_computation.4 | async-start | bytes 1179648 | tf_op jit(solution)/shard_map/all_to_all | solution.py:460
